TPU v7x, 256 devices: a whole 4x4x8 slice. The times are simulated.
256 devices in a mesh: refl: 8 (over x, y_hi), grid: 32 (over z, y_lo, core).
Axes of the slice: x: 4, y: 4 (y_hi: 2, y_lo: 2; y = y_hi * 2 + y_lo), z: 8, core: 2. Of those that a mesh axis runs over, the one named last changes fastest.
Arguments:
- density: bfloat16 [2, 256, 256, 256], P(None, 'grid'), may hold values from -6 to 6
- displacement: bfloat16 [3, 256, 256, 256], P(None, 'grid'), may hold values from -0.8984375 to 0.8984375
- support: int32 [256, 256, 256], P('grid'), may hold values 0 or 1
- millers: int32 [8, 3], replicated, may hold values from -3 to 3
- amplitude: float32 [8, 256, 256, 256], P('refl', None, 'grid'), may hold values from 0.1 to 3
Outputs:
- grad_density: float32 [2, 256, 256, 256], P(None, 'grid', 'refl')
- grad_displacement: float32 [3, 256, 256, 256], P(None, 'grid', 'refl')
All inputs are finite; a program needn't handle non-finite values. No bound on the sum of `support` on one device may be relied on, other than what follows from the above.
Results may differ from a plain program's by a relative error of at most 0.00065.
Values sent between devices are 32-bit elements; how exact they have to be, the bound alone decides.
No kernel may reach another device: no remote copies, remote signals or barrier semaphores. Data moves between devices by JAX's collectives and lax.ppermute only.
A program may use at most 128 MiB of HBM per device.

v0:
```python
import math

import jax
import jax.numpy as jnp
from jax import lax
from jax.sharding import PartitionSpec as P


def dft_tables(length):
    counter = jnp.arange(length, dtype=jnp.int32)
    product = counter[:, None] * counter[None, :] % length
    angles = product.astype(jnp.float32) * (2.0 * math.pi / length)
    factor = 1.0 / math.sqrt(length)
    return (jnp.cos(angles) * factor, jnp.sin(angles) * factor)


def transform_axis(real_part, imag_part, pattern, tables, inverse):
    cosine, sine = tables
    real_cos = jnp.einsum(pattern, real_part, cosine, precision=lax.Precision.HIGHEST)
    real_sin = jnp.einsum(pattern, real_part, sine, precision=lax.Precision.HIGHEST)
    imag_cos = jnp.einsum(pattern, imag_part, cosine, precision=lax.Precision.HIGHEST)
    imag_sin = jnp.einsum(pattern, imag_part, sine, precision=lax.Precision.HIGHEST)
    if inverse:
        return (real_cos - imag_sin, imag_cos + real_sin)
    return (real_cos + imag_sin, imag_cos - real_sin)


def phase_terms(hkl_rows, shift):
    angle = (
        2.0
        * math.pi
        * jnp.einsum("gc,cxyz->gxyz", hkl_rows, shift, precision=lax.Precision.HIGHEST)
    )
    return (jnp.cos(angle), jnp.sin(angle))


def gradient_terms(hkl_rows, mask, rho_real, rho_imag, cosine, sine, back_real, back_imag):
    obj_real = mask * (rho_real * cosine - rho_imag * sine)
    obj_imag = mask * (rho_real * sine + rho_imag * cosine)
    grad_real = jnp.sum(mask * (cosine * back_real + sine * back_imag), axis=0)
    grad_imag = jnp.sum(mask * (cosine * back_imag - sine * back_real), axis=0)
    twist = obj_real * back_imag - obj_imag * back_real
    grad_shift = jnp.einsum("gc,gxyz->cxyz", hkl_rows, twist, precision=lax.Precision.HIGHEST)
    return (jnp.stack([grad_real, grad_imag]), grad_shift)


def body(density, displacement, support, millers, amplitude):
    local_refl = amplitude.shape[0]
    total_refl = millers.shape[0]
    full_x = amplitude.shape[1]
    full_y = support.shape[1]
    full_z = support.shape[2]
    rho_real = density[0].astype(jnp.float32)
    rho_imag = density[1].astype(jnp.float32)
    shift = displacement.astype(jnp.float32)
    mask = support.astype(jnp.float32)
    indices = millers.astype(jnp.float32)
    table_x = dft_tables(full_x)
    table_y = dft_tables(full_y)
    table_z = dft_tables(full_z)
    first_refl = lax.axis_index("refl") * local_refl
    own_hkl = lax.dynamic_slice_in_dim(indices, first_refl, local_refl, 0)
    cosine, sine = phase_terms(own_hkl, shift)
    obj_real = mask * (rho_real * cosine - rho_imag * sine)
    obj_imag = mask * (rho_real * sine + rho_imag * cosine)
    real_part, imag_part = transform_axis(obj_real[0], obj_imag[0], "xyz,zk->xyk", table_z, False)
    real_part, imag_part = transform_axis(real_part, imag_part, "xyz,yk->xkz", table_y, False)
    columns = lax.all_to_all(
        jnp.stack([real_part, imag_part]), "grid", split_axis=2, concat_axis=1, tiled=True
    )
    spec_real, spec_imag = transform_axis(columns[0], columns[1], "xyz,xk->kyz", table_x, False)
    magnitude = jnp.sqrt(spec_real * spec_real + spec_imag * spec_imag)
    ratio = amplitude[0] / jnp.maximum(magnitude, 0.5)
    resid_real = spec_real - ratio * spec_real
    resid_imag = spec_imag - ratio * spec_imag
    real_part, imag_part = transform_axis(resid_real, resid_imag, "xyz,xk->kyz", table_x, True)
    slabs = lax.all_to_all(
        jnp.stack([real_part, imag_part]), "grid", split_axis=1, concat_axis=2, tiled=True
    )
    real_part, imag_part = transform_axis(slabs[0], slabs[1], "xyz,yk->xkz", table_y, True)
    real_part, imag_part = transform_axis(real_part, imag_part, "xyz,zk->xyk", table_z, True)
    back_reals = [real_part]
    back_imags = [imag_part]
    back_real = jnp.stack(back_reals)
    back_imag = jnp.stack(back_imags)
    scale = 1.0 / total_refl
    moved = lax.all_to_all(
        jnp.stack([back_real, back_imag]), "refl", split_axis=3, concat_axis=1, tiled=True
    )
    part_y = moved.shape[3]
    offset = lax.axis_index("refl") * part_y
    mask_part = lax.dynamic_slice_in_dim(mask, offset, part_y, 1)
    real_part = lax.dynamic_slice_in_dim(rho_real, offset, part_y, 1)
    imag_part = lax.dynamic_slice_in_dim(rho_imag, offset, part_y, 1)
    shift_part = lax.dynamic_slice_in_dim(shift, offset, part_y, 2)
    cos_all, sin_all = phase_terms(indices, shift_part)
    grad_rho, grad_shift = gradient_terms(
        indices, mask_part, real_part, imag_part, cos_all, sin_all, moved[0], moved[1]
    )
    return (grad_rho * scale, grad_shift * scale)


def solution(mesh):
    in_specs = (
        P(None, "grid", None, None),
        P(None, "grid", None, None),
        P("grid", None, None),
        P(),
        P("refl", None, "grid", None),
    )
    out_specs = (P(None, "grid", "refl", None), P(None, "grid", "refl", None))
    return jax.shard_map(body, mesh=mesh, in_specs=in_specs, out_specs=out_specs, check_vma=False)
```

profile of v0, /device:TPU:8, one launch (start us, length us, event | category | flops | bytes accessed | tf_op | source)
XLA Modules:
  0.0 437.6 jit_solution(726167056296597526)
XLA Ops:
  0.6 0.7 convert_element_type.71
  1.3 6.5 %copy.54 = bf16[3,8,256,256]{3,0,2,1:T(4,128)(2,1)} copy(bf16[3,8,256,256]{3,2,1,0:T(8,128)(2,1)} %param.6) | data formatting | bytes 6291456 | tf_op args[1]
  7.8 0.2 dynamic-slice_reduce_fusion
  8.0 0.0 copy-start
  8.0 0.0 copy-start.1
  8.0 8.8 %fusion.121 = f32[1,8,256,256]{3,0,2,1:T(1,128)S(1)} fusion(bf16[3,8,256,256]{3,0,2,1:T(4,128)(2,1)} %copy.54, f32[3]{0:T(128)S(1)} %dynamic-slice_reduce_fusion), kind=kOutput, calls=%fused_computation.161 | convolution fusion | flops 18874368 | bytes 5242892 | tf_op jit(solution)/shard_map/gc,cxyz->gxyz/dot_general | solution.py:32
  16.9 0.0 copy-done
  16.9 0.0 copy-done.1
  16.9 10.6 %fusion.83 = f32[8,256,256]{2,1,0:T(8,128)S(1)} fusion(f32[1,8,256,256]{3,0,2,1:T(1,128)S(1)} %fusion.121, bf16[2,8,256,256]{3,2,1,0:T(8,128)(2,1)S(1)} %copy-done.1, s32[8,256,256]{2,1,0:T(8,128)S(1)} %copy-done), kind=kOutput, calls=%fused_computation.117 | convolution fusion | flops 1615790080 | bytes 8388608 | tf_op jit(solution)/shard_map/xyz,zk->xyk/dot_general | solution.py:19
  27.5 11.0 %fusion.81 = f32[8,256,256]{2,1,0:T(8,128)S(1)} fusion(f32[1,8,256,256]{3,0,2,1:T(1,128)S(1)} %fusion.121, bf16[2,8,256,256]{3,2,1,0:T(8,128)(2,1)S(1)} %copy-done.1, s32[8,256,256]{2,1,0:T(8,128)S(1)} %copy-done), kind=kOutput, calls=%fused_computation.115 | convolution fusion | flops 1615790080 | bytes 8388608 | tf_op jit(solution)/shard_map/xyz,zk->xyk/dot_general | solution.py:21
  38.5 10.8 %convolution_add_fusion = f32[8,256,256]{2,1,0:T(8,128)S(1)} fusion(f32[8,256,256]{2,1,0:T(8,128)S(1)} %fusion.83, f32[1,8,256,256]{3,0,2,1:T(1,128)S(1)} %fusion.121, bf16[2,8,256,256]{3,2,1,0:T(8,128)(2,1)S(1)} %copy-done.1, s32[8,256,256]{2,1,0:T(8,128)S(1)} %copy-done), kind=kOutput, calls=%fused_computation.77 | convolution fusion | flops 1616314368 | bytes 10485760 | tf_op jit(solution)/shard_map/xyz,zk->xyk/dot_general | solution.py:22
  49.3 3.1 fusion.85
  52.4 10.7 %convolution_subtract_fusion = f32[8,256,256]{2,1,0:T(8,128)S(1)} fusion(f32[8,256,256]{2,1,0:T(8,128)S(1)} %fusion.81, f32[1,8,256,256]{3,0,2,1:T(1,128)S(1)} %fusion.121, bf16[2,8,256,256]{3,2,1,0:T(8,128)(2,1)S(1)} %copy-done.1, s32[8,256,256]{2,1,0:T(8,128)S(1)} %copy-done), kind=kOutput, calls=%fused_computation.76 | convolution fusion | flops 1616314368 | bytes 10485760 | tf_op jit(solution)/shard_map/xyz,zk->xyk/dot_general | solution.py:20
  63.1 3.3 fusion.77
  66.4 2.9 add_bitcast_fusion.2
  69.4 2.9 subtract_bitcast_fusion.2
  72.3 0.4 pad_maximum_fusion
  72.7 2.4 copy.59
  75.2 106.2 %all_to_all.45 = f32[2,8,256,256]{3,1,0,2:T(8,128)S(1)} all-to-all(f32[2,8,256,256]{3,1,0,2:T(8,128)S(1)} %copy.59), channel_id=1, replica_groups=mesh['refl'=8,'grid'=32] {'grid'}, dimensions={2} | all-to-all | bytes 8388608 | tf_op jit(solution)/shard_map/all_to_all | solution.py:68
  181.4 0.4 copy.144
  181.8 2.9 fusion.28
  184.8 2.9 fusion.29
  187.7 0.0 copy-start.3
  187.7 3.0 fusion.41
  190.6 0.0 copy-done.3
  190.7 4.8 %multiply_subtract_fusion.1 = (f32[256,8,256]{2,0,1:T(8,128)S(1)}, f32[256,8,256]{2,0,1:T(8,128)S(1)}) fusion(f32[1,256,8,256]{3,2,1,0:T(8,128)S(1)} %copy-done.3, f32[256,8,256]{2,0,1:T(8,128)S(1)} %fusion.41, f32[256,8,256]{2,0,1:T(8,128)S(1)} %fusion.29, f32[2,32,8,8,256]{4,2,1,3,0:T(8,128)S(1)} %bitcast.316), kind=kOutput, calls=%fused_computation.7 | convolution fusion | flops 1616838656 | bytes 12582912 | tf_op jit(solution)/shard_map/xyz,xk->kyz/dot_general | solution.py:22
  195.4 2.9 fusion.88
  198.3 2.9 fusion.74
  201.2 2.9 subtract_bitcast_fusion.1
  204.2 3.1 add_bitcast_fusion.1
  207.3 0.3 pad_maximum_fusion.1
  207.6 2.4 copy.70
  210.0 99.6 %all_to_all.46 = f32[2,256,8,256]{3,2,0,1:T(8,128)S(1)} all-to-all(f32[2,256,8,256]{3,2,0,1:T(8,128)S(1)} %copy.70), channel_id=1, replica_groups=mesh['refl'=8,'grid'=32] {'grid'}, dimensions={1} | all-to-all | bytes 8388608 | tf_op jit(solution)/shard_map/all_to_all | solution.py:77
  309.7 0.4 copy.143
  310.1 2.9 fusion.33
  313.0 2.9 fusion.32
  315.9 3.0 fusion.39
  318.9 2.8 fusion.18
  321.8 3.0 fusion.16
  324.8 3.0 fusion.38
  327.8 2.9 subtract_bitcast_fusion
  330.7 2.9 add_bitcast_fusion
  333.6 0.4 pad_maximum_fusion.2
  334.0 4.6 %copy.76 = f32[2,1,8,256,256]{4,2,1,0,3:T(8,128)} copy(f32[2,1,8,256,256]{4,3,2,1,0:T(8,128)S(1)} %pad_maximum_fusion.2) | data formatting | bytes 8388608 | tf_op jit(solution)/shard_map/stack | solution.py:88
  338.6 6.0 %all-to-all-start.2 = ((f32[2,1,8,256,256]{4,2,1,0,3:T(8,128)}), f32[2,1,8,256,256]{4,2,1,0,3:T(8,128)}, u32[]{:S(2)}, u32[]{:S(2)}) async-start(f32[2,1,8,256,256]{4,2,1,0,3:T(8,128)} %copy.76), calls=%async_computation.2 | async-start | bytes 8388608 | tf_op jit(solution)/shard_map/all_to_all | solution.py:87
  344.7 1.5 convert_element_type.70
  346.2 1.0 constant_dynamic-slice_fusion
  347.2 2.0 slice_convert_fusion.1
  349.2 54.7 %all-to-all-done.2 = f32[2,1,8,256,256]{4,2,1,0,3:T(8,128)} async-done(((f32[2,1,8,256,256]{4,2,1,0,3:T(8,128)}), f32[2,1,8,256,256]{4,2,1,0,3:T(8,128)}, u32[]{:S(2)}, u32[]{:S(2)}) %all-to-all-start.2) | async-done | bytes 4194336 | tf_op jit(solution)/shard_map/all_to_all | solution.py:87
  403.9 0.0 copy-start.2
  403.9 4.6 %copy.142 = f32[2,1,8,8,32,256]{5,3,4,2,1,0:T(8,128)S(1)} copy(f32[2,1,8,8,32,256]{5,2,0,4,3,1:T(8,128)} %bitcast.44) | data formatting | bytes 8388608 | tf_op jit(solution)/shard_map/all_to_all | solution.py:87
  408.5 0.0 copy-done.2
  408.5 14.3 %fusion.2 = (f32[8,32,256]{2,1,0:T(8,128)S(1)}, f32[8,32,256]{2,1,0:T(8,128)S(1)}, f32[8,32,256,8]{2,3,1,0:T(8,128)S(1)}) fusion(f32[2,8,1,8,32,256]{5,1,4,3,2,0:T(8,128)S(1)} %bitcast.319, f32[8,32,256]{2,1,0:T(8,128)S(1)} %constant_dynamic-slice_fusion, s32[8,3]{0,1:T(4,128)S(1)} %copy-done.2, bf16[3,8,256,256]{3,0,2,1:T(4,128)(2,1)} %copy.54, ...), kind=kOutput, calls=%fused_computation.20 | convolution fusion | flops 24510488 | bytes 7602276 | tf_op jit(solution)/shard_map/gc,cxyz->gxyz/dot_general | solution.py:32
  422.8 12.5 %fusion.49 = f32[3,8,32,256]{3,0,2,1:T(4,128)S(1)} fusion(f32[2,8,1,8,32,256]{5,1,4,3,2,0:T(8,128)S(1)} %bitcast.320, f32[8,32,256,8]{2,3,1,0:T(8,128)S(1)} %get-tuple-element.14, f32[8,32,256]{2,1,0:T(8,128)S(1)} %get-tuple-element.15, f32[8,32,256]{2,1,0:T(8,128)S(1)} %get-tuple-element.16, f32[8,32,256]{2,1,0:T(8,128)S(1)} %constant_dynamic-slice_fusion, ...), kind=kOutput, calls=%fused_computation.79 | convolution fusion | flops 25362456 | bytes 7864416 | tf_op jit(solution)/shard_map/gc,gxyz->cxyz/dot_general | solution.py:43
  435.3 1.0 copy.79
  436.4 0.8 maximum_multiply_fusion
  (1 shorter events, 0.0 us)
Async XLA Ops:
  8.0 8.9 %copy-start = (s32[8,256,256]{2,1,0:T(8,128)S(1)}, s32[8,256,256]{2,1,0:T(8,128)}, u32[]{:S(2)}) copy-start(s32[8,256,256]{2,1,0:T(8,128)} %param.7) | copy-start | bytes 6291460
  8.0 8.9 %copy-start.1 = (bf16[2,8,256,256]{3,2,1,0:T(8,128)(2,1)S(1)}, bf16[2,8,256,256]{3,2,1,0:T(8,128)(2,1)}, u32[]{:S(2)}) copy-start(bf16[2,8,256,256]{3,2,1,0:T(8,128)(2,1)} %param.5) | copy-start | bytes 6291460
  187.7 3.0 copy-start.3
  338.6 65.3 %all-to-all-start.2 = ((f32[2,1,8,256,256]{4,2,1,0,3:T(8,128)}), f32[2,1,8,256,256]{4,2,1,0,3:T(8,128)}, u32[]{:S(2)}, u32[]{:S(2)}) async-start(f32[2,1,8,256,256]{4,2,1,0,3:T(8,128)} %copy.76), calls=%async_computation.2 | async-start | bytes 8388608 | tf_op jit(solution)/shard_map/all_to_all | solution.py:87
  403.9 4.6 %copy-start.2 = (s32[8,3]{0,1:T(4,128)S(1)}, s32[8,3]{0,1:T(4,128)}, u32[]{:S(2)}) copy-start(s32[8,3]{0,1:T(4,128)} %param.8) | copy-start | bytes 292
where the time goes:
time: 443 us; the launch traced here: 438 us
  blocking collectives  206 us (47%)
  matrix products  140 us (32%)
  waiting for transfers between devices  54.7 us (12%)
  local copies, waits for them, and re-layouts  23.8 us (5%)
  other arithmetic  6.1 us (1%)
  starting transfers between devices  6.05 us (1%)
    all_to_all x1, blocking collectives, body(): lax.all_to_all(jnp.stack([real_part, imag_part]), 'grid', split_axis=2, c...  106 us
    all_to_all x1, blocking collectives, body(): lax.all_to_all(jnp.stack([real_part, imag_part]), 'grid', split_axis=1, c...  99.6 us
    all_to_all x1, waiting for transfers between devices, body(): lax.all_to_all(jnp.stack([back_real, back_imag]), 'refl', split_axis=3, c...  54.7 us
    dot_general x6, matrix products, transform_axis(): jnp.einsum(pattern, imag_part, sine, precision=lax.Precision.HIGHEST)  27.3 us
    dot_general x6, matrix products, transform_axis(): jnp.einsum(pattern, imag_part, cosine, precision=lax.Precision.HIGHEST)  26.2 us
    dot_general x6, matrix products, transform_axis(): jnp.einsum(pattern, real_part, sine, precision=lax.Precision.HIGHEST)  25.4 us
    dot_general x6, matrix products, transform_axis(): jnp.einsum(pattern, real_part, cosine, precision=lax.Precision.HIGHEST)  25.2 us
    dot_general x2, matrix products, phase_terms(): jnp.einsum('gc,cxyz->gxyz', hkl_rows, shift, precision=lax.Precision.HIGH...  23.1 us
  transfers between devices with their start and end apart: 1, of which 1 were waited for; matrix products, arithmetic and copies ran while one was open for 1% of the time, Pallas kernels for 0%

commit v1 on v0

v1 whole, which is shorter than its diff:
```python
import functools
import math

import jax
import jax.numpy as jnp
import ml_dtypes
import numpy as np
from jax import lax
from jax.experimental import pallas as pl
from jax.experimental.pallas import tpu as pltpu
from jax.sharding import PartitionSpec as P

N = 256
CH = 2
KC = N // CH
SLABS = 32
XL = 8
NREF = 8
BF = jnp.bfloat16
F32 = jnp.float32


def split_np(table):
    high = table.astype(ml_dtypes.bfloat16)
    low = (table - high.astype(np.float64)).astype(ml_dtypes.bfloat16)
    return high, low


def dft_np():
    n = np.arange(N)
    angle = 2.0 * np.pi * (np.outer(n, n) % N) / N
    return np.cos(angle) / math.sqrt(N), -np.sin(angle) / math.sqrt(N)


def left_table(inverse):
    re, im = dft_np()
    high, low = split_np(np.concatenate([re, -im if inverse else im], 0))
    return np.concatenate([high, high, low], 1)


def packed_columns():
    chunk = np.arange(N) // KC
    inner = np.arange(N) % KC
    real = chunk * 2 * KC + inner
    return real, real + KC


def right_forward():
    re, im = dft_np()
    real, imag = packed_columns()
    table = np.zeros((2 * N, 2 * N))
    table[:N, real] = re
    table[:N, imag] = im
    table[N:, real] = -im
    table[N:, imag] = re
    high, low = split_np(table)
    return np.concatenate([high, high, low], 0)


def right_inverse():
    re, im = dft_np()
    real, imag = packed_columns()
    table = np.zeros((2 * N, 2 * N))
    table[real, :N] = re
    table[real, N:] = -im
    table[imag, :N] = im
    table[imag, N:] = re
    return split_np(table)


def sine_coefficients():
    b = 0.25 * np.cos((np.arange(400) + 0.5) / 400 * np.pi / 2)
    powers = np.stack([b ** (2 * k + 1) for k in range(6)], 1)
    return [float(v) for v in np.linalg.lstsq(powers, np.sin(2 * np.pi * b), rcond=None)[0]]


SINE = sine_coefficients()


def sine_turns(b):
    q = b * b
    acc = jnp.full_like(b, SINE[5])
    for k in range(4, -1, -1):
        acc = acc * q + SINE[k]
    return acc * b


def cos_sin_turns(t):
    t = t - jnp.round(t)
    cosine = sine_turns(0.25 - jnp.abs(t))
    u = t - 0.25
    u = u - jnp.round(u)
    return cosine, sine_turns(0.25 - jnp.abs(u))


def split(value):
    high = value.astype(BF)
    return high, (value - high.astype(F32)).astype(BF)


def left_multiply(table, packed):
    high, low = split(packed)
    both = jnp.dot(table, jnp.concatenate([high, low, high], 0), preferred_element_type=F32)
    real = both[:N, :KC] - both[N:, KC:]
    imag = both[:N, KC:] + both[N:, :KC]
    return jnp.concatenate([real, imag], 1)


def object_kernel(idx_ref, miller_ref, rho_ref, shift_ref, support_ref, table_ref, out_ref, high_ref, low_ref):
    r = idx_ref[0]
    h = miller_ref[r, 0].astype(F32)
    k = miller_ref[r, 1].astype(F32)
    l = miller_ref[r, 2].astype(F32)
    rows = 32

    def step(i, carry):
        at = pl.ds(pl.multiple_of(i * rows, rows), rows)
        u = [shift_ref[c, 0, at, :].astype(F32) for c in range(3)]
        mask = support_ref[0, at, :].astype(F32)
        cosine, sine = cos_sin_turns(h * u[0] + k * u[1] + l * u[2])
        real = mask * rho_ref[0, 0, at, :].astype(F32)
        imag = mask * rho_ref[1, 0, at, :].astype(F32)
        for part, value in enumerate((real * cosine - imag * sine, real * sine + imag * cosine)):
            high, low = split(value)
            high_ref[at, part * N : (part + 1) * N] = high
            low_ref[at, part * N : (part + 1) * N] = low
        return carry

    lax.fori_loop(0, N // rows, step, 0)
    high = high_ref[...]
    out_ref[0] = jnp.dot(
        jnp.concatenate([high, low_ref[...], high], 1), table_ref[...], preferred_element_type=F32
    )


def y_forward_kernel(a_ref, table_ref, out_ref):
    def step(x, carry):
        out_ref[:, x] = left_multiply(table_ref[...], a_ref[x]).reshape(SLABS, XL, 2 * KC)
        return carry

    lax.fori_loop(0, XL, step, 0)


def x_kernel(in_ref, amp_ref, forward_ref, inverse_ref, out_ref, real_ref, imag_ref):
    real_ref[...] = in_ref[:, :KC]
    imag_ref[...] = in_ref[:, KC:]

    def step(i, carry):
        at = pl.ds(i, N, stride=XL)
        spec = left_multiply(forward_ref[...], jnp.concatenate([real_ref[at, :], imag_ref[at, :]], 1))
        real, imag = spec[:, :KC], spec[:, KC:]
        ratio = amp_ref[at, :] * lax.rsqrt(jnp.maximum(real * real + imag * imag, 0.25))
        resid = jnp.concatenate([real - ratio * real, imag - ratio * imag], 1)
        back = left_multiply(inverse_ref[...], resid)
        real_ref[at, :] = back[:, :KC]
        imag_ref[at, :] = back[:, KC:]
        return carry

    lax.fori_loop(0, XL, step, 0)
    out_ref[:, :KC] = real_ref[...]
    out_ref[:, KC:] = imag_ref[...]


def y_inverse_kernel(idx_ref, in_ref, table_ref, *refs):
    outs, t_ref = refs[:NREF], refs[NREF]
    r = idx_ref[0]

    def step(x, carry):
        t_ref[...] = left_multiply(table_ref[...], in_ref[:, x].reshape(N, 2 * KC))
        for s in range(NREF):
            start = pl.multiple_of(lax.rem(r + s, NREF) * 32, 32)
            outs[s][x] = t_ref[pl.ds(start, 32), :]
        return carry

    lax.fori_loop(0, XL, step, 0)


def gradient_kernel(shift_by, idx_ref, miller_ref, rho_ref, shift_ref, support_ref, *refs):
    ins, high_ref, low_ref = refs[:CH], refs[CH], refs[CH + 1]
    sums = refs[CH + 2 : -3]
    rho_out, shift_out, back_ref = refs[-3:]
    g = lax.rem(idx_ref[0] + NREF - shift_by, NREF)
    h = miller_ref[g, 0].astype(F32)
    k = miller_ref[g, 1].astype(F32)
    l = miller_ref[g, 2].astype(F32)
    high, low = split(jnp.concatenate([ref[...].reshape(N, 2 * KC) for ref in ins], 1))
    dot = functools.partial(jnp.dot, preferred_element_type=F32)
    back_ref[...] = dot(high, high_ref[...]) + dot(low, high_ref[...]) + dot(high, low_ref[...])

    def step(x, carry):
        at = pl.ds(pl.multiple_of(x * 32, 32), 32)
        u = [shift_ref[c, x].astype(F32) for c in range(3)]
        mask = support_ref[x].astype(F32) * (1.0 / NREF)
        cosine, sine = cos_sin_turns(h * u[0] + k * u[1] + l * u[2])
        real, imag = back_ref[at, :N], back_ref[at, N:]
        p = mask * (cosine * real + sine * imag)
        q = mask * (cosine * imag - sine * real)
        twist = rho_ref[0, x].astype(F32) * q - rho_ref[1, x].astype(F32) * p
        for out, old, n, value in (
            (rho_out, 0, 0, p),
            (rho_out, 0, 1, q),
            (shift_out, 1, 0, h * twist),
            (shift_out, 1, 1, k * twist),
            (shift_out, 1, 2, l * twist),
        ):
            out[n, x] = sums[old][n, x] + value if sums else value
        return carry

    lax.fori_loop(0, XL, step, 0)


SMEM = pl.BlockSpec(memory_space=pltpu.SMEM)
VMEM = pl.BlockSpec(memory_space=pltpu.VMEM)


def cost(flops, size):
    return pl.CostEstimate(flops=int(flops), bytes_accessed=int(size), transcendentals=0)


def f32(*shape):
    return jax.ShapeDtypeStruct(shape, F32)


def params(mib):
    return pltpu.CompilerParams(vmem_limit_bytes=mib * 1024 * 1024)


def after(value, *earlier):
    return lax.optimization_barrier((value, earlier))[0]


def body(density, displacement, support, millers, amplitude):
    r = lax.axis_index("refl")
    idx = jnp.stack([r]).astype(jnp.int32)
    forward, inverse = jnp.asarray(left_table(False)), jnp.asarray(left_table(True))
    high, low = (jnp.asarray(t) for t in right_inverse())
    amp = amplitude.reshape(N * XL, N)
    a = pl.pallas_call(
        object_kernel,
        grid=(XL,),
        in_specs=[
            SMEM,
            SMEM,
            pl.BlockSpec((2, 1, N, N), lambda x: (0, x, 0, 0)),
            pl.BlockSpec((3, 1, N, N), lambda x: (0, x, 0, 0)),
            pl.BlockSpec((1, N, N), lambda x: (x, 0, 0)),
            pl.BlockSpec((6 * N, 2 * N), lambda x: (0, 0)),
        ],
        out_specs=pl.BlockSpec((1, N, 2 * N), lambda x: (x, 0, 0)),
        out_shape=f32(XL, N, 2 * N),
        scratch_shapes=[pltpu.VMEM((N, 2 * N), BF)] * 2,
        compiler_params=params(24),
        cost_estimate=cost(3.2e9, 12e6),
        name="object_z",
    )(idx, millers, density, displacement, support, jnp.asarray(right_forward()))

    def y_forward(c):
        return pl.pallas_call(
            y_forward_kernel,
            grid=(1,),
            in_specs=[pl.BlockSpec((XL, N, 2 * KC), lambda i: (0, 0, c)), VMEM],
            out_specs=VMEM,
            out_shape=f32(SLABS, XL, XL, 2 * KC),
            compiler_params=params(24),
            cost_estimate=cost(3.2e9, 12e6),
            name=f"y_forward_{c}",
        )(a, forward)

    def x_both(c, part):
        return pl.pallas_call(
            x_kernel,
            grid=(1,),
            in_specs=[VMEM, pl.BlockSpec((N * XL, KC), lambda i: (0, c)), VMEM, VMEM],
            out_specs=VMEM,
            out_shape=f32(N * XL, 2 * KC),
            scratch_shapes=[pltpu.VMEM((N * XL, KC), F32)] * 2,
            compiler_params=params(24),
            cost_estimate=cost(6.4e9, 24e6),
            name=f"x_{c}",
        )(part.reshape(N * XL, 2 * KC), amp, forward, inverse).reshape(SLABS, XL, XL, 2 * KC)

    def y_inverse(c, part):
        return pl.pallas_call(
            y_inverse_kernel,
            in_specs=[SMEM, VMEM, VMEM],
            out_specs=[VMEM] * NREF,
            out_shape=[f32(XL, 32, 2 * KC)] * NREF,
            scratch_shapes=[pltpu.VMEM((N, 2 * KC), F32)],
            compiler_params=params(24),
            cost_estimate=cost(3.2e9, 12e6),
            name=f"y_inverse_{c}",
        )(idx, part, inverse)

    def over_grid(part):
        return lax.all_to_all(part, "grid", 0, 0, tiled=True)

    def over_refl(parts):
        ring = lambda s: [(i, (i + s) % NREF) for i in range(NREF)]
        moved = {s: lax.ppermute(parts[s], "refl", ring(s)) for s in R_ORDER}
        return [parts[0]] + [moved[s] for s in range(1, NREF)]

    def gradient(s, parts, sums):
        out_block = lambda n: pl.BlockSpec((n, XL, 32, N), lambda i, idx: (0, 0, 0, 0))
        whole = lambda i, idx: (0, 0)
        return pl.pallas_call(
            functools.partial(gradient_kernel, s),
            grid_spec=pltpu.PrefetchScalarGridSpec(
                num_scalar_prefetch=1,
                grid=(1,),
                in_specs=[
                    SMEM,
                    pl.BlockSpec((2, XL, 32, N), lambda i, idx: (0, 0, idx[0], 0)),
                    pl.BlockSpec((3, XL, 32, N), lambda i, idx: (0, 0, idx[0], 0)),
                    pl.BlockSpec((XL, 32, N), lambda i, idx: (0, idx[0], 0)),
                ]
                + [pl.BlockSpec((XL, 32, 2 * KC), lambda i, idx: (0, 0, 0))] * CH
                + [pl.BlockSpec((2 * N, 2 * N), whole)] * 2
                + ([out_block(2), out_block(3)] if sums else []),
                out_specs=[out_block(2), out_block(3)],
                scratch_shapes=[pltpu.VMEM((N, 2 * N), F32)],
            ),
            out_shape=[f32(2, XL, 32, N), f32(3, XL, 32, N)],
            compiler_params=params(24),
            cost_estimate=cost(0.8e9, 5e6),
            name=f"gradient_{s}",
        )(idx, millers, density, displacement, support, *parts, high, low, *sums)

    f0 = over_grid(y_forward(0))
    f1 = over_grid(after(y_forward(1), f0))
    b0 = over_grid(after(x_both(0, f0), f1))
    b1 = over_grid(after(x_both(1, f1), b0))
    r0 = over_refl(y_inverse(0, b0))
    r1 = over_refl(y_inverse(1, after(b1, *r0)))
    sums = ()
    for s in (0,) + R_ORDER:
        sums = tuple(gradient(s, (r0[s], r1[s]), sums))
    return sums


R_ORDER = (4, 3, 5, 2, 6, 1, 7)


def solution(mesh):
    in_specs = (
        P(None, "grid", None, None),
        P(None, "grid", None, None),
        P("grid", None, None),
        P(),
        P("refl", None, "grid", None),
    )
    out_specs = (P(None, "grid", "refl", None), P(None, "grid", "refl", None))
    return jax.shard_map(body, mesh=mesh, in_specs=in_specs, out_specs=out_specs, check_vma=False)
```

time: 443 us -> 304 us (0.69)
  blocking collectives: 206 us -> 0 us
  matrix products: 140 us -> 0 us
  waiting for transfers between devices: 54.7 us -> 133 us
  starting transfers between devices: 6.05 us -> 72.8 us
  Pallas kernels: 0 us -> 56.9 us
  local copies, waits for them, and re-layouts: 23.8 us -> 34.4 us
  other arithmetic: 6.1 us -> 0 us
    all_to_all x2 -> x0, blocking collectives: 206 us -> none  [the longest x1 106 us: body(): lax.all_to_all(jnp.stack([real_part, imag_part]), 'grid', split_axis=2, c...]
    dot_general x27 -> x0, matrix products: 140 us -> none  [the longest x6 27.3 us: transform_axis(): jnp.einsum(pattern, imag_part, sine, precision=lax.Precision.HIGHEST)]
    all_to_all x1 -> x4, waiting for transfers between devices: 54.7 us -> 114 us  [over_grid(): return lax.all_to_all(part, 'grid', 0, 0, tiled=True)]
    pallas_call x0 -> x15, Pallas kernels: none -> 56.9 us  [the longest x2 19.1 us: x_both(): pl.pallas_call(x_kernel, grid=(1,), in_specs=[VMEM, pl.BlockSpec((N * XL,...]
    ppermute x0 -> x14, starting transfers between devices: none -> 48.7 us  [over_refl(): moved = {s: lax.ppermute(parts[s], 'refl', ring(s)) for s in R_ORDER}]
    unnamed x10 -> x69, local copies, waits for them, and re-layouts: 7.56 us -> 34.4 us
    ppermute x0 -> x14, waiting for transfers between devices: none -> 20 us  [over_refl(): moved = {s: lax.ppermute(parts[s], 'refl', ring(s)) for s in R_ORDER}]
    all_to_all x1 -> x4, starting transfers between devices: 6.05 us -> 24.1 us  [over_grid(): return lax.all_to_all(part, 'grid', 0, 0, tiled=True)]
  transfers between devices with their start and end apart: 1 -> 18, of which waited for: 1 -> 7; matrix products, arithmetic and copies ran while one was open for 1% -> 0% of each run, Pallas kernels for 0% -> 13%
where the time goes in v1:
time: 304 us; the launch traced here: 299 us
  waiting for transfers between devices  133 us (44%)
  starting transfers between devices  72.8 us (24%)
  Pallas kernels  56.9 us (19%)
  local copies, waits for them, and re-layouts  34.4 us (11%)
    all_to_all x4, waiting for transfers between devices, over_grid(): return lax.all_to_all(part, 'grid', 0, 0, tiled=True)  114 us
    ppermute x14, starting transfers between devices, over_refl(): moved = {s: lax.ppermute(parts[s], 'refl', ring(s)) for s in R_ORDER}  48.7 us
    unnamed x69, local copies, waits for them, and re-layouts  34.4 us
    all_to_all x4, starting transfers between devices, over_grid(): return lax.all_to_all(part, 'grid', 0, 0, tiled=True)  24.1 us
    ppermute x14, waiting for transfers between devices, over_refl(): moved = {s: lax.ppermute(parts[s], 'refl', ring(s)) for s in R_ORDER}  20 us
    pallas_call x2, Pallas kernels, x_both(): pl.pallas_call(x_kernel, grid=(1,), in_specs=[VMEM, pl.BlockSpec((N * XL,...  19.1 us
    pallas_call x8, Pallas kernels, gradient(): pl.pallas_call(functools.partial(gradient_kernel, s), grid_spec=pltpu.Pre...  15.2 us
    pallas_call x1, Pallas kernels, body(): pl.pallas_call(object_kernel, grid=(XL,), in_specs=[SMEM, SMEM, pl.BlockS...  9.96 us
  transfers between devices with their start and end apart: 18, of which 7 were waited for; matrix products, arithmetic and copies ran while one was open for 0% of the time, Pallas kernels for 13%

profile of v1, /device:TPU:8, one launch (start us, length us, event | category | flops | bytes accessed | tf_op | source)
XLA Modules:
  0.0 298.6 jit_solution(4674984011406515716)
XLA Ops:
  0.6 0.8 copy.20.miller_ref
  1.4 1.9 copy-done
  3.3 1.6 copy-done.2
  4.9 1.6 copy-done.4
  6.5 1.4 copy-done.20
  7.9 10.0 %object_z.1.a_ref = f32[8,256,512]{2,1,0:T(8,128)S(1)} custom-call(s32[1]{0:T(128)} %bitcast.idx_ref, s32[8,3]{1,0:T(8,128)S(1)} %copy.20.miller_ref, bf16[2,8,256,256]{3,2,1,0:T(8,128)(2,1)S(1)} %copy-done.2, bf16[3,8,256,256]{3,2,1,0:T(8,128)(2,1)S(1)} %copy-done, s32[8,256,256]{2,1,0:T(8,128)S(1)} %copy-done.4, bf16[1536,512]{1,0:T(8,128)(2,1)S(1)} %copy-done.20), custom_call_target="tpu_custom_call" | custom-call | flops 3200000000 | bytes 12000000 | tf_op jit(solution)/shard_map/object_z/pallas_call | solution.py:238
  17.9 3.2 %y_forward_0.1 = f32[32,8,8,256]{3,2,1,0:T(8,128)S(1)} custom-call(f32[8,256,512]{2,1,0:T(8,128)S(1)} %object_z.1.a_ref, bf16[512,768]{1,0:T(8,128)(2,1)S(1)} %copy-done.31), custom_call_target="tpu_custom_call" | custom-call | flops 3200000000 | bytes 12000000 | tf_op jit(solution)/shard_map/y_forward_0/pallas_call | solution.py:258
  21.0 2.0 copy-done.8
  23.0 1.4 copy-done.19
  24.4 10.1 %all-to-all-start = ((f32[32,8,8,256]{3,2,1,0:T(8,128)}), f32[32,8,8,256]{3,2,1,0:T(8,128)S(1)}, u32[]{:S(2)}, u32[]{:S(2)}) async-start(f32[32,8,8,256]{3,2,1,0:T(8,128)} %copy-done.19), calls=%async_computation | async-start | bytes 4194304 | tf_op jit(solution)/shard_map/all_to_all | solution.py:295
  34.5 2.2 copy-done.9
  36.7 3.2 %y_forward_1.1 = f32[32,8,8,256]{3,2,1,0:T(8,128)S(1)} custom-call(f32[8,256,512]{2,1,0:T(8,128)S(1)} %copy-done.9, bf16[512,768]{1,0:T(8,128)(2,1)S(1)} %copy-done.31), custom_call_target="tpu_custom_call" | custom-call | flops 3200000000 | bytes 12000000 | tf_op jit(solution)/shard_map/y_forward_1/pallas_call | solution.py:258
  39.8 1.4 copy-done.18
  41.2 43.5 %all-to-all-done = f32[32,8,8,256]{3,2,1,0:T(8,128)S(1)} async-done(((f32[32,8,8,256]{3,2,1,0:T(8,128)}), f32[32,8,8,256]{3,2,1,0:T(8,128)S(1)}, u32[]{:S(2)}, u32[]{:S(2)}) %all-to-all-start) | async-done | bytes 2097184 | tf_op jit(solution)/shard_map/all_to_all | solution.py:295
  84.7 1.3 copy-done.15
  86.1 4.7 %all-to-all-start.1 = ((f32[32,8,8,256]{3,2,1,0:T(8,128)}), f32[32,8,8,256]{3,2,1,0:T(8,128)S(1)}, u32[]{:S(2)}, u32[]{:S(2)}) async-start(f32[32,8,8,256]{3,2,1,0:T(8,128)} %copy-done.18), calls=%async_computation.1 | async-start | bytes 4194304 | tf_op jit(solution)/shard_map/all_to_all | solution.py:295
  90.8 1.6 copy-done.16
  92.4 1.6 copy-done.27
  94.0 1.1 copy-done.32
  95.1 9.6 %x_0.1 = f32[2048,256]{1,0:T(8,128)S(1)} custom-call(f32[2048,256]{1,0:T(8,128)S(1)} %bitcast.8, f32[2048,256]{1,0:T(8,128)S(1)} %bitcast.10, bf16[512,768]{1,0:T(8,128)(2,1)S(1)} %copy-done.32, bf16[512,768]{1,0:T(8,128)(2,1)S(1)} %copy-done.29), custom_call_target="tpu_custom_call" | custom-call | flops 6400000000 | bytes 24000000 | tf_op jit(solution)/shard_map/x_0/pallas_call | solution.py:270
  104.7 1.3 copy-done.17
  106.0 35.0 %all-to-all-done.1 = f32[32,8,8,256]{3,2,1,0:T(8,128)S(1)} async-done(((f32[32,8,8,256]{3,2,1,0:T(8,128)}), f32[32,8,8,256]{3,2,1,0:T(8,128)S(1)}, u32[]{:S(2)}, u32[]{:S(2)}) %all-to-all-start.1) | async-done | bytes 2097184 | tf_op jit(solution)/shard_map/all_to_all | solution.py:295
  141.0 1.4 copy-done.13
  142.4 4.7 %all-to-all-start.2 = ((f32[32,8,8,256]{3,2,1,0:T(8,128)}), f32[32,8,8,256]{3,2,1,0:T(8,128)S(1)}, u32[]{:S(2)}, u32[]{:S(2)}) async-start(f32[32,8,8,256]{3,2,1,0:T(8,128)} %bitcast.9), calls=%async_computation.2 | async-start | bytes 4194304 | tf_op jit(solution)/shard_map/all_to_all | solution.py:295
  147.1 1.6 copy-done.14
  148.6 1.6 copy-done.28
  150.2 1.1 copy-done.33
  151.4 9.6 %x_1.1 = f32[2048,256]{1,0:T(8,128)S(1)} custom-call(f32[2048,256]{1,0:T(8,128)S(1)} %bitcast.7, f32[2048,256]{1,0:T(8,128)S(1)} %bitcast.11, bf16[512,768]{1,0:T(8,128)(2,1)S(1)} %copy-done.33, bf16[512,768]{1,0:T(8,128)(2,1)S(1)} %copy-done.29), custom_call_target="tpu_custom_call" | custom-call | flops 6400000000 | bytes 24000000 | tf_op jit(solution)/shard_map/x_1/pallas_call | solution.py:270
  160.9 1.4 copy-done.10
  162.3 35.0 %all-to-all-done.2.in_ref = f32[32,8,8,256]{3,2,1,0:T(8,128)S(1)} async-done(((f32[32,8,8,256]{3,2,1,0:T(8,128)}), f32[32,8,8,256]{3,2,1,0:T(8,128)S(1)}, u32[]{:S(2)}, u32[]{:S(2)}) %all-to-all-start.2) | async-done | bytes 2097184 | tf_op jit(solution)/shard_map/all_to_all | solution.py:295
  197.3 1.3 copy-done.11
  198.6 4.7 %all-to-all-start.3 = ((f32[32,8,8,256]{3,2,1,0:T(8,128)}), f32[32,8,8,256]{3,2,1,0:T(8,128)S(1)}, u32[]{:S(2)}, u32[]{:S(2)}) async-start(f32[32,8,8,256]{3,2,1,0:T(8,128)} %bitcast.6), calls=%async_computation.3 | async-start | bytes 4194304 | tf_op jit(solution)/shard_map/all_to_all | solution.py:295
  203.3 1.6 copy-done.12
  204.9 3.2 %y_inverse_0.1 = (f32[8,32,256]{2,1,0:T(8,128)S(1)}, f32[8,32,256]{2,1,0:T(8,128)S(1)}, f32[8,32,256]{2,1,0:T(8,128)S(1)}, f32[8,32,256]{2,1,0:T(8,128)S(1)}, f3...) custom-call(s32[1]{0:T(128)} %bitcast.idx_ref, ...), custom_call_target="tpu_custom_call" | custom-call | flops 3200000000 | bytes 12000000 | tf_op jit(solution)/shard_map/y_inverse_0/pallas_call | solution.py:283
  208.1 0.7 copy-done.23
  208.8 4.5 %collective-permute-start = (f32[8,32,256]{2,1,0:T(8,128)S(1)}, f32[8,32,256]{2,1,0:T(8,128)S(1)}, u32[]{:S(2)}, u32[]{:S(2)}) collective-permute-start(f32[8,32,256]{2,1,0:T(8,128)S(1)} %get-tuple-element.38), channel_id=1, source_target_pairs={{0,224},{32,0},{64,32},{96,64},{128,96},{160,128},{192,160},{224,1... | collective-permute-start | bytes 786440 | tf_op jit(solution)/shard_map/ppermute | solution.py:299
  213.4 0.5 collective-permute-start.2
  213.8 4.1 %collective-permute-start.3 = (f32[8,32,256]{2,1,0:T(8,128)S(1)}, f32[8,32,256]{2,1,0:T(8,128)S(1)}, u32[]{:S(2)}, u32[]{:S(2)}) collective-permute-start(f32[8,32,256]{2,1,0:T(8,128)S(1)} %get-tuple-element.43), channel_id=1, source_target_pairs={{0,96},{32,128},{64,160},{96,192},{128,224},{160,0},{192,32},{224,... | collective-permute-start | bytes 786440 | tf_op jit(solution)/shard_map/ppermute | solution.py:299
  217.9 2.5 collective-permute-start.4
  220.5 14.2 %collective-permute-done.refs_0_ = f32[8,32,256]{2,1,0:T(8,128)S(1)} collective-permute-done((f32[8,32,256]{2,1,0:T(8,128)S(1)}, f32[8,32,256]{2,1,0:T(8,128)S(1)}, u32[]{:S(2)}, u32[]{:S(2)}) %collective-permute-start) | collective-permute-done | bytes 262176 | tf_op jit(solution)/shard_map/ppermute | solution.py:299
  234.6 18.9 %collective-permute-start.5 = (f32[8,32,256]{2,1,0:T(8,128)S(1)}, f32[8,32,256]{2,1,0:T(8,128)S(1)}, u32[]{:S(2)}, u32[]{:S(2)}) collective-permute-start(f32[8,32,256]{2,1,0:T(8,128)S(1)} %get-tuple-element.45), channel_id=1, source_target_pairs={{0,160},{32,192},{64,224},{96,0},{128,32},{160,64},{192,96},{224,1... | collective-permute-start | bytes 786440 | tf_op jit(solution)/shard_map/ppermute | solution.py:299
  253.6 0.7 copy-done.25
  254.3 3.2 %collective-permute-done.5.refs_0_ = f32[8,32,256]{2,1,0:T(8,128)S(1)} collective-permute-done((f32[8,32,256]{2,1,0:T(8,128)S(1)}, f32[8,32,256]{2,1,0:T(8,128)S(1)}, u32[]{:S(2)}, u32[]{:S(2)}) %collective-permute-start.5) | collective-permute-done | bytes 262176 | tf_op jit(solution)/shard_map/ppermute | solution.py:299
  257.4 0.7 copy-done.21
  258.1 1.8 collective-permute-done.6.refs_0_
  259.9 1.1 copy-done.30
  261.1 0.0 copy-start.7
  261.1 3.2 %y_inverse_1.1 = (f32[8,32,256]{2,1,0:T(8,128)S(1)}, f32[8,32,256]{2,1,0:T(8,128)S(1)}, f32[8,32,256]{2,1,0:T(8,128)S(1)}, f32[8,32,256]{2,1,0:T(8,128)S(1)}, f3...) custom-call(s32[1]{0:T(128)} %bitcast.idx_ref, ...), custom_call_target="tpu_custom_call" | custom-call | flops 3200000000 | bytes 12000000 | tf_op jit(solution)/shard_map/y_inverse_1/pallas_call | solution.py:283
  264.2 4.5 %collective-permute-start.13 = (f32[8,32,256]{2,1,0:T(8,128)S(1)}, f32[8,32,256]{2,1,0:T(8,128)S(1)}, u32[]{:S(2)}, u32[]{:S(2)}) collective-permute-start(f32[8,32,256]{2,1,0:T(8,128)S(1)} %get-tuple-element.54), channel_id=1, source_target_pairs={{0,128},{32,160},{64,192},{96,224},{128,0},{160,32},{192,64},{224,... | collective-permute-start | bytes 786440 | tf_op jit(solution)/shard_map/ppermute | solution.py:299
  268.8 1.6 collective-permute-start.12
  270.4 4.3 %collective-permute-start.11 = (f32[8,32,256]{2,1,0:T(8,128)S(1)}, f32[8,32,256]{2,1,0:T(8,128)S(1)}, u32[]{:S(2)}, u32[]{:S(2)}) collective-permute-start(f32[8,32,256]{2,1,0:T(8,128)S(1)} %get-tuple-element.52), channel_id=1, source_target_pairs={{0,160},{32,192},{64,224},{96,0},{128,32},{160,64},{192,96},{224,1... | collective-permute-start | bytes 786440 | tf_op jit(solution)/shard_map/ppermute | solution.py:299
  274.7 0.4 collective-permute-start.7
  275.1 3.4 %collective-permute-start.10 = (f32[8,32,256]{2,1,0:T(8,128)S(1)}, f32[8,32,256]{2,1,0:T(8,128)S(1)}, u32[]{:S(2)}, u32[]{:S(2)}) collective-permute-start(f32[8,32,256]{2,1,0:T(8,128)S(1)} %get-tuple-element.51), channel_id=1, source_target_pairs={{0,64},{32,96},{64,128},{96,160},{128,192},{160,224},{192,0},{224,... | collective-permute-start | bytes 786440 | tf_op jit(solution)/shard_map/ppermute | solution.py:299
  278.6 1.7 gradient_0.1
  280.3 0.1 collective-permute-start.9
  280.4 1.8 gradient_4.1
  282.2 0.8 collective-permute-done.12.refs_1_
  283.1 3.8 %collective-permute-start.8 = (f32[8,32,256]{2,1,0:T(8,128)S(1)}, f32[8,32,256]{2,1,0:T(8,128)S(1)}, u32[]{:S(2)}, u32[]{:S(2)}) collective-permute-start(f32[8,32,256]{2,1,0:T(8,128)S(1)} %get-tuple-element.49), channel_id=1, source_target_pairs={{0,32},{32,64},{64,96},{96,128},{128,160},{160,192},{192,224},{224... | collective-permute-start | bytes 786440 | tf_op jit(solution)/shard_map/ppermute | solution.py:299
  286.9 1.8 gradient_3.1
  288.7 1.8 gradient_5.1
  290.4 1.8 gradient_2.1
  292.2 1.8 gradient_6.1
  294.0 1.8 gradient_1.1
  295.8 2.8 gradient_7.1
  (56 shorter events, 0.1 us)
Async XLA Ops:
  1.4 1.9 copy-start
  3.3 1.6 copy-start.2
  4.9 1.6 copy-start.4
  6.5 1.4 copy-start.20
  7.9 10.0 %copy-start.31 = (bf16[512,768]{1,0:T(8,128)(2,1)S(1)}, bf16[512,768]{1,0:T(8,128)(2,1)}, u32[]{:S(2)}) copy-start(bf16[512,768]{1,0:T(8,128)(2,1)} %constant.16.clone.table_ref.forward_ref) | copy-start | bytes 2359300
  21.0 2.0 copy-start.8
  23.0 1.4 copy-start.19
  24.4 60.3 %all-to-all-start = ((f32[32,8,8,256]{3,2,1,0:T(8,128)}), f32[32,8,8,256]{3,2,1,0:T(8,128)S(1)}, u32[]{:S(2)}, u32[]{:S(2)}) async-start(f32[32,8,8,256]{3,2,1,0:T(8,128)} %copy-done.19), calls=%async_computation | async-start | bytes 4194304 | tf_op jit(solution)/shard_map/all_to_all | solution.py:295
  34.5 2.2 copy-start.9
  39.8 1.4 copy-start.18
  41.2 49.6 %copy-start.29 = (bf16[512,768]{1,0:T(8,128)(2,1)S(1)}, bf16[512,768]{1,0:T(8,128)(2,1)}, u32[]{:S(2)}) copy-start(bf16[512,768]{1,0:T(8,128)(2,1)} %constant.17.clone.inverse_ref.table_ref) | copy-start | bytes 2359300
  84.7 1.3 copy-start.15
  86.1 54.9 %all-to-all-start.1 = ((f32[32,8,8,256]{3,2,1,0:T(8,128)}), f32[32,8,8,256]{3,2,1,0:T(8,128)S(1)}, u32[]{:S(2)}, u32[]{:S(2)}) async-start(f32[32,8,8,256]{3,2,1,0:T(8,128)} %copy-done.18), calls=%async_computation.1 | async-start | bytes 4194304 | tf_op jit(solution)/shard_map/all_to_all | solution.py:295
  90.8 1.6 copy-start.16
  92.4 1.6 copy-start.27
  93.9 1.1 copy-start.32
  104.7 1.3 copy-start.17
  141.0 1.4 copy-start.13
  142.4 54.9 %all-to-all-start.2 = ((f32[32,8,8,256]{3,2,1,0:T(8,128)}), f32[32,8,8,256]{3,2,1,0:T(8,128)S(1)}, u32[]{:S(2)}, u32[]{:S(2)}) async-start(f32[32,8,8,256]{3,2,1,0:T(8,128)} %bitcast.9), calls=%async_computation.2 | async-start | bytes 4194304 | tf_op jit(solution)/shard_map/all_to_all | solution.py:295
  147.0 1.6 copy-start.14
  148.6 1.6 copy-start.28
  150.2 1.1 copy-start.33
  160.9 1.4 copy-start.10
  197.3 1.3 copy-start.11
  198.6 61.3 %all-to-all-start.3 = ((f32[32,8,8,256]{3,2,1,0:T(8,128)}), f32[32,8,8,256]{3,2,1,0:T(8,128)S(1)}, u32[]{:S(2)}, u32[]{:S(2)}) async-start(f32[32,8,8,256]{3,2,1,0:T(8,128)} %bitcast.6), calls=%async_computation.3 | async-start | bytes 4194304 | tf_op jit(solution)/shard_map/all_to_all | solution.py:295
  203.3 1.6 copy-start.12
  208.1 0.7 copy-start.23
  208.8 25.8 %collective-permute-start = (f32[8,32,256]{2,1,0:T(8,128)S(1)}, f32[8,32,256]{2,1,0:T(8,128)S(1)}, u32[]{:S(2)}, u32[]{:S(2)}) collective-permute-start(f32[8,32,256]{2,1,0:T(8,128)S(1)} %get-tuple-element.38), channel_id=1, source_target_pairs={{0,224},{32,0},{64,32},{96,64},{128,96},{160,128},{192,160},{224,1... | collective-permute-start | bytes 786440 | tf_op jit(solution)/shard_map/ppermute | solution.py:299
  213.4 40.2 %collective-permute-start.1 = (f32[8,32,256]{2,1,0:T(8,128)S(1)}, f32[8,32,256]{2,1,0:T(8,128)S(1)}, u32[]{:S(2)}, u32[]{:S(2)}) collective-permute-start(f32[8,32,256]{2,1,0:T(8,128)S(1)} %get-tuple-element.41), channel_id=1, source_target_pairs={{0,32},{32,64},{64,96},{96,128},{128,160},{160,192},{192,224},{224... | collective-permute-start | bytes 786440 | tf_op jit(solution)/shard_map/ppermute | solution.py:299
  213.4 40.2 %collective-permute-start.2 = (f32[8,32,256]{2,1,0:T(8,128)S(1)}, f32[8,32,256]{2,1,0:T(8,128)S(1)}, u32[]{:S(2)}, u32[]{:S(2)}) collective-permute-start(f32[8,32,256]{2,1,0:T(8,128)S(1)} %get-tuple-element.42), channel_id=1, source_target_pairs={{0,64},{32,96},{64,128},{96,160},{128,192},{160,224},{192,0},{224,... | collective-permute-start | bytes 786440 | tf_op jit(solution)/shard_map/ppermute | solution.py:299
  213.8 39.7 %collective-permute-start.3 = (f32[8,32,256]{2,1,0:T(8,128)S(1)}, f32[8,32,256]{2,1,0:T(8,128)S(1)}, u32[]{:S(2)}, u32[]{:S(2)}) collective-permute-start(f32[8,32,256]{2,1,0:T(8,128)S(1)} %get-tuple-element.43), channel_id=1, source_target_pairs={{0,96},{32,128},{64,160},{96,192},{128,224},{160,0},{192,32},{224,... | collective-permute-start | bytes 786440 | tf_op jit(solution)/shard_map/ppermute | solution.py:299
  217.9 35.6 %collective-permute-start.4 = (f32[8,32,256]{2,1,0:T(8,128)S(1)}, f32[8,32,256]{2,1,0:T(8,128)S(1)}, u32[]{:S(2)}, u32[]{:S(2)}) collective-permute-start(f32[8,32,256]{2,1,0:T(8,128)S(1)} %get-tuple-element.44), channel_id=1, source_target_pairs={{0,128},{32,160},{64,192},{96,224},{128,0},{160,32},{192,64},{224,... | collective-permute-start | bytes 786440 | tf_op jit(solution)/shard_map/ppermute | solution.py:299
  234.6 22.8 %collective-permute-start.5 = (f32[8,32,256]{2,1,0:T(8,128)S(1)}, f32[8,32,256]{2,1,0:T(8,128)S(1)}, u32[]{:S(2)}, u32[]{:S(2)}) collective-permute-start(f32[8,32,256]{2,1,0:T(8,128)S(1)} %get-tuple-element.45), channel_id=1, source_target_pairs={{0,160},{32,192},{64,224},{96,0},{128,32},{160,64},{192,96},{224,1... | collective-permute-start | bytes 786440 | tf_op jit(solution)/shard_map/ppermute | solution.py:299
  253.5 6.4 %collective-permute-start.6 = (f32[8,32,256]{2,1,0:T(8,128)S(1)}, f32[8,32,256]{2,1,0:T(8,128)S(1)}, u32[]{:S(2)}, u32[]{:S(2)}) collective-permute-start(f32[8,32,256]{2,1,0:T(8,128)S(1)} %get-tuple-element.46), channel_id=1, source_target_pairs={{0,192},{32,224},{64,0},{96,32},{128,64},{160,96},{192,128},{224,1... | collective-permute-start | bytes 786440 | tf_op jit(solution)/shard_map/ppermute | solution.py:299
  253.6 0.7 copy-start.25
  257.4 0.7 copy-start.21
  259.9 1.1 copy-start.30
  261.0 17.5 %copy-start.1 = (bf16[3,8,256,256]{3,2,1,0:T(8,128)(2,1)S(1)}, bf16[3,8,256,256]{3,2,1,0:T(8,128)(2,1)}, u32[]{:S(2)}) copy-start(bf16[3,8,256,256]{3,2,1,0:T(8,128)(2,1)} %shift_ref.17) | copy-start | bytes 9437188
  261.0 17.5 %copy-start.3 = (bf16[2,8,256,256]{3,2,1,0:T(8,128)(2,1)S(1)}, bf16[2,8,256,256]{3,2,1,0:T(8,128)(2,1)}, u32[]{:S(2)}) copy-start(bf16[2,8,256,256]{3,2,1,0:T(8,128)(2,1)} %rho_ref.17) | copy-start | bytes 6291460
  261.0 17.5 %copy-start.5 = (s32[8,256,256]{2,1,0:T(8,128)S(1)}, s32[8,256,256]{2,1,0:T(8,128)}, u32[]{:S(2)}) copy-start(s32[8,256,256]{2,1,0:T(8,128)} %support_ref.17) | copy-start | bytes 6291460
  261.0 17.5 %copy-start.6 = (bf16[512,512]{1,0:T(8,128)(2,1)S(1)}, bf16[512,512]{1,0:T(8,128)(2,1)}, u32[]{:S(2)}) copy-start(bf16[512,512]{1,0:T(8,128)(2,1)} %constant.19.clone.refs_3_) | copy-start | bytes 1572868
  261.1 17.5 %copy-start.7 = (bf16[512,512]{1,0:T(8,128)(2,1)S(1)}, bf16[512,512]{1,0:T(8,128)(2,1)}, u32[]{:S(2)}) copy-start(bf16[512,512]{1,0:T(8,128)(2,1)} %constant.18.clone.refs_2_) | copy-start | bytes 1572868
  261.1 17.5 %copy-start.24 = (f32[8,32,256]{2,1,0:T(8,128)S(1)}, f32[8,32,256]{2,1,0:T(8,128)}, u32[]{:S(2)}) copy-start(f32[8,32,256]{2,1,0:T(8,128)} %copy-done.23) | copy-start | bytes 786436
  264.2 16.1 %collective-permute-start.13 = (f32[8,32,256]{2,1,0:T(8,128)S(1)}, f32[8,32,256]{2,1,0:T(8,128)S(1)}, u32[]{:S(2)}, u32[]{:S(2)}) collective-permute-start(f32[8,32,256]{2,1,0:T(8,128)S(1)} %get-tuple-element.54), channel_id=1, source_target_pairs={{0,128},{32,160},{64,192},{96,224},{128,0},{160,32},{192,64},{224,... | collective-permute-start | bytes 786440 | tf_op jit(solution)/shard_map/ppermute | solution.py:299
  268.8 14.3 %collective-permute-start.12 = (f32[8,32,256]{2,1,0:T(8,128)S(1)}, f32[8,32,256]{2,1,0:T(8,128)S(1)}, u32[]{:S(2)}, u32[]{:S(2)}) collective-permute-start(f32[8,32,256]{2,1,0:T(8,128)S(1)} %get-tuple-element.53), channel_id=1, source_target_pairs={{0,96},{32,128},{64,160},{96,192},{128,224},{160,0},{192,32},{224,... | collective-permute-start | bytes 786440 | tf_op jit(solution)/shard_map/ppermute | solution.py:299
  270.4 18.3 %collective-permute-start.11 = (f32[8,32,256]{2,1,0:T(8,128)S(1)}, f32[8,32,256]{2,1,0:T(8,128)S(1)}, u32[]{:S(2)}, u32[]{:S(2)}) collective-permute-start(f32[8,32,256]{2,1,0:T(8,128)S(1)} %get-tuple-element.52), channel_id=1, source_target_pairs={{0,160},{32,192},{64,224},{96,0},{128,32},{160,64},{192,96},{224,1... | collective-permute-start | bytes 786440 | tf_op jit(solution)/shard_map/ppermute | solution.py:299
  274.7 21.1 %collective-permute-start.7 = (f32[8,32,256]{2,1,0:T(8,128)S(1)}, f32[8,32,256]{2,1,0:T(8,128)S(1)}, u32[]{:S(2)}, u32[]{:S(2)}) collective-permute-start(f32[8,32,256]{2,1,0:T(8,128)S(1)} %get-tuple-element.48), channel_id=1, source_target_pairs={{0,224},{32,0},{64,32},{96,64},{128,96},{160,128},{192,160},{224,1... | collective-permute-start | bytes 786440 | tf_op jit(solution)/shard_map/ppermute | solution.py:299
  275.1 15.3 %collective-permute-start.10 = (f32[8,32,256]{2,1,0:T(8,128)S(1)}, f32[8,32,256]{2,1,0:T(8,128)S(1)}, u32[]{:S(2)}, u32[]{:S(2)}) collective-permute-start(f32[8,32,256]{2,1,0:T(8,128)S(1)} %get-tuple-element.51), channel_id=1, source_target_pairs={{0,64},{32,96},{64,128},{96,160},{128,192},{160,224},{192,0},{224,... | collective-permute-start | bytes 786440 | tf_op jit(solution)/shard_map/ppermute | solution.py:299
  278.6 1.9 copy-start.26
  280.3 11.9 %collective-permute-start.9 = (f32[8,32,256]{2,1,0:T(8,128)S(1)}, f32[8,32,256]{2,1,0:T(8,128)S(1)}, u32[]{:S(2)}, u32[]{:S(2)}) collective-permute-start(f32[8,32,256]{2,1,0:T(8,128)S(1)} %get-tuple-element.50), channel_id=1, source_target_pairs={{0,192},{32,224},{64,0},{96,32},{128,64},{160,96},{192,128},{224,1... | collective-permute-start | bytes 786440 | tf_op jit(solution)/shard_map/ppermute | solution.py:299
  283.1 10.9 %collective-permute-start.8 = (f32[8,32,256]{2,1,0:T(8,128)S(1)}, f32[8,32,256]{2,1,0:T(8,128)S(1)}, u32[]{:S(2)}, u32[]{:S(2)}) collective-permute-start(f32[8,32,256]{2,1,0:T(8,128)S(1)} %get-tuple-element.49), channel_id=1, source_target_pairs={{0,32},{32,64},{64,96},{96,128},{128,160},{160,192},{192,224},{224... | collective-permute-start | bytes 786440 | tf_op jit(solution)/shard_map/ppermute | solution.py:299
  286.9 1.8 copy-start.22

commit v2 on v1

v2 whole, which is shorter than its diff:
```python
import functools
import math

import jax
import jax.numpy as jnp
import ml_dtypes
import numpy as np
from jax import lax
from jax.experimental import pallas as pl
from jax.experimental.pallas import tpu as pltpu
from jax.sharding import PartitionSpec as P

N = 256
CH = 2
KC = N // CH
SLABS = 32
XL = 8
NREF = 8
HEAD_ROWS = 32
HALF = XL // 2
R_ORDER = (4, 3, 5, 2, 6, 1, 7)
BF = jnp.bfloat16
F32 = jnp.float32


def split_np(table):
    high = table.astype(ml_dtypes.bfloat16)
    low = (table - high.astype(np.float64)).astype(ml_dtypes.bfloat16)
    return high, low


def dft_np():
    n = np.arange(N)
    angle = 2.0 * np.pi * (np.outer(n, n) % N) / N
    return np.cos(angle) / math.sqrt(N), -np.sin(angle) / math.sqrt(N)


def left_table(inverse):
    re, im = dft_np()
    high, low = split_np(np.concatenate([re, -im if inverse else im], 0))
    return np.concatenate([high, high, low], 1)


def halves_of_slabs(table):
    rows = np.arange(N).reshape(SLABS, 2, XL // 2).transpose(1, 0, 2).reshape(-1)
    return table[np.concatenate([rows, rows + N])]


def packed_columns():
    chunk = np.arange(N) // KC
    inner = np.arange(N) % KC
    real = chunk * 2 * KC + inner
    return real, real + KC


def right_forward():
    re, im = dft_np()
    real, imag = packed_columns()
    table = np.zeros((2 * N, 2 * N))
    table[:N, real] = re
    table[:N, imag] = im
    table[N:, real] = -im
    table[N:, imag] = re
    high, low = split_np(table)
    return np.concatenate([high, high, low], 0)


def right_inverse():
    re, im = dft_np()
    real, imag = packed_columns()
    table = np.zeros((2 * N, 2 * N))
    table[real, :N] = re
    table[real, N:] = -im
    table[imag, :N] = im
    table[imag, N:] = re
    return split_np(table)


def sine_coefficients():
    b = 0.25 * np.cos((np.arange(400) + 0.5) / 400 * np.pi / 2)
    powers = np.stack([b ** (2 * k + 1) for k in range(6)], 1)
    return [float(v) for v in np.linalg.lstsq(powers, np.sin(2 * np.pi * b), rcond=None)[0]]


SINE = sine_coefficients()


def sine_turns(b):
    q = b * b
    acc = jnp.full_like(b, SINE[5])
    for k in range(4, -1, -1):
        acc = acc * q + SINE[k]
    return acc * b


def cos_sin_turns(t):
    t = t - jnp.round(t)
    cosine = sine_turns(0.25 - jnp.abs(t))
    u = t - 0.25
    u = u - jnp.round(u)
    return cosine, sine_turns(0.25 - jnp.abs(u))


def split(value):
    high = value.astype(BF)
    return high, (value - high.astype(F32)).astype(BF)


def left_multiply(table, packed):
    return left_split(table, *split(packed))


def left_split(table, high, low):
    both = jnp.dot(table, jnp.concatenate([high, low, high], 0), preferred_element_type=F32)
    real = both[:N, :KC] - both[N:, KC:]
    imag = both[:N, KC:] + both[N:, :KC]
    return jnp.concatenate([real, imag], 1)


def object_rows(hkl, rho_ref, shift_ref, support_ref, high_ref, low_ref, start, rows):
    at = pl.ds(start, rows)
    u = [shift_ref[c, 0, at, :].astype(F32) for c in range(3)]
    mask = support_ref[0, at, :].astype(F32)
    cosine, sine = cos_sin_turns(hkl[0] * u[0] + hkl[1] * u[1] + hkl[2] * u[2])
    real = mask * rho_ref[0, 0, at, :].astype(F32)
    imag = mask * rho_ref[1, 0, at, :].astype(F32)
    for part, value in enumerate((real * cosine - imag * sine, real * sine + imag * cosine)):
        high, low = split(value)
        high_ref[at, part * N : (part + 1) * N] = high
        low_ref[at, part * N : (part + 1) * N] = low


def head_kernel(miller_ref, rho_ref, shift_ref, support_ref, table_ref, left_ref, out_ref, high_ref, low_ref, ah_ref, al_ref):
    i = pl.program_id(0)
    r = lax.axis_index("refl")
    hkl = [miller_ref[c, r].astype(F32) for c in range(3)]
    now, before = lax.rem(i, 2), lax.rem(i + 1, 2)
    out_ref[:, 0] = left_split(left_ref[...], ah_ref[now], al_ref[now]).reshape(SLABS, XL, 2 * KC)
    high = high_ref[before]
    a = jnp.dot(jnp.concatenate([high, low_ref[before], high], 1), table_ref[...], preferred_element_type=F32)
    ah_ref[before], al_ref[before] = split(a)
    for row in range(0, N, HEAD_ROWS):
        object_rows(hkl, rho_ref, shift_ref, support_ref, high_ref.at[now], low_ref.at[now], row, HEAD_ROWS)


def x_kernel(in_ref, amp_ref, forward_ref, inverse_ref, *refs):
    outs, (real_ref, imag_ref, sems) = refs[:-3], refs[-3:]
    parts = ((real_ref, pl.ds(0, KC)), (imag_ref, pl.ds(KC, KC)))
    copies = [
        pltpu.make_async_copy(in_ref.at[:, lanes], part, sems.at[i]) for i, (part, lanes) in enumerate(parts)
    ]
    for copy in copies:
        copy.start()
    for copy in copies:
        copy.wait()

    def step(i, carry):
        at = pl.ds(i, N, stride=XL)
        spec = left_multiply(forward_ref[...], jnp.concatenate([real_ref[at, :], imag_ref[at, :]], 1))
        real, imag = spec[:, :KC], spec[:, KC:]
        ratio = amp_ref[at, :] * lax.rsqrt(jnp.maximum(real * real + imag * imag, 0.25))
        resid = jnp.concatenate([real - ratio * real, imag - ratio * imag], 1)
        back = left_multiply(inverse_ref[...], resid)
        real_ref[at, :] = back[:, :KC]
        imag_ref[at, :] = back[:, KC:]
        return carry

    lax.fori_loop(0, XL, step, 0)
    rows = N * XL // len(outs)
    copies = [
        pltpu.make_async_copy(part.at[pl.ds(n * rows, rows), :], out.at[:, lanes], sems.at[2 * n + i])
        for n, out in enumerate(outs)
        for i, (part, lanes) in enumerate(parts)
    ]
    for copy in copies:
        copy.start()
    for copy in copies:
        copy.wait()


def y_inverse_kernel(idx_ref, in_ref, table_ref, *refs):
    outs, (u_ref, t_ref, sems) = refs[:NREF], refs[NREF:]
    r = idx_ref[0]
    planes = u_ref.shape[0]
    copies = [pltpu.make_async_copy(in_ref.at[:, x], u_ref.at[x], sems.at[x]) for x in range(planes)]
    for copy in copies:
        copy.start()
    for x in range(planes):
        copies[x].wait()
        t_ref[x] = left_multiply(table_ref[...], u_ref[x].reshape(N, 2 * KC))
    copies = []
    for s in range(NREF):
        start = pl.multiple_of(lax.rem(r + s, NREF) * 32, 32)
        if planes < XL:
            outs[s][...] = t_ref[:, pl.ds(start, 32), :]
        else:
            copies.append(pltpu.make_async_copy(t_ref.at[:, pl.ds(start, 32), :], outs[s], sems.at[s]))
            copies[-1].start()
    for copy in copies:
        copy.wait()


def gradient_kernel(shift_by, adds, idx_ref, miller_ref, rho_ref, shift_ref, support_ref, *refs):
    ins, high_ref, low_ref = refs[:CH], refs[CH], refs[CH + 1]
    sums = refs[CH + 2 : -3]
    rho_out, shift_out, back_ref = refs[-3:]
    g = lax.rem(idx_ref[0] + NREF - shift_by, NREF)
    h, k, l = (miller_ref[c, g].astype(F32) for c in range(3))
    high, low = split(jnp.concatenate([ref[...].reshape(HALF * 32, 2 * KC) for ref in ins], 1))
    dot = functools.partial(jnp.dot, preferred_element_type=F32)
    back_ref[...] = dot(high, high_ref[...]) + dot(low, high_ref[...]) + dot(high, low_ref[...])

    def step(x, carry):
        at = pl.ds(pl.multiple_of(x * 32, 32), 32)
        u = [shift_ref[c, x].astype(F32) for c in range(3)]
        mask = support_ref[x].astype(F32) * (1.0 / NREF)
        cosine, sine = cos_sin_turns(h * u[0] + k * u[1] + l * u[2])
        real, imag = back_ref[at, :N], back_ref[at, N:]
        p = mask * (cosine * real + sine * imag)
        q = mask * (cosine * imag - sine * real)
        twist = rho_ref[0, x].astype(F32) * q - rho_ref[1, x].astype(F32) * p
        for out, old, n, value in (
            (rho_out, 0, 0, p),
            (rho_out, 0, 1, q),
            (shift_out, 1, 0, h * twist),
            (shift_out, 1, 1, k * twist),
            (shift_out, 1, 2, l * twist),
        ):
            out[n, x] = sums[old][n, x] + value if adds else value
        return carry

    lax.fori_loop(0, HALF, step, 0)


SMEM = pl.BlockSpec(memory_space=pltpu.SMEM)
VMEM = pl.BlockSpec(memory_space=pltpu.VMEM)
HBM = pl.BlockSpec(memory_space=pltpu.HBM)


def cost(flops, size):
    return pl.CostEstimate(flops=int(flops), bytes_accessed=int(size), transcendentals=0)


def f32(*shape):
    return jax.ShapeDtypeStruct(shape, F32)


def params(mib):
    return pltpu.CompilerParams(vmem_limit_bytes=mib * 1024 * 1024)


def hbm(*shape):
    return pltpu.HBM(shape, F32)


def in_hbm(value):
    return pltpu.with_memory_space_constraint(value, pltpu.HBM)


def after(value, *earlier):
    return lax.optimization_barrier((value, earlier))[0]


def head(c, millers, density, displacement, support):
    plane = lambda i: jnp.minimum(i, XL - 1)
    last = lambda i: jnp.maximum(i - 2, 0)
    return pl.pallas_call(
        head_kernel,
        grid=(XL + 2,),
        in_specs=[
            SMEM,
            pl.BlockSpec((2, 1, N, N), lambda i: (0, plane(i), 0, 0)),
            pl.BlockSpec((3, 1, N, N), lambda i: (0, plane(i), 0, 0)),
            pl.BlockSpec((1, N, N), lambda i: (plane(i), 0, 0)),
            pl.BlockSpec((6 * N, 2 * KC), lambda i: (0, c)),
            pl.BlockSpec((2 * N, 3 * N), lambda i: (0, 0)),
        ],
        out_specs=pl.BlockSpec((SLABS, 1, XL, 2 * KC), lambda i: (0, last(i), 0, 0)),
        out_shape=f32(SLABS, XL, XL, 2 * KC),
        scratch_shapes=[pltpu.VMEM((2, N, 2 * N), BF)] * 2 + [pltpu.VMEM((2, N, 2 * KC), BF)] * 2,
        compiler_params=params(60),
        cost_estimate=cost(6.4e9, 16e6),
        name=f"head_{c}",
    )(millers, density, displacement, support, jnp.asarray(right_forward()), jnp.asarray(left_table(False)))


def body(density, displacement, support, millers, amplitude):
    r = lax.axis_index("refl")
    idx = jnp.stack([r]).astype(jnp.int32)
    forward, inverse = jnp.asarray(left_table(False)), jnp.asarray(left_table(True))
    high, low = (jnp.asarray(t) for t in right_inverse())
    amp = amplitude.reshape(N * XL, N)
    millers = millers.T

    def x_both(c, part):
        pieces = c + 1
        table = inverse if c == 0 else jnp.asarray(halves_of_slabs(left_table(True)))
        parts = pl.pallas_call(
            x_kernel,
            grid=(1,),
            in_specs=[HBM, pl.BlockSpec((N * XL, KC), lambda i: (0, c)), VMEM, VMEM],
            out_specs=[HBM] * pieces,
            out_shape=[hbm(N * XL // pieces, 2 * KC)] * pieces,
            scratch_shapes=[pltpu.VMEM((N * XL, KC), F32)] * 2 + [pltpu.SemaphoreType.DMA((4,))],
            compiler_params=params(24),
            cost_estimate=cost(6.4e9, 24e6),
            name=f"x_{c}",
        )(in_hbm(part.reshape(N * XL, 2 * KC)), amp, forward, table)
        return [p.reshape(SLABS, XL // pieces, XL, 2 * KC) for p in parts]

    def y_inverse(name, part):
        planes = part.shape[1]
        return pl.pallas_call(
            y_inverse_kernel,
            in_specs=[SMEM, HBM, VMEM],
            out_specs=[VMEM if planes < XL else HBM] * NREF,
            out_shape=[(f32 if planes < XL else hbm)(planes, 32, 2 * KC)] * NREF,
            scratch_shapes=[
                pltpu.VMEM((planes, SLABS, XL, 2 * KC), F32),
                pltpu.VMEM((planes, N, 2 * KC), F32),
                pltpu.SemaphoreType.DMA((XL,)),
            ],
            compiler_params=params(24),
            cost_estimate=cost(0.4e9 * planes, 1.5e6 * planes),
            name=f"y_inverse_{name}",
        )(idx, in_hbm(part), inverse)

    def over_grid(part):
        return lax.all_to_all(part, "grid", 0, 0, tiled=True)

    def over_refl(parts):
        ring = lambda s: [(i, (i + s) % NREF) for i in range(NREF)]
        moved = {s: lax.ppermute(parts[s], "refl", ring(s)) for s in R_ORDER}
        return [parts[0]] + [moved[s] for s in range(1, NREF)]

    def gradient(s, half, parts, sums):
        adds = s > 0
        out_block = lambda n: pl.BlockSpec((n, HALF, 32, N), lambda i, idx: (0, half, 0, 0))
        whole = lambda i, idx: (0, 0)
        return tuple(
            pl.pallas_call(
                functools.partial(gradient_kernel, s, adds),
                grid_spec=pltpu.PrefetchScalarGridSpec(
                    num_scalar_prefetch=1,
                    grid=(1,),
                    in_specs=[
                        SMEM,
                        pl.BlockSpec((2, HALF, 32, N), lambda i, idx: (0, half, idx[0], 0)),
                        pl.BlockSpec((3, HALF, 32, N), lambda i, idx: (0, half, idx[0], 0)),
                        pl.BlockSpec((HALF, 32, N), lambda i, idx: (half, idx[0], 0)),
                        pl.BlockSpec((HALF, 32, 2 * KC), lambda i, idx: (half, 0, 0)),
                        pl.BlockSpec((HALF, 32, 2 * KC), lambda i, idx: (0, 0, 0)),
                    ]
                    + [pl.BlockSpec((2 * N, 2 * N), whole)] * 2
                    + [out_block(2 + n) if adds else pl.BlockSpec(memory_space=pl.ANY) for n, _ in enumerate(sums)],
                    out_specs=[out_block(2), out_block(3)],
                    scratch_shapes=[pltpu.VMEM((HALF * 32, 2 * N), F32)],
                ),
                out_shape=[f32(2, XL, 32, N), f32(3, XL, 32, N)],
                input_output_aliases={9 + n: n for n, _ in enumerate(sums)},
                compiler_params=params(24),
                cost_estimate=cost(0.4e9, 3e6),
                name=f"gradient_{half}_{s}",
            )(idx, millers, density, displacement, support, *parts, high, low, *sums)
        )

    f0 = over_grid(head(0, millers, density, displacement, support))
    f1 = over_grid(after(head(1, millers, density, displacement, support), f0))
    b0 = over_grid(after(x_both(0, f0)[0], f1))
    halves = x_both(1, f1)
    b1 = [over_grid(after(halves[0], b0))]
    r0 = over_refl(y_inverse("0", b0))
    b1.append(over_grid(after(halves[1], b1[0], *(r0[s] for s in R_ORDER[:4]))))
    r1 = over_refl(y_inverse("1a", after(b1[0], *r0)))
    sums = ()
    for s in (0,) + R_ORDER:
        sums = gradient(s, 0, (in_hbm(r0[s]), r1[s]), sums)
    r1 = over_refl(y_inverse("1b", after(b1[1], *sums)))
    for s in (0,) + R_ORDER:
        sums = gradient(s, 1, (in_hbm(r0[s]), r1[s]), sums)
    return sums


def solution(mesh):
    in_specs = (
        P(None, "grid", None, None),
        P(None, "grid", None, None),
        P("grid", None, None),
        P(),
        P("refl", None, "grid", None),
    )
    out_specs = (P(None, "grid", "refl", None), P(None, "grid", "refl", None))
    return jax.shard_map(body, mesh=mesh, in_specs=in_specs, out_specs=out_specs, check_vma=False)
```

time: 304 us -> 349 us (1.15); the launches traced: 299 us -> 347 us
  Pallas kernels: 56.9 us -> 103 us
  local copies, waits for them, and re-layouts: 34.4 us -> 8.58 us
  waiting for transfers between devices: 133 us -> 157 us
  starting transfers between devices: 72.8 us -> 78.1 us
    pallas_call x15 -> x23, Pallas kernels: 56.9 us -> 103 us  [the longest x16 42.6 us: gradient(): pl.pallas_call(functools.partial(gradient_kernel, s, adds), grid_spec=plt...]
    unnamed x69 -> x56, local copies, waits for them, and re-layouts: 34.4 us -> 8.58 us
    ppermute x14 -> x21, waiting for transfers between devices: 20 us -> 44.9 us  [over_refl(): moved = {s: lax.ppermute(parts[s], 'refl', ring(s)) for s in R_ORDER}]
    all_to_all x4 -> x5, starting transfers between devices: 24.1 us -> 31.6 us  [over_grid(): return lax.all_to_all(part, 'grid', 0, 0, tiled=True)]
    ppermute x14 -> x21, starting transfers between devices: 48.7 us -> 46.6 us  [over_refl(): moved = {s: lax.ppermute(parts[s], 'refl', ring(s)) for s in R_ORDER}]
    all_to_all x4 -> x5, waiting for transfers between devices: 114 us -> 112 us  [over_grid(): return lax.all_to_all(part, 'grid', 0, 0, tiled=True)]
  transfers between devices with their start and end apart: 18 -> 26, of which waited for: 7 -> 8; matrix products, arithmetic and copies ran while one was open for 0% -> 0% of each run, Pallas kernels for 13% -> 25%
where the time goes in v2:
time: 349 us; the launch traced here: 347 us
  waiting for transfers between devices  157 us (45%)
  Pallas kernels  103 us (30%)
  starting transfers between devices  78.1 us (22%)
  local copies, waits for them, and re-layouts  8.58 us (2%)
    all_to_all x5, waiting for transfers between devices, over_grid(): return lax.all_to_all(part, 'grid', 0, 0, tiled=True)  112 us
    ppermute x21, starting transfers between devices, over_refl(): moved = {s: lax.ppermute(parts[s], 'refl', ring(s)) for s in R_ORDER}  46.6 us
    ppermute x21, waiting for transfers between devices, over_refl(): moved = {s: lax.ppermute(parts[s], 'refl', ring(s)) for s in R_ORDER}  44.9 us
    pallas_call x16, Pallas kernels, gradient(): pl.pallas_call(functools.partial(gradient_kernel, s, adds), grid_spec=plt...  42.6 us
    all_to_all x5, starting transfers between devices, over_grid(): return lax.all_to_all(part, 'grid', 0, 0, tiled=True)  31.6 us
    pallas_call x2, Pallas kernels, x_both(): pl.pallas_call(x_kernel, grid=(1,), in_specs=[HBM, pl.BlockSpec((N * XL,...  24.3 us
    pallas_call x2, Pallas kernels, head(): pl.pallas_call(head_kernel, grid=(XL + 2,), in_specs=[SMEM, pl.BlockSpec(...  22.1 us
    pallas_call x3, Pallas kernels, y_inverse(): pl.pallas_call(y_inverse_kernel, in_specs=[SMEM, HBM, VMEM], out_specs=[V...  13.7 us
  transfers between devices with their start and end apart: 26, of which 8 were waited for; matrix products, arithmetic and copies ran while one was open for 0% of the time, Pallas kernels for 25%

profile of v2, /device:TPU:8, one launch (start us, length us, event | category | flops | bytes accessed | tf_op | source)
XLA Modules:
  0.0 347.5 jit_solution(4070496389634120553)
XLA Ops:
  0.6 11.1 %head_0.1 = f32[32,8,8,256]{3,2,1,0:T(8,128)} custom-call(s32[3,8]{1,0:T(4,128)} %bitcast.8, bf16[2,8,256,256]{3,2,1,0:T(8,128)(2,1)} %rho_ref.35, bf16[3,8,256,256]{3,2,1,0:T(8,128)(2,1)} %shift_ref.35, s32[8,256,256]{2,1,0:T(8,128)} %support_ref.35, bf16[1536,512]{1,0:T(8,128)(2,1)} %constant.22.clone.table_ref, ...), custom_call_target="tpu_custom_call" | custom-call | flops 6400000000 | bytes 16000000 | tf_op jit(solution)/shard_map/head_0/pallas_call | solution.py:267
  11.7 10.1 %all-to-all-start = ((f32[32,8,8,256]{3,2,1,0:T(8,128)}), f32[32,8,8,256]{3,2,1,0:T(8,128)}, u32[]{:S(2)}, u32[]{:S(2)}) async-start(f32[32,8,8,256]{3,2,1,0:T(8,128)} %head_0.1), calls=%async_computation | async-start | bytes 4194304 | tf_op jit(solution)/shard_map/all_to_all | solution.py:329
  21.8 11.1 %head_1.1 = f32[32,8,8,256]{3,2,1,0:T(8,128)} custom-call(s32[3,8]{1,0:T(4,128)} %bitcast.9, bf16[2,8,256,256]{3,2,1,0:T(8,128)(2,1)} %rho_ref.35, bf16[3,8,256,256]{3,2,1,0:T(8,128)(2,1)} %shift_ref.35, s32[8,256,256]{2,1,0:T(8,128)} %support_ref.35, bf16[1536,512]{1,0:T(8,128)(2,1)} %constant.22.clone.table_ref, ...), custom_call_target="tpu_custom_call" | custom-call | flops 6400000000 | bytes 16000000 | tf_op jit(solution)/shard_map/head_1/pallas_call | solution.py:267
  32.9 39.2 %all-to-all-done = f32[32,8,8,256]{3,2,1,0:T(8,128)} async-done(((f32[32,8,8,256]{3,2,1,0:T(8,128)}), f32[32,8,8,256]{3,2,1,0:T(8,128)}, u32[]{:S(2)}, u32[]{:S(2)}) %all-to-all-start) | async-done | bytes 2097184 | tf_op jit(solution)/shard_map/all_to_all | solution.py:329
  72.1 4.7 %all-to-all-start.1 = ((f32[32,8,8,256]{3,2,1,0:T(8,128)}), f32[32,8,8,256]{3,2,1,0:T(8,128)}, u32[]{:S(2)}, u32[]{:S(2)}) async-start(f32[32,8,8,256]{3,2,1,0:T(8,128)} %head_1.1), calls=%async_computation.1 | async-start | bytes 4194304 | tf_op jit(solution)/shard_map/all_to_all | solution.py:329
  76.9 0.0 copy-start.14
  76.9 1.1 copy-done.14
  78.0 12.2 %x_0.1 = f32[2048,256]{1,0:T(8,128)} custom-call(f32[2048,256]{1,0:T(8,128)} %bitcast.2.in_ref, f32[2048,256]{1,0:T(8,128)S(1)} %bitcast.26, bf16[512,768]{1,0:T(8,128)(2,1)S(1)} %copy-done.14, bf16[512,768]{1,0:T(8,128)(2,1)S(1)} %copy-done.11), custom_call_target="tpu_custom_call" | custom-call | flops 6400000000 | bytes 24000000 | tf_op jit(solution)/shard_map/x_0/pallas_call | solution.py:298
  90.2 37.0 %all-to-all-done.1 = f32[32,8,8,256]{3,2,1,0:T(8,128)} async-done(((f32[32,8,8,256]{3,2,1,0:T(8,128)}), f32[32,8,8,256]{3,2,1,0:T(8,128)}, u32[]{:S(2)}, u32[]{:S(2)}) %all-to-all-start.1) | async-done | bytes 2097184 | tf_op jit(solution)/shard_map/all_to_all | solution.py:329
  127.1 4.7 %all-to-all-start.2 = ((f32[32,8,8,256]{3,2,1,0:T(8,128)}), f32[32,8,8,256]{3,2,1,0:T(8,128)}, u32[]{:S(2)}, u32[]{:S(2)}) async-start(f32[32,8,8,256]{3,2,1,0:T(8,128)} %bitcast.28), calls=%async_computation.2 | async-start | bytes 4194304 | tf_op jit(solution)/shard_map/all_to_all | solution.py:329
  131.9 0.0 copy-start.15
  131.9 1.1 copy-done.15
  133.0 1.1 copy-done.16
  134.2 12.2 %x_1.1 = (f32[1024,256]{1,0:T(8,128)}, f32[1024,256]{1,0:T(8,128)}) custom-call(f32[2048,256]{1,0:T(8,128)} %bitcast.5.in_ref, f32[2048,256]{1,0:T(8,128)S(1)} %bitcast.27, bf16[512,768]{1,0:T(8,128)(2,1)S(1)} %copy-done.15, bf16[512,768]{1,0:T(8,128)(2,1)S(1)} %copy-done.16), custom_call_target="tpu_custom_call" | custom-call | flops 6400000000 | bytes 24000000 | tf_op jit(solution)/shard_map/x_1/pallas_call | solution.py:298
  146.3 35.9 %all-to-all-done.2.in_ref = f32[32,8,8,256]{3,2,1,0:T(8,128)} async-done(((f32[32,8,8,256]{3,2,1,0:T(8,128)}), f32[32,8,8,256]{3,2,1,0:T(8,128)}, u32[]{:S(2)}, u32[]{:S(2)}) %all-to-all-start.2) | async-done | bytes 2097184 | tf_op jit(solution)/shard_map/all_to_all | solution.py:329
  182.2 4.7 %all-to-all-start.3 = ((f32[32,4,8,256]{3,2,1,0:T(8,128)}), f32[32,4,8,256]{3,2,1,0:T(8,128)S(1)}, u32[]{:S(2)}, u32[]{:S(2)}) async-start(f32[32,4,8,256]{3,2,1,0:T(8,128)} %bitcast.29), calls=%async_computation.3 | async-start | bytes 2097152 | tf_op jit(solution)/shard_map/all_to_all | solution.py:329
  186.9 6.8 %y_inverse_0.1 = (f32[8,32,256]{2,1,0:T(8,128)}, f32[8,32,256]{2,1,0:T(8,128)}, f32[8,32,256]{2,1,0:T(8,128)}, f32[8,32,256]{2,1,0:T(8,128)}, f32[8,32,256]{2,1,...) custom-call(s32[1]{0:T(128)} %bitcast.idx_ref, ...), custom_call_target="tpu_custom_call" | custom-call | flops 3200000000 | bytes 12000000 | tf_op jit(solution)/shard_map/y_inverse_0/pallas_call | solution.py:313
  193.7 3.1 collective-permute-start.1
  196.8 2.3 collective-permute-start.2
  199.2 3.6 %collective-permute-start.3 = (f32[8,32,256]{2,1,0:T(8,128)}, f32[8,32,256]{2,1,0:T(8,128)S(1)}, u32[]{:S(2)}, u32[]{:S(2)}) collective-permute-start(f32[8,32,256]{2,1,0:T(8,128)} %get-tuple-element.72), channel_id=1, source_target_pairs={{0,160},{32,192},{64,224},{96,0},{128,32},{160,64},{192,96},{224,1... | collective-permute-start | bytes 786440 | tf_op jit(solution)/shard_map/ppermute | solution.py:333
  202.8 0.6 collective-permute-start.4
  203.4 1.3 collective-permute-done.1.refs_0_
  204.6 13.5 %collective-permute-done.2.refs_0_ = f32[8,32,256]{2,1,0:T(8,128)S(1)} collective-permute-done((f32[8,32,256]{2,1,0:T(8,128)}, f32[8,32,256]{2,1,0:T(8,128)S(1)}, u32[]{:S(2)}, u32[]{:S(2)}) %collective-permute-start.2) | collective-permute-done | bytes 262176 | tf_op jit(solution)/shard_map/ppermute | solution.py:333
  218.2 5.7 %collective-permute-done.3.refs_0_ = f32[8,32,256]{2,1,0:T(8,128)S(1)} collective-permute-done((f32[8,32,256]{2,1,0:T(8,128)}, f32[8,32,256]{2,1,0:T(8,128)S(1)}, u32[]{:S(2)}, u32[]{:S(2)}) %collective-permute-start.3) | collective-permute-done | bytes 262176 | tf_op jit(solution)/shard_map/ppermute | solution.py:333
  223.9 4.8 %collective-permute-done.4.refs_0_ = f32[8,32,256]{2,1,0:T(8,128)S(1)} collective-permute-done((f32[8,32,256]{2,1,0:T(8,128)}, f32[8,32,256]{2,1,0:T(8,128)S(1)}, u32[]{:S(2)}, u32[]{:S(2)}) %collective-permute-start.4) | collective-permute-done | bytes 262176 | tf_op jit(solution)/shard_map/ppermute | solution.py:333
  228.7 7.3 %all-to-all-start.4 = ((f32[32,4,8,256]{3,2,1,0:T(8,128)}), f32[32,4,8,256]{3,2,1,0:T(8,128)}, u32[]{:S(2)}, u32[]{:S(2)}) async-start(f32[32,4,8,256]{3,2,1,0:T(8,128)} %bitcast.6), calls=%async_computation.4 | async-start | bytes 2097152 | tf_op jit(solution)/shard_map/all_to_all | solution.py:329
  236.0 0.1 collective-permute-start
  236.1 3.5 %collective-permute-start.5 = (f32[8,32,256]{2,1,0:T(8,128)S(1)}, f32[8,32,256]{2,1,0:T(8,128)S(1)}, u32[]{:S(2)}, u32[]{:S(2)}) collective-permute-start(f32[8,32,256]{2,1,0:T(8,128)S(1)} %copy-done.26), channel_id=1, source_target_pairs={{0,32},{32,64},{64,96},{96,128},{128,160},{160,192},{192,224},{224... | collective-permute-start | bytes 786440 | tf_op jit(solution)/shard_map/ppermute | solution.py:333
  239.7 2.0 collective-permute-start.6
  241.6 19.6 %collective-permute-done.refs_0_ = f32[8,32,256]{2,1,0:T(8,128)S(1)} collective-permute-done((f32[8,32,256]{2,1,0:T(8,128)S(1)}, f32[8,32,256]{2,1,0:T(8,128)S(1)}, u32[]{:S(2)}, u32[]{:S(2)}) %collective-permute-start) | collective-permute-done | bytes 262176 | tf_op jit(solution)/shard_map/ppermute | solution.py:333
  261.3 1.3 copy-done.12
  262.7 3.5 %y_inverse_1a.1 = (f32[4,32,256]{2,1,0:T(8,128)S(1)}, f32[4,32,256]{2,1,0:T(8,128)S(1)}, f32[4,32,256]{2,1,0:T(8,128)S(1)}, f32[4,32,256]{2,1,0:T(8,128)S(1)}, f...) custom-call(s32[1]{0:T(128)} %bitcast.idx_ref, ...), custom_call_target="tpu_custom_call" | custom-call | flops 1600000000 | bytes 6000000 | tf_op jit(solution)/shard_map/y_inverse_1a/pallas_call | solution.py:313
  266.2 1.3 collective-permute-start.13
  267.5 2.1 collective-permute-start.12
  269.6 3.8 %collective-permute-start.11 = (f32[4,32,256]{2,1,0:T(8,128)S(1)}, f32[4,32,256]{2,1,0:T(8,128)S(1)}, u32[]{:S(2)}, u32[]{:S(2)}) collective-permute-start(f32[4,32,256]{2,1,0:T(8,128)S(1)} %get-tuple-element.83), channel_id=1, source_target_pairs={{0,160},{32,192},{64,224},{96,0},{128,32},{160,64},{192,96},{224,1... | collective-permute-start | bytes 393224 | tf_op jit(solution)/shard_map/ppermute | solution.py:333
  273.4 3.2 collective-permute-start.9
  276.7 1.6 copy-done.3
  278.3 1.0 copy-done.7
  279.3 2.4 gradient_0_0.1
  281.8 1.5 collective-permute-start.8
  283.2 2.7 gradient_0_4.1
  285.9 4.2 %collective-permute-start.7 = (f32[4,32,256]{2,1,0:T(8,128)S(1)}, f32[4,32,256]{2,1,0:T(8,128)S(1)}, u32[]{:S(2)}, u32[]{:S(2)}) collective-permute-start(f32[4,32,256]{2,1,0:T(8,128)S(1)} %get-tuple-element.79), channel_id=1, source_target_pairs={{0,224},{32,0},{64,32},{96,64},{128,96},{160,128},{192,160},{224,1... | collective-permute-start | bytes 393224 | tf_op jit(solution)/shard_map/ppermute | solution.py:333
  290.1 2.7 gradient_0_3.1
  292.8 2.7 gradient_0_5.1
  295.5 2.7 gradient_0_2.1
  298.2 2.7 gradient_0_6.1
  300.9 2.7 gradient_0_1.1
  303.6 2.7 gradient_0_7.1
  306.3 1.1 copy-done.13
  307.4 3.5 %y_inverse_1b.1 = (f32[4,32,256]{2,1,0:T(8,128)S(1)}, f32[4,32,256]{2,1,0:T(8,128)S(1)}, f32[4,32,256]{2,1,0:T(8,128)S(1)}, f32[4,32,256]{2,1,0:T(8,128)S(1)}, f...) custom-call(s32[1]{0:T(128)} %bitcast.idx_ref, ...), custom_call_target="tpu_custom_call" | custom-call | flops 1600000000 | bytes 6000000 | tf_op jit(solution)/shard_map/y_inverse_1b/pallas_call | solution.py:313
  310.9 0.1 collective-permute-start.20
  311.0 0.9 collective-permute-start.19
  311.9 5.4 %collective-permute-start.18 = (f32[4,32,256]{2,1,0:T(8,128)S(1)}, f32[4,32,256]{2,1,0:T(8,128)S(1)}, u32[]{:S(2)}, u32[]{:S(2)}) collective-permute-start(f32[4,32,256]{2,1,0:T(8,128)S(1)} %get-tuple-element.108), channel_id=1, source_target_pairs={{0,160},{32,192},{64,224},{96,0},{128,32},{160,64},{192,96},{224,1... | collective-permute-start | bytes 393224 | tf_op jit(solution)/shard_map/ppermute | solution.py:333
  317.3 2.4 gradient_1_0.1
  319.7 3.2 collective-permute-start.16
  322.9 0.3 collective-permute-start.15
  323.2 2.7 gradient_1_4.1
  325.9 5.4 %collective-permute-start.14 = (f32[4,32,256]{2,1,0:T(8,128)S(1)}, f32[4,32,256]{2,1,0:T(8,128)S(1)}, u32[]{:S(2)}, u32[]{:S(2)}) collective-permute-start(f32[4,32,256]{2,1,0:T(8,128)S(1)} %get-tuple-element.104), channel_id=1, source_target_pairs={{0,224},{32,0},{64,32},{96,64},{128,96},{160,128},{192,160},{224,1... | collective-permute-start | bytes 393224 | tf_op jit(solution)/shard_map/ppermute | solution.py:333
  331.3 2.7 gradient_1_3.1
  334.0 2.7 gradient_1_5.1
  336.7 2.7 gradient_1_2.1
  339.4 2.7 gradient_1_6.1
  342.1 2.7 gradient_1_1.1
  344.8 2.7 gradient_1_7.1
  (67 shorter events, 0.1 us)
Async XLA Ops:
  11.7 60.4 %all-to-all-start = ((f32[32,8,8,256]{3,2,1,0:T(8,128)}), f32[32,8,8,256]{3,2,1,0:T(8,128)}, u32[]{:S(2)}, u32[]{:S(2)}) async-start(f32[32,8,8,256]{3,2,1,0:T(8,128)} %head_0.1), calls=%async_computation | async-start | bytes 4194304 | tf_op jit(solution)/shard_map/all_to_all | solution.py:329
  32.9 44.0 %copy-start.10 = (f32[1,256,8,256]{3,2,1,0:T(8,128)S(1)}, f32[1,256,8,256]{3,2,1,0:T(8,128)}, u32[]{:S(2)}) copy-start(f32[1,256,8,256]{3,2,1,0:T(8,128)} %param.18) | copy-start | bytes 6291460
  32.9 44.0 %copy-start.11 = (bf16[512,768]{1,0:T(8,128)(2,1)S(1)}, bf16[512,768]{1,0:T(8,128)(2,1)}, u32[]{:S(2)}) copy-start(bf16[512,768]{1,0:T(8,128)(2,1)} %constant.19.clone.inverse_ref.table_ref) | copy-start | bytes 2359300
  72.1 55.0 %all-to-all-start.1 = ((f32[32,8,8,256]{3,2,1,0:T(8,128)}), f32[32,8,8,256]{3,2,1,0:T(8,128)}, u32[]{:S(2)}, u32[]{:S(2)}) async-start(f32[32,8,8,256]{3,2,1,0:T(8,128)} %head_1.1), calls=%async_computation.1 | async-start | bytes 4194304 | tf_op jit(solution)/shard_map/all_to_all | solution.py:329
  76.9 1.1 copy-start.14
  127.1 55.0 %all-to-all-start.2 = ((f32[32,8,8,256]{3,2,1,0:T(8,128)}), f32[32,8,8,256]{3,2,1,0:T(8,128)}, u32[]{:S(2)}, u32[]{:S(2)}) async-start(f32[32,8,8,256]{3,2,1,0:T(8,128)} %bitcast.28), calls=%async_computation.2 | async-start | bytes 4194304 | tf_op jit(solution)/shard_map/all_to_all | solution.py:329
  131.9 1.1 copy-start.15
  133.0 1.1 copy-start.16
  182.2 46.5 %all-to-all-start.3 = ((f32[32,4,8,256]{3,2,1,0:T(8,128)}), f32[32,4,8,256]{3,2,1,0:T(8,128)S(1)}, u32[]{:S(2)}, u32[]{:S(2)}) async-start(f32[32,4,8,256]{3,2,1,0:T(8,128)} %bitcast.29), calls=%async_computation.3 | async-start | bytes 2097152 | tf_op jit(solution)/shard_map/all_to_all | solution.py:329
  193.7 42.4 %copy-start.27 = (f32[8,32,256]{2,1,0:T(8,128)S(1)}, f32[8,32,256]{2,1,0:T(8,128)}, u32[]{:S(2)}) copy-start(f32[8,32,256]{2,1,0:T(8,128)} %get-tuple-element.66) | copy-start | bytes 786436
  193.7 42.5 %copy-start.26 = (f32[8,32,256]{2,1,0:T(8,128)S(1)}, f32[8,32,256]{2,1,0:T(8,128)}, u32[]{:S(2)}) copy-start(f32[8,32,256]{2,1,0:T(8,128)} %get-tuple-element.76) | copy-start | bytes 786436
  193.7 46.0 %copy-start.25 = (f32[8,32,256]{2,1,0:T(8,128)S(1)}, f32[8,32,256]{2,1,0:T(8,128)}, u32[]{:S(2)}) copy-start(f32[8,32,256]{2,1,0:T(8,128)} %get-tuple-element.77) | copy-start | bytes 786436
  193.7 11.0 %collective-permute-start.1 = (f32[8,32,256]{2,1,0:T(8,128)}, f32[8,32,256]{2,1,0:T(8,128)S(1)}, u32[]{:S(2)}, u32[]{:S(2)}) collective-permute-start(f32[8,32,256]{2,1,0:T(8,128)} %get-tuple-element.70), channel_id=1, source_target_pairs={{0,128},{32,160},{64,192},{96,224},{128,0},{160,32},{192,64},{224,... | collective-permute-start | bytes 786440 | tf_op jit(solution)/shard_map/ppermute | solution.py:333
  196.8 21.4 %collective-permute-start.2 = (f32[8,32,256]{2,1,0:T(8,128)}, f32[8,32,256]{2,1,0:T(8,128)S(1)}, u32[]{:S(2)}, u32[]{:S(2)}) collective-permute-start(f32[8,32,256]{2,1,0:T(8,128)} %get-tuple-element.71), channel_id=1, source_target_pairs={{0,96},{32,128},{64,160},{96,192},{128,224},{160,0},{192,32},{224,... | collective-permute-start | bytes 786440 | tf_op jit(solution)/shard_map/ppermute | solution.py:333
  199.2 24.7 %collective-permute-start.3 = (f32[8,32,256]{2,1,0:T(8,128)}, f32[8,32,256]{2,1,0:T(8,128)S(1)}, u32[]{:S(2)}, u32[]{:S(2)}) collective-permute-start(f32[8,32,256]{2,1,0:T(8,128)} %get-tuple-element.72), channel_id=1, source_target_pairs={{0,160},{32,192},{64,224},{96,0},{128,32},{160,64},{192,96},{224,1... | collective-permute-start | bytes 786440 | tf_op jit(solution)/shard_map/ppermute | solution.py:333
  202.8 25.9 %collective-permute-start.4 = (f32[8,32,256]{2,1,0:T(8,128)}, f32[8,32,256]{2,1,0:T(8,128)S(1)}, u32[]{:S(2)}, u32[]{:S(2)}) collective-permute-start(f32[8,32,256]{2,1,0:T(8,128)} %get-tuple-element.73), channel_id=1, source_target_pairs={{0,64},{32,96},{64,128},{96,160},{128,192},{160,224},{192,0},{224,... | collective-permute-start | bytes 786440 | tf_op jit(solution)/shard_map/ppermute | solution.py:333
  204.6 56.6 %copy-start.23 = (f32[8,32,256]{2,1,0:T(8,128)}, f32[8,32,256]{2,1,0:T(8,128)S(1)}, u32[]{:S(2)}) copy-start(f32[8,32,256]{2,1,0:T(8,128)S(1)} %collective-permute-done.1.refs_0_) | copy-start | bytes 786436
  218.2 43.1 %copy-start.21 = (f32[8,32,256]{2,1,0:T(8,128)}, f32[8,32,256]{2,1,0:T(8,128)S(1)}, u32[]{:S(2)}) copy-start(f32[8,32,256]{2,1,0:T(8,128)S(1)} %collective-permute-done.2.refs_0_) | copy-start | bytes 786436
  223.9 37.4 %copy-start.19 = (f32[8,32,256]{2,1,0:T(8,128)}, f32[8,32,256]{2,1,0:T(8,128)S(1)}, u32[]{:S(2)}) copy-start(f32[8,32,256]{2,1,0:T(8,128)S(1)} %collective-permute-done.3.refs_0_) | copy-start | bytes 786436
  228.7 32.6 %copy-start.18 = (f32[8,32,256]{2,1,0:T(8,128)}, f32[8,32,256]{2,1,0:T(8,128)S(1)}, u32[]{:S(2)}) copy-start(f32[8,32,256]{2,1,0:T(8,128)S(1)} %collective-permute-done.4.refs_0_) | copy-start | bytes 786436
  228.7 32.6 %copy-start.24 = (f32[32,4,8,256]{3,2,1,0:T(8,128)}, f32[32,4,8,256]{3,2,1,0:T(8,128)S(1)}, u32[]{:S(2)}) copy-start(f32[32,4,8,256]{3,2,1,0:T(8,128)S(1)} %all-to-all-done.3.in_ref) | copy-start | bytes 3145732
  228.7 77.6 %all-to-all-start.4 = ((f32[32,4,8,256]{3,2,1,0:T(8,128)}), f32[32,4,8,256]{3,2,1,0:T(8,128)}, u32[]{:S(2)}, u32[]{:S(2)}) async-start(f32[32,4,8,256]{3,2,1,0:T(8,128)} %bitcast.6), calls=%async_computation.4 | async-start | bytes 2097152 | tf_op jit(solution)/shard_map/all_to_all | solution.py:329
  236.0 25.2 %collective-permute-start = (f32[8,32,256]{2,1,0:T(8,128)S(1)}, f32[8,32,256]{2,1,0:T(8,128)S(1)}, u32[]{:S(2)}, u32[]{:S(2)}) collective-permute-start(f32[8,32,256]{2,1,0:T(8,128)S(1)} %copy-done.27), channel_id=1, source_target_pairs={{0,224},{32,0},{64,32},{96,64},{128,96},{160,128},{192,160},{224,1... | collective-permute-start | bytes 786440 | tf_op jit(solution)/shard_map/ppermute | solution.py:333
  236.1 25.1 %collective-permute-start.5 = (f32[8,32,256]{2,1,0:T(8,128)S(1)}, f32[8,32,256]{2,1,0:T(8,128)S(1)}, u32[]{:S(2)}, u32[]{:S(2)}) collective-permute-start(f32[8,32,256]{2,1,0:T(8,128)S(1)} %copy-done.26), channel_id=1, source_target_pairs={{0,32},{32,64},{64,96},{96,128},{128,160},{160,192},{192,224},{224... | collective-permute-start | bytes 786440 | tf_op jit(solution)/shard_map/ppermute | solution.py:333
  239.7 21.6 %collective-permute-start.6 = (f32[8,32,256]{2,1,0:T(8,128)S(1)}, f32[8,32,256]{2,1,0:T(8,128)S(1)}, u32[]{:S(2)}, u32[]{:S(2)}) collective-permute-start(f32[8,32,256]{2,1,0:T(8,128)S(1)} %copy-done.25), channel_id=1, source_target_pairs={{0,192},{32,224},{64,0},{96,32},{128,64},{160,96},{192,128},{224,1... | collective-permute-start | bytes 786440 | tf_op jit(solution)/shard_map/ppermute | solution.py:333
  261.2 4.9 %copy-start.17 = (f32[8,32,256]{2,1,0:T(8,128)}, f32[8,32,256]{2,1,0:T(8,128)S(1)}, u32[]{:S(2)}) copy-start(f32[8,32,256]{2,1,0:T(8,128)S(1)} %collective-permute-done.refs_0_) | copy-start | bytes 786436
  261.2 4.9 %copy-start.20 = (f32[8,32,256]{2,1,0:T(8,128)}, f32[8,32,256]{2,1,0:T(8,128)S(1)}, u32[]{:S(2)}) copy-start(f32[8,32,256]{2,1,0:T(8,128)S(1)} %collective-permute-done.5.refs_0_) | copy-start | bytes 786436
  261.3 4.9 %copy-start.22 = (f32[8,32,256]{2,1,0:T(8,128)}, f32[8,32,256]{2,1,0:T(8,128)S(1)}, u32[]{:S(2)}) copy-start(f32[8,32,256]{2,1,0:T(8,128)S(1)} %collective-permute-done.6.refs_0_) | copy-start | bytes 786436
  261.3 1.4 copy-start.12
  262.7 14.0 %copy-start = (bf16[3,8,256,256]{3,2,1,0:T(8,128)(2,1)S(1)}, bf16[3,8,256,256]{3,2,1,0:T(8,128)(2,1)}, u32[]{:S(2)}) copy-start(bf16[3,8,256,256]{3,2,1,0:T(8,128)(2,1)} %shift_ref.35) | copy-start | bytes 9437188
  262.7 14.0 %copy-start.1 = (bf16[2,8,256,256]{3,2,1,0:T(8,128)(2,1)S(1)}, bf16[2,8,256,256]{3,2,1,0:T(8,128)(2,1)}, u32[]{:S(2)}) copy-start(bf16[2,8,256,256]{3,2,1,0:T(8,128)(2,1)} %rho_ref.35) | copy-start | bytes 6291460
  262.7 14.0 %copy-start.5 = (bf16[512,512]{1,0:T(8,128)(2,1)S(1)}, bf16[512,512]{1,0:T(8,128)(2,1)}, u32[]{:S(2)}) copy-start(bf16[512,512]{1,0:T(8,128)(2,1)} %constant.20.clone.refs_2_) | copy-start | bytes 1572868
  262.7 14.0 %copy-start.9 = (s32[8,3]{0,1:T(4,128)S(1)}, s32[8,3]{0,1:T(4,128)}, u32[]{:S(2)}) copy-start(s32[8,3]{0,1:T(4,128)} %param.17) | copy-start | bytes 292
  266.2 15.6 %collective-permute-start.13 = (f32[4,32,256]{2,1,0:T(8,128)S(1)}, f32[4,32,256]{2,1,0:T(8,128)S(1)}, u32[]{:S(2)}, u32[]{:S(2)}) collective-permute-start(f32[4,32,256]{2,1,0:T(8,128)S(1)} %get-tuple-element.85), channel_id=1, source_target_pairs={{0,128},{32,160},{64,192},{96,224},{128,0},{160,32},{192,64},{224,... | collective-permute-start | bytes 393224 | tf_op jit(solution)/shard_map/ppermute | solution.py:333
  267.5 18.4 %collective-permute-start.12 = (f32[4,32,256]{2,1,0:T(8,128)S(1)}, f32[4,32,256]{2,1,0:T(8,128)S(1)}, u32[]{:S(2)}, u32[]{:S(2)}) collective-permute-start(f32[4,32,256]{2,1,0:T(8,128)S(1)} %get-tuple-element.84), channel_id=1, source_target_pairs={{0,96},{32,128},{64,160},{96,192},{128,224},{160,0},{192,32},{224,... | collective-permute-start | bytes 393224 | tf_op jit(solution)/shard_map/ppermute | solution.py:333
  269.6 23.2 %collective-permute-start.11 = (f32[4,32,256]{2,1,0:T(8,128)S(1)}, f32[4,32,256]{2,1,0:T(8,128)S(1)}, u32[]{:S(2)}, u32[]{:S(2)}) collective-permute-start(f32[4,32,256]{2,1,0:T(8,128)S(1)} %get-tuple-element.83), channel_id=1, source_target_pairs={{0,160},{32,192},{64,224},{96,0},{128,32},{160,64},{192,96},{224,1... | collective-permute-start | bytes 393224 | tf_op jit(solution)/shard_map/ppermute | solution.py:333
  273.4 22.1 %collective-permute-start.10 = (f32[4,32,256]{2,1,0:T(8,128)S(1)}, f32[4,32,256]{2,1,0:T(8,128)S(1)}, u32[]{:S(2)}, u32[]{:S(2)}) collective-permute-start(f32[4,32,256]{2,1,0:T(8,128)S(1)} %get-tuple-element.82), channel_id=1, source_target_pairs={{0,64},{32,96},{64,128},{96,160},{128,192},{160,224},{192,0},{224,... | collective-permute-start | bytes 393224 | tf_op jit(solution)/shard_map/ppermute | solution.py:333
  273.4 24.8 %collective-permute-start.9 = (f32[4,32,256]{2,1,0:T(8,128)S(1)}, f32[4,32,256]{2,1,0:T(8,128)S(1)}, u32[]{:S(2)}, u32[]{:S(2)}) collective-permute-start(f32[4,32,256]{2,1,0:T(8,128)S(1)} %get-tuple-element.81), channel_id=1, source_target_pairs={{0,192},{32,224},{64,0},{96,32},{128,64},{160,96},{192,128},{224,1... | collective-permute-start | bytes 393224 | tf_op jit(solution)/shard_map/ppermute | solution.py:333
  276.7 1.6 copy-start.3
  278.3 1.0 copy-start.7
  281.8 19.1 %collective-permute-start.8 = (f32[4,32,256]{2,1,0:T(8,128)S(1)}, f32[4,32,256]{2,1,0:T(8,128)S(1)}, u32[]{:S(2)}, u32[]{:S(2)}) collective-permute-start(f32[4,32,256]{2,1,0:T(8,128)S(1)} %get-tuple-element.80), channel_id=1, source_target_pairs={{0,32},{32,64},{64,96},{96,128},{128,160},{160,192},{192,224},{224... | collective-permute-start | bytes 393224 | tf_op jit(solution)/shard_map/ppermute | solution.py:333
  285.9 17.7 %collective-permute-start.7 = (f32[4,32,256]{2,1,0:T(8,128)S(1)}, f32[4,32,256]{2,1,0:T(8,128)S(1)}, u32[]{:S(2)}, u32[]{:S(2)}) collective-permute-start(f32[4,32,256]{2,1,0:T(8,128)S(1)} %get-tuple-element.79), channel_id=1, source_target_pairs={{0,224},{32,0},{64,32},{96,64},{128,96},{160,128},{192,160},{224,1... | collective-permute-start | bytes 393224 | tf_op jit(solution)/shard_map/ppermute | solution.py:333
  306.3 1.1 copy-start.13
  307.4 9.8 %copy-start.2 = (bf16[2,8,256,256]{3,2,1,0:T(8,128)(2,1)S(1)}, bf16[2,8,256,256]{3,2,1,0:T(8,128)(2,1)}, u32[]{:S(2)}) copy-start(bf16[2,8,256,256]{3,2,1,0:T(8,128)(2,1)} %rho_ref.35) | copy-start | bytes 6291460
  307.4 9.8 %copy-start.4 = (s32[8,256,256]{2,1,0:T(8,128)S(1)}, s32[8,256,256]{2,1,0:T(8,128)}, u32[]{:S(2)}) copy-start(s32[8,256,256]{2,1,0:T(8,128)} %support_ref.35) | copy-start | bytes 6291460
  307.4 9.8 %copy-start.6 = (bf16[512,512]{1,0:T(8,128)(2,1)S(1)}, bf16[512,512]{1,0:T(8,128)(2,1)}, u32[]{:S(2)}) copy-start(bf16[512,512]{1,0:T(8,128)(2,1)} %constant.20.clone.refs_2_) | copy-start | bytes 1572868
  307.4 9.8 %copy-start.8 = (bf16[512,512]{1,0:T(8,128)(2,1)S(1)}, bf16[512,512]{1,0:T(8,128)(2,1)}, u32[]{:S(2)}) copy-start(bf16[512,512]{1,0:T(8,128)(2,1)} %constant.21.clone.refs_3_) | copy-start | bytes 1572868
  310.9 12.0 %collective-permute-start.20 = (f32[4,32,256]{2,1,0:T(8,128)S(1)}, f32[4,32,256]{2,1,0:T(8,128)S(1)}, u32[]{:S(2)}, u32[]{:S(2)}) collective-permute-start(f32[4,32,256]{2,1,0:T(8,128)S(1)} %get-tuple-element.110), channel_id=1, source_target_pairs={{0,128},{32,160},{64,192},{96,224},{128,0},{160,32},{192,64},{224,... | collective-permute-start | bytes 393224 | tf_op jit(solution)/shard_map/ppermute | solution.py:333
  311.0 14.9 %collective-permute-start.19 = (f32[4,32,256]{2,1,0:T(8,128)S(1)}, f32[4,32,256]{2,1,0:T(8,128)S(1)}, u32[]{:S(2)}, u32[]{:S(2)}) collective-permute-start(f32[4,32,256]{2,1,0:T(8,128)S(1)} %get-tuple-element.109), channel_id=1, source_target_pairs={{0,96},{32,128},{64,160},{96,192},{128,224},{160,0},{192,32},{224,... | collective-permute-start | bytes 393224 | tf_op jit(solution)/shard_map/ppermute | solution.py:333
  311.9 22.1 %collective-permute-start.18 = (f32[4,32,256]{2,1,0:T(8,128)S(1)}, f32[4,32,256]{2,1,0:T(8,128)S(1)}, u32[]{:S(2)}, u32[]{:S(2)}) collective-permute-start(f32[4,32,256]{2,1,0:T(8,128)S(1)} %get-tuple-element.108), channel_id=1, source_target_pairs={{0,160},{32,192},{64,224},{96,0},{128,32},{160,64},{192,96},{224,1... | collective-permute-start | bytes 393224 | tf_op jit(solution)/shard_map/ppermute | solution.py:333
  317.3 19.4 %collective-permute-start.17 = (f32[4,32,256]{2,1,0:T(8,128)S(1)}, f32[4,32,256]{2,1,0:T(8,128)S(1)}, u32[]{:S(2)}, u32[]{:S(2)}) collective-permute-start(f32[4,32,256]{2,1,0:T(8,128)S(1)} %get-tuple-element.107), channel_id=1, source_target_pairs={{0,64},{32,96},{64,128},{96,160},{128,192},{160,224},{192,0},{224,... | collective-permute-start | bytes 393224 | tf_op jit(solution)/shard_map/ppermute | solution.py:333
  319.7 19.7 %collective-permute-start.16 = (f32[4,32,256]{2,1,0:T(8,128)S(1)}, f32[4,32,256]{2,1,0:T(8,128)S(1)}, u32[]{:S(2)}, u32[]{:S(2)}) collective-permute-start(f32[4,32,256]{2,1,0:T(8,128)S(1)} %get-tuple-element.106), channel_id=1, source_target_pairs={{0,192},{32,224},{64,0},{96,32},{128,64},{160,96},{192,128},{224,1... | collective-permute-start | bytes 393224 | tf_op jit(solution)/shard_map/ppermute | solution.py:333
  322.9 19.1 %collective-permute-start.15 = (f32[4,32,256]{2,1,0:T(8,128)S(1)}, f32[4,32,256]{2,1,0:T(8,128)S(1)}, u32[]{:S(2)}, u32[]{:S(2)}) collective-permute-start(f32[4,32,256]{2,1,0:T(8,128)S(1)} %get-tuple-element.105), channel_id=1, source_target_pairs={{0,32},{32,64},{64,96},{96,128},{128,160},{160,192},{192,224},{224... | collective-permute-start | bytes 393224 | tf_op jit(solution)/shard_map/ppermute | solution.py:333
  325.9 18.9 %collective-permute-start.14 = (f32[4,32,256]{2,1,0:T(8,128)S(1)}, f32[4,32,256]{2,1,0:T(8,128)S(1)}, u32[]{:S(2)}, u32[]{:S(2)}) collective-permute-start(f32[4,32,256]{2,1,0:T(8,128)S(1)} %get-tuple-element.104), channel_id=1, source_target_pairs={{0,224},{32,0},{64,32},{96,64},{128,96},{160,128},{192,160},{224,1... | collective-permute-start | bytes 393224 | tf_op jit(solution)/shard_map/ppermute | solution.py:333

commit v3 on v2

--- a/solution.py
+++ b/solution.py
@@ -17,7 +17,6 @@
 XL = 8
 NREF = 8
 HEAD_ROWS = 32
-HALF = XL // 2
 R_ORDER = (4, 3, 5, 2, 6, 1, 7)
 BF = jnp.bfloat16
 F32 = jnp.float32
@@ -39,11 +38,6 @@
     re, im = dft_np()
     high, low = split_np(np.concatenate([re, -im if inverse else im], 0))
     return np.concatenate([high, high, low], 1)
-
-
-def halves_of_slabs(table):
-    rows = np.arange(N).reshape(SLABS, 2, XL // 2).transpose(1, 0, 2).reshape(-1)
-    return table[np.concatenate([rows, rows + N])]
 
 
 def packed_columns():
@@ -144,7 +138,7 @@
 
 
 def x_kernel(in_ref, amp_ref, forward_ref, inverse_ref, *refs):
-    outs, (real_ref, imag_ref, sems) = refs[:-3], refs[-3:]
+    out_ref, real_ref, imag_ref, sems = refs
     parts = ((real_ref, pl.ds(0, KC)), (imag_ref, pl.ds(KC, KC)))
     copies = [
         pltpu.make_async_copy(in_ref.at[:, lanes], part, sems.at[i]) for i, (part, lanes) in enumerate(parts)
@@ -166,11 +160,8 @@
         return carry
 
     lax.fori_loop(0, XL, step, 0)
-    rows = N * XL // len(outs)
     copies = [
-        pltpu.make_async_copy(part.at[pl.ds(n * rows, rows), :], out.at[:, lanes], sems.at[2 * n + i])
-        for n, out in enumerate(outs)
-        for i, (part, lanes) in enumerate(parts)
+        pltpu.make_async_copy(part, out_ref.at[:, lanes], sems.at[i]) for i, (part, lanes) in enumerate(parts)
     ]
     for copy in copies:
         copy.start()
@@ -181,32 +172,24 @@
 def y_inverse_kernel(idx_ref, in_ref, table_ref, *refs):
     outs, (u_ref, t_ref, sems) = refs[:NREF], refs[NREF:]
     r = idx_ref[0]
-    planes = u_ref.shape[0]
-    copies = [pltpu.make_async_copy(in_ref.at[:, x], u_ref.at[x], sems.at[x]) for x in range(planes)]
+    copies = [pltpu.make_async_copy(in_ref.at[:, x], u_ref.at[x], sems.at[x]) for x in range(XL)]
     for copy in copies:
         copy.start()
-    for x in range(planes):
+    for x in range(XL):
         copies[x].wait()
-        t_ref[x] = left_multiply(table_ref[...], u_ref[x].reshape(N, 2 * KC))
-    copies = []
-    for s in range(NREF):
-        start = pl.multiple_of(lax.rem(r + s, NREF) * 32, 32)
-        if planes < XL:
-            outs[s][...] = t_ref[:, pl.ds(start, 32), :]
-        else:
-            copies.append(pltpu.make_async_copy(t_ref.at[:, pl.ds(start, 32), :], outs[s], sems.at[s]))
-            copies[-1].start()
-    for copy in copies:
-        copy.wait()
-
-
-def gradient_kernel(shift_by, adds, idx_ref, miller_ref, rho_ref, shift_ref, support_ref, *refs):
+        t_ref[...] = left_multiply(table_ref[...], u_ref[x].reshape(N, 2 * KC))
+        for s in range(NREF):
+            start = pl.multiple_of(lax.rem(r + s, NREF) * 32, 32)
+            outs[s][x] = t_ref[pl.ds(start, 32), :]
+
+
+def gradient_kernel(shift_by, idx_ref, miller_ref, rho_ref, shift_ref, support_ref, *refs):
     ins, high_ref, low_ref = refs[:CH], refs[CH], refs[CH + 1]
     sums = refs[CH + 2 : -3]
     rho_out, shift_out, back_ref = refs[-3:]
     g = lax.rem(idx_ref[0] + NREF - shift_by, NREF)
     h, k, l = (miller_ref[c, g].astype(F32) for c in range(3))
-    high, low = split(jnp.concatenate([ref[...].reshape(HALF * 32, 2 * KC) for ref in ins], 1))
+    high, low = split(jnp.concatenate([ref[...].reshape(N, 2 * KC) for ref in ins], 1))
     dot = functools.partial(jnp.dot, preferred_element_type=F32)
     back_ref[...] = dot(high, high_ref[...]) + dot(low, high_ref[...]) + dot(high, low_ref[...])
 
@@ -226,10 +209,10 @@
             (shift_out, 1, 1, k * twist),
             (shift_out, 1, 2, l * twist),
         ):
-            out[n, x] = sums[old][n, x] + value if adds else value
+            out[n, x] = sums[old][n, x] + value if sums else value
         return carry
 
-    lax.fori_loop(0, HALF, step, 0)
+    lax.fori_loop(0, XL, step, 0)
 
 
 SMEM = pl.BlockSpec(memory_space=pltpu.SMEM)
@@ -293,36 +276,32 @@
     millers = millers.T
 
     def x_both(c, part):
-        pieces = c + 1
-        table = inverse if c == 0 else jnp.asarray(halves_of_slabs(left_table(True)))
-        parts = pl.pallas_call(
+        return pl.pallas_call(
             x_kernel,
             grid=(1,),
             in_specs=[HBM, pl.BlockSpec((N * XL, KC), lambda i: (0, c)), VMEM, VMEM],
-            out_specs=[HBM] * pieces,
-            out_shape=[hbm(N * XL // pieces, 2 * KC)] * pieces,
-            scratch_shapes=[pltpu.VMEM((N * XL, KC), F32)] * 2 + [pltpu.SemaphoreType.DMA((4,))],
+            out_specs=HBM,
+            out_shape=hbm(N * XL, 2 * KC),
+            scratch_shapes=[pltpu.VMEM((N * XL, KC), F32)] * 2 + [pltpu.SemaphoreType.DMA((2,))],
             compiler_params=params(24),
             cost_estimate=cost(6.4e9, 24e6),
             name=f"x_{c}",
-        )(in_hbm(part.reshape(N * XL, 2 * KC)), amp, forward, table)
-        return [p.reshape(SLABS, XL // pieces, XL, 2 * KC) for p in parts]
-
-    def y_inverse(name, part):
-        planes = part.shape[1]
+        )(in_hbm(part.reshape(N * XL, 2 * KC)), amp, forward, inverse).reshape(SLABS, XL, XL, 2 * KC)
+
+    def y_inverse(c, part):
         return pl.pallas_call(
             y_inverse_kernel,
             in_specs=[SMEM, HBM, VMEM],
-            out_specs=[VMEM if planes < XL else HBM] * NREF,
-            out_shape=[(f32 if planes < XL else hbm)(planes, 32, 2 * KC)] * NREF,
+            out_specs=[VMEM] * NREF,
+            out_shape=[f32(XL, 32, 2 * KC)] * NREF,
             scratch_shapes=[
-                pltpu.VMEM((planes, SLABS, XL, 2 * KC), F32),
-                pltpu.VMEM((planes, N, 2 * KC), F32),
+                pltpu.VMEM((XL, SLABS, XL, 2 * KC), F32),
+                pltpu.VMEM((N, 2 * KC), F32),
                 pltpu.SemaphoreType.DMA((XL,)),
             ],
             compiler_params=params(24),
-            cost_estimate=cost(0.4e9 * planes, 1.5e6 * planes),
-            name=f"y_inverse_{name}",
+            cost_estimate=cost(3.2e9, 12e6),
+            name=f"y_inverse_{c}",
         )(idx, in_hbm(part), inverse)
 
     def over_grid(part):
@@ -333,51 +312,43 @@
         moved = {s: lax.ppermute(parts[s], "refl", ring(s)) for s in R_ORDER}
         return [parts[0]] + [moved[s] for s in range(1, NREF)]
 
-    def gradient(s, half, parts, sums):
-        adds = s > 0
-        out_block = lambda n: pl.BlockSpec((n, HALF, 32, N), lambda i, idx: (0, half, 0, 0))
+    def gradient(s, parts, sums):
+        out_block = lambda n: pl.BlockSpec((n, XL, 32, N), lambda i, idx: (0, 0, 0, 0))
         whole = lambda i, idx: (0, 0)
         return tuple(
             pl.pallas_call(
-                functools.partial(gradient_kernel, s, adds),
+                functools.partial(gradient_kernel, s),
                 grid_spec=pltpu.PrefetchScalarGridSpec(
                     num_scalar_prefetch=1,
                     grid=(1,),
                     in_specs=[
                         SMEM,
-                        pl.BlockSpec((2, HALF, 32, N), lambda i, idx: (0, half, idx[0], 0)),
-                        pl.BlockSpec((3, HALF, 32, N), lambda i, idx: (0, half, idx[0], 0)),
-                        pl.BlockSpec((HALF, 32, N), lambda i, idx: (half, idx[0], 0)),
-                        pl.BlockSpec((HALF, 32, 2 * KC), lambda i, idx: (half, 0, 0)),
-                        pl.BlockSpec((HALF, 32, 2 * KC), lambda i, idx: (0, 0, 0)),
+                        pl.BlockSpec((2, XL, 32, N), lambda i, idx: (0, 0, idx[0], 0)),
+                        pl.BlockSpec((3, XL, 32, N), lambda i, idx: (0, 0, idx[0], 0)),
+                        pl.BlockSpec((XL, 32, N), lambda i, idx: (0, idx[0], 0)),
                     ]
+                    + [pl.BlockSpec((XL, 32, 2 * KC), lambda i, idx: (0, 0, 0))] * CH
                     + [pl.BlockSpec((2 * N, 2 * N), whole)] * 2
-                    + [out_block(2 + n) if adds else pl.BlockSpec(memory_space=pl.ANY) for n, _ in enumerate(sums)],
+                    + ([out_block(2), out_block(3)] if sums else []),
                     out_specs=[out_block(2), out_block(3)],
-                    scratch_shapes=[pltpu.VMEM((HALF * 32, 2 * N), F32)],
+                    scratch_shapes=[pltpu.VMEM((N, 2 * N), F32)],
                 ),
                 out_shape=[f32(2, XL, 32, N), f32(3, XL, 32, N)],
-                input_output_aliases={9 + n: n for n, _ in enumerate(sums)},
                 compiler_params=params(24),
-                cost_estimate=cost(0.4e9, 3e6),
-                name=f"gradient_{half}_{s}",
+                cost_estimate=cost(0.8e9, 5e6),
+                name=f"gradient_{s}",
             )(idx, millers, density, displacement, support, *parts, high, low, *sums)
         )
 
     f0 = over_grid(head(0, millers, density, displacement, support))
     f1 = over_grid(after(head(1, millers, density, displacement, support), f0))
-    b0 = over_grid(after(x_both(0, f0)[0], f1))
-    halves = x_both(1, f1)
-    b1 = [over_grid(after(halves[0], b0))]
-    r0 = over_refl(y_inverse("0", b0))
-    b1.append(over_grid(after(halves[1], b1[0], *(r0[s] for s in R_ORDER[:4]))))
-    r1 = over_refl(y_inverse("1a", after(b1[0], *r0)))
+    b0 = over_grid(after(x_both(0, f0), f1))
+    b1 = over_grid(after(x_both(1, f1), b0))
+    r0 = over_refl(y_inverse(0, b0))
+    r1 = over_refl(y_inverse(1, after(b1, *r0)))
     sums = ()
     for s in (0,) + R_ORDER:
-        sums = gradient(s, 0, (in_hbm(r0[s]), r1[s]), sums)
-    r1 = over_refl(y_inverse("1b", after(b1[1], *sums)))
-    for s in (0,) + R_ORDER:
-        sums = gradient(s, 1, (in_hbm(r0[s]), r1[s]), sums)
+        sums = gradient(s, (r0[s], r1[s]), sums)
     return sums
 
 

time: 349 us -> 289 us (0.83)
  Pallas kernels: 103 us -> 72.5 us
  waiting for transfers between devices: 157 us -> 135 us
  local copies, waits for them, and re-layouts: 8.58 us -> 2.3 us
  starting transfers between devices: 78.1 us -> 74.1 us
    pallas_call x16 -> x8, Pallas kernels: 42.6 us -> 14.9 us  [gradient(): pl.pallas_call(functools.partial(gradient_kernel, s), grid_spec=pltpu.Pre...]
    ppermute x21 -> x14, waiting for transfers between devices: 44.9 us -> 21.9 us  [over_refl(): moved = {s: lax.ppermute(parts[s], 'refl', ring(s)) for s in R_ORDER}]
    all_to_all x5 -> x4, starting transfers between devices: 31.6 us -> 24.3 us  [over_grid(): return lax.all_to_all(part, 'grid', 0, 0, tiled=True)]
    unnamed x56 -> x20, local copies, waits for them, and re-layouts: 8.58 us -> 2.3 us
    ppermute x21 -> x14, starting transfers between devices: 46.6 us -> 49.8 us  [over_refl(): moved = {s: lax.ppermute(parts[s], 'refl', ring(s)) for s in R_ORDER}]
    pallas_call x3 -> x2, Pallas kernels: 13.7 us -> 11.4 us  [y_inverse(): pl.pallas_call(y_inverse_kernel, in_specs=[SMEM, HBM, VMEM], out_specs=[V...]
    all_to_all x5 -> x4, waiting for transfers between devices: 112 us -> 113 us  [over_grid(): return lax.all_to_all(part, 'grid', 0, 0, tiled=True)]
  transfers between devices with their start and end apart: 26 -> 18, of which waited for: 8 -> 7; matrix products, arithmetic and copies ran while one was open for 0% -> 0% of each run, Pallas kernels for 25% -> 19%
where the time goes in v3:
time: 289 us; the launch traced here: 285 us
  waiting for transfers between devices  135 us (47%)
  starting transfers between devices  74.1 us (26%)
  Pallas kernels  72.5 us (25%)
    all_to_all x4, waiting for transfers between devices, over_grid(): return lax.all_to_all(part, 'grid', 0, 0, tiled=True)  113 us
    ppermute x14, starting transfers between devices, over_refl(): moved = {s: lax.ppermute(parts[s], 'refl', ring(s)) for s in R_ORDER}  49.8 us
    all_to_all x4, starting transfers between devices, over_grid(): return lax.all_to_all(part, 'grid', 0, 0, tiled=True)  24.3 us
    pallas_call x2, Pallas kernels, x_both(): pl.pallas_call(x_kernel, grid=(1,), in_specs=[HBM, pl.BlockSpec((N * XL,...  24.3 us
    ppermute x14, waiting for transfers between devices, over_refl(): moved = {s: lax.ppermute(parts[s], 'refl', ring(s)) for s in R_ORDER}  21.9 us
    pallas_call x2, Pallas kernels, head(): pl.pallas_call(head_kernel, grid=(XL + 2,), in_specs=[SMEM, pl.BlockSpec(...  21.9 us
    pallas_call x8, Pallas kernels, gradient(): pl.pallas_call(functools.partial(gradient_kernel, s), grid_spec=pltpu.Pre...  14.9 us
    pallas_call x2, Pallas kernels, y_inverse(): pl.pallas_call(y_inverse_kernel, in_specs=[SMEM, HBM, VMEM], out_specs=[V...  11.4 us
  transfers between devices with their start and end apart: 18, of which 7 were waited for; matrix products, arithmetic and copies ran while one was open for 0% of the time, Pallas kernels for 19%

profile of v3, /device:TPU:8, one launch (start us, length us, event | category | flops | bytes accessed | tf_op | source)
XLA Modules:
  0.0 285.1 jit_solution(15617988361362831879)
XLA Ops:
  0.6 10.9 %head_0.1 = f32[32,8,8,256]{3,2,1,0:T(8,128)} custom-call(s32[3,8]{1,0:T(4,128)} %bitcast.7, bf16[2,8,256,256]{3,2,1,0:T(8,128)(2,1)} %rho_ref.19, bf16[3,8,256,256]{3,2,1,0:T(8,128)(2,1)} %shift_ref.19, s32[8,256,256]{2,1,0:T(8,128)} %support_ref.19, bf16[1536,512]{1,0:T(8,128)(2,1)} %constant.20.clone.table_ref, ...), custom_call_target="tpu_custom_call" | custom-call | flops 6400000000 | bytes 16000000 | tf_op jit(solution)/shard_map/head_0/pallas_call | solution.py:250
  11.5 10.1 %all-to-all-start = ((f32[32,8,8,256]{3,2,1,0:T(8,128)}), f32[32,8,8,256]{3,2,1,0:T(8,128)}, u32[]{:S(2)}, u32[]{:S(2)}) async-start(f32[32,8,8,256]{3,2,1,0:T(8,128)} %head_0.1), calls=%async_computation | async-start | bytes 4194304 | tf_op jit(solution)/shard_map/all_to_all | solution.py:308
  21.7 11.0 %head_1.1 = f32[32,8,8,256]{3,2,1,0:T(8,128)} custom-call(s32[3,8]{1,0:T(4,128)} %bitcast.8, bf16[2,8,256,256]{3,2,1,0:T(8,128)(2,1)} %rho_ref.19, bf16[3,8,256,256]{3,2,1,0:T(8,128)(2,1)} %shift_ref.19, s32[8,256,256]{2,1,0:T(8,128)} %support_ref.19, bf16[1536,512]{1,0:T(8,128)(2,1)} %constant.20.clone.table_ref, ...), custom_call_target="tpu_custom_call" | custom-call | flops 6400000000 | bytes 16000000 | tf_op jit(solution)/shard_map/head_1/pallas_call | solution.py:250
  32.7 39.3 %all-to-all-done = f32[32,8,8,256]{3,2,1,0:T(8,128)} async-done(((f32[32,8,8,256]{3,2,1,0:T(8,128)}), f32[32,8,8,256]{3,2,1,0:T(8,128)}, u32[]{:S(2)}, u32[]{:S(2)}) %all-to-all-start) | async-done | bytes 2097184 | tf_op jit(solution)/shard_map/all_to_all | solution.py:308
  72.0 4.7 %all-to-all-start.1 = ((f32[32,8,8,256]{3,2,1,0:T(8,128)}), f32[32,8,8,256]{3,2,1,0:T(8,128)}, u32[]{:S(2)}, u32[]{:S(2)}) async-start(f32[32,8,8,256]{3,2,1,0:T(8,128)} %head_1.1), calls=%async_computation.1 | async-start | bytes 4194304 | tf_op jit(solution)/shard_map/all_to_all | solution.py:308
  76.7 0.0 copy-done.6
  76.7 0.0 copy-done.7
  76.7 0.0 copy-start.8
  76.7 1.1 copy-done.8
  77.9 12.1 %x_0.1 = f32[2048,256]{1,0:T(8,128)} custom-call(f32[2048,256]{1,0:T(8,128)} %bitcast.2.in_ref, f32[2048,256]{1,0:T(8,128)S(1)} %bitcast.17, bf16[512,768]{1,0:T(8,128)(2,1)S(1)} %copy-done.8, bf16[512,768]{1,0:T(8,128)(2,1)S(1)} %copy-done.7), custom_call_target="tpu_custom_call" | custom-call | flops 6400000000 | bytes 24000000 | tf_op jit(solution)/shard_map/x_0/pallas_call | solution.py:279
  90.0 37.0 %all-to-all-done.1 = f32[32,8,8,256]{3,2,1,0:T(8,128)} async-done(((f32[32,8,8,256]{3,2,1,0:T(8,128)}), f32[32,8,8,256]{3,2,1,0:T(8,128)}, u32[]{:S(2)}, u32[]{:S(2)}) %all-to-all-start.1) | async-done | bytes 2097184 | tf_op jit(solution)/shard_map/all_to_all | solution.py:308
  127.0 4.7 %all-to-all-start.2 = ((f32[32,8,8,256]{3,2,1,0:T(8,128)}), f32[32,8,8,256]{3,2,1,0:T(8,128)}, u32[]{:S(2)}, u32[]{:S(2)}) async-start(f32[32,8,8,256]{3,2,1,0:T(8,128)} %bitcast.20), calls=%async_computation.2 | async-start | bytes 4194304 | tf_op jit(solution)/shard_map/all_to_all | solution.py:308
  131.8 0.0 copy-start.9
  131.8 1.1 copy-done.9
  132.9 12.1 %x_1.1 = f32[2048,256]{1,0:T(8,128)} custom-call(f32[2048,256]{1,0:T(8,128)} %bitcast.5.in_ref, f32[2048,256]{1,0:T(8,128)S(1)} %bitcast.18, bf16[512,768]{1,0:T(8,128)(2,1)S(1)} %copy-done.9, bf16[512,768]{1,0:T(8,128)(2,1)S(1)} %copy-done.7), custom_call_target="tpu_custom_call" | custom-call | flops 6400000000 | bytes 24000000 | tf_op jit(solution)/shard_map/x_1/pallas_call | solution.py:279
  145.0 37.0 %all-to-all-done.2.in_ref = f32[32,8,8,256]{3,2,1,0:T(8,128)} async-done(((f32[32,8,8,256]{3,2,1,0:T(8,128)}), f32[32,8,8,256]{3,2,1,0:T(8,128)}, u32[]{:S(2)}, u32[]{:S(2)}) %all-to-all-start.2) | async-done | bytes 2097184 | tf_op jit(solution)/shard_map/all_to_all | solution.py:308
  182.1 4.7 %all-to-all-start.3 = ((f32[32,8,8,256]{3,2,1,0:T(8,128)}), f32[32,8,8,256]{3,2,1,0:T(8,128)}, u32[]{:S(2)}, u32[]{:S(2)}) async-start(f32[32,8,8,256]{3,2,1,0:T(8,128)} %bitcast.19), calls=%async_computation.3 | async-start | bytes 4194304 | tf_op jit(solution)/shard_map/all_to_all | solution.py:308
  186.8 5.6 %y_inverse_0.1 = (f32[8,32,256]{2,1,0:T(8,128)S(1)}, f32[8,32,256]{2,1,0:T(8,128)S(1)}, f32[8,32,256]{2,1,0:T(8,128)S(1)}, f32[8,32,256]{2,1,0:T(8,128)S(1)}, f3...) custom-call(s32[1]{0:T(128)} %bitcast.idx_ref, ...), custom_call_target="tpu_custom_call" | custom-call | flops 3200000000 | bytes 12000000 | tf_op jit(solution)/shard_map/y_inverse_0/pallas_call | solution.py:292
  192.4 4.6 %collective-permute-start = (f32[8,32,256]{2,1,0:T(8,128)S(1)}, f32[8,32,256]{2,1,0:T(8,128)S(1)}, u32[]{:S(2)}, u32[]{:S(2)}) collective-permute-start(f32[8,32,256]{2,1,0:T(8,128)S(1)} %get-tuple-element.38), channel_id=1, source_target_pairs={{0,224},{32,0},{64,32},{96,64},{128,96},{160,128},{192,160},{224,1... | collective-permute-start | bytes 786440 | tf_op jit(solution)/shard_map/ppermute | solution.py:312
  197.0 0.0 collective-permute-start.1
  197.0 0.5 collective-permute-start.2
  197.6 4.1 %collective-permute-start.3 = (f32[8,32,256]{2,1,0:T(8,128)S(1)}, f32[8,32,256]{2,1,0:T(8,128)S(1)}, u32[]{:S(2)}, u32[]{:S(2)}) collective-permute-start(f32[8,32,256]{2,1,0:T(8,128)S(1)} %get-tuple-element.43), channel_id=1, source_target_pairs={{0,96},{32,128},{64,160},{96,192},{128,224},{160,0},{192,32},{224,... | collective-permute-start | bytes 786440 | tf_op jit(solution)/shard_map/ppermute | solution.py:312
  201.7 2.5 collective-permute-start.4
  204.1 14.0 %collective-permute-done.refs_0_ = f32[8,32,256]{2,1,0:T(8,128)S(1)} collective-permute-done((f32[8,32,256]{2,1,0:T(8,128)S(1)}, f32[8,32,256]{2,1,0:T(8,128)S(1)}, u32[]{:S(2)}, u32[]{:S(2)}) %collective-permute-start) | collective-permute-done | bytes 262176 | tf_op jit(solution)/shard_map/ppermute | solution.py:312
  218.2 18.9 %collective-permute-start.5 = (f32[8,32,256]{2,1,0:T(8,128)S(1)}, f32[8,32,256]{2,1,0:T(8,128)S(1)}, u32[]{:S(2)}, u32[]{:S(2)}) collective-permute-start(f32[8,32,256]{2,1,0:T(8,128)S(1)} %get-tuple-element.45), channel_id=1, source_target_pairs={{0,160},{32,192},{64,224},{96,0},{128,32},{160,64},{192,96},{224,1... | collective-permute-start | bytes 786440 | tf_op jit(solution)/shard_map/ppermute | solution.py:312
  237.1 0.0 collective-permute-done.1.refs_0_
  237.1 0.0 collective-permute-start.6
  237.1 0.0 collective-permute-done.2.refs_0_
  237.1 0.0 collective-permute-done.3.refs_0_
  237.1 0.0 collective-permute-done.4.refs_0_
  237.1 3.9 %collective-permute-done.5.refs_0_ = f32[8,32,256]{2,1,0:T(8,128)S(1)} collective-permute-done((f32[8,32,256]{2,1,0:T(8,128)S(1)}, f32[8,32,256]{2,1,0:T(8,128)S(1)}, u32[]{:S(2)}, u32[]{:S(2)}) %collective-permute-start.5) | collective-permute-done | bytes 262176 | tf_op jit(solution)/shard_map/ppermute | solution.py:312
  241.0 2.5 collective-permute-done.6.refs_0_
  243.5 0.0 all-to-all-done.3.in_ref
  243.5 0.0 copy-start.3
  243.5 0.0 copy-start.4
  243.5 0.0 copy-start.5
  243.5 5.8 %y_inverse_1.1 = (f32[8,32,256]{2,1,0:T(8,128)S(1)}, f32[8,32,256]{2,1,0:T(8,128)S(1)}, f32[8,32,256]{2,1,0:T(8,128)S(1)}, f32[8,32,256]{2,1,0:T(8,128)S(1)}, f3...) custom-call(s32[1]{0:T(128)} %bitcast.idx_ref, ...), custom_call_target="tpu_custom_call" | custom-call | flops 3200000000 | bytes 12000000 | tf_op jit(solution)/shard_map/y_inverse_1/pallas_call | solution.py:292
  249.3 4.3 %collective-permute-start.13 = (f32[8,32,256]{2,1,0:T(8,128)S(1)}, f32[8,32,256]{2,1,0:T(8,128)S(1)}, u32[]{:S(2)}, u32[]{:S(2)}) collective-permute-start(f32[8,32,256]{2,1,0:T(8,128)S(1)} %get-tuple-element.54), channel_id=1, source_target_pairs={{0,128},{32,160},{64,192},{96,224},{128,0},{160,32},{192,64},{224,... | collective-permute-start | bytes 786440 | tf_op jit(solution)/shard_map/ppermute | solution.py:312
  253.6 1.9 collective-permute-start.12
  255.4 4.1 %collective-permute-start.11 = (f32[8,32,256]{2,1,0:T(8,128)S(1)}, f32[8,32,256]{2,1,0:T(8,128)S(1)}, u32[]{:S(2)}, u32[]{:S(2)}) collective-permute-start(f32[8,32,256]{2,1,0:T(8,128)S(1)} %get-tuple-element.52), channel_id=1, source_target_pairs={{0,160},{32,192},{64,224},{96,0},{128,32},{160,64},{192,96},{224,1... | collective-permute-start | bytes 786440 | tf_op jit(solution)/shard_map/ppermute | solution.py:312
  259.5 0.0 collective-permute-start.10
  259.5 3.2 %collective-permute-start.9 = (f32[8,32,256]{2,1,0:T(8,128)S(1)}, f32[8,32,256]{2,1,0:T(8,128)S(1)}, u32[]{:S(2)}, u32[]{:S(2)}) collective-permute-start(f32[8,32,256]{2,1,0:T(8,128)S(1)} %get-tuple-element.50), channel_id=1, source_target_pairs={{0,192},{32,224},{64,0},{96,32},{128,64},{160,96},{192,128},{224,1... | collective-permute-start | bytes 786440 | tf_op jit(solution)/shard_map/ppermute | solution.py:312
  262.7 0.0 copy-done
  262.7 0.0 copy-done.1
  262.7 0.0 copy-done.2
  262.7 0.0 copy-done.3
  262.7 0.0 copy-done.4
  262.8 1.7 gradient_0.1
  264.5 0.0 collective-permute-done.13.refs_1_
  264.5 3.1 %collective-permute-start.8 = (f32[8,32,256]{2,1,0:T(8,128)S(1)}, f32[8,32,256]{2,1,0:T(8,128)S(1)}, u32[]{:S(2)}, u32[]{:S(2)}) collective-permute-start(f32[8,32,256]{2,1,0:T(8,128)S(1)} %get-tuple-element.49), channel_id=1, source_target_pairs={{0,32},{32,64},{64,96},{96,128},{128,160},{160,192},{192,224},{224... | collective-permute-start | bytes 786440 | tf_op jit(solution)/shard_map/ppermute | solution.py:312
  267.6 1.7 gradient_4.1
  269.4 0.0 collective-permute-done.12.refs_1_
  269.4 2.6 collective-permute-start.7
  272.0 1.7 gradient_3.1
  273.8 0.0 collective-permute-done.11.refs_1_
  273.8 1.7 gradient_5.1
  275.5 0.0 collective-permute-done.10.refs_1_
  275.5 1.7 gradient_2.1
  277.3 0.0 collective-permute-done.9.refs_1_
  277.3 1.7 gradient_6.1
  279.0 1.5 collective-permute-done.8.refs_1_
  280.5 1.7 gradient_1.1
  282.2 0.0 collective-permute-done.7.refs_1_
  282.3 2.8 gradient_7.1
  (6 shorter events, 0.0 us)
Async XLA Ops:
  11.5 60.4 %all-to-all-start = ((f32[32,8,8,256]{3,2,1,0:T(8,128)}), f32[32,8,8,256]{3,2,1,0:T(8,128)}, u32[]{:S(2)}, u32[]{:S(2)}) async-start(f32[32,8,8,256]{3,2,1,0:T(8,128)} %head_0.1), calls=%async_computation | async-start | bytes 4194304 | tf_op jit(solution)/shard_map/all_to_all | solution.py:308
  32.6 44.1 %copy-start.6 = (f32[1,256,8,256]{3,2,1,0:T(8,128)S(1)}, f32[1,256,8,256]{3,2,1,0:T(8,128)}, u32[]{:S(2)}) copy-start(f32[1,256,8,256]{3,2,1,0:T(8,128)} %param.17) | copy-start | bytes 6291460
  32.7 44.1 %copy-start.7 = (bf16[512,768]{1,0:T(8,128)(2,1)S(1)}, bf16[512,768]{1,0:T(8,128)(2,1)}, u32[]{:S(2)}) copy-start(bf16[512,768]{1,0:T(8,128)(2,1)} %constant.17.clone.inverse_ref.table_ref) | copy-start | bytes 2359300
  72.0 55.0 %all-to-all-start.1 = ((f32[32,8,8,256]{3,2,1,0:T(8,128)}), f32[32,8,8,256]{3,2,1,0:T(8,128)}, u32[]{:S(2)}, u32[]{:S(2)}) async-start(f32[32,8,8,256]{3,2,1,0:T(8,128)} %head_1.1), calls=%async_computation.1 | async-start | bytes 4194304 | tf_op jit(solution)/shard_map/all_to_all | solution.py:308
  76.7 1.1 copy-start.8
  127.0 55.0 %all-to-all-start.2 = ((f32[32,8,8,256]{3,2,1,0:T(8,128)}), f32[32,8,8,256]{3,2,1,0:T(8,128)}, u32[]{:S(2)}, u32[]{:S(2)}) async-start(f32[32,8,8,256]{3,2,1,0:T(8,128)} %bitcast.20), calls=%async_computation.2 | async-start | bytes 4194304 | tf_op jit(solution)/shard_map/all_to_all | solution.py:308
  131.8 1.1 copy-start.9
  182.1 61.4 %all-to-all-start.3 = ((f32[32,8,8,256]{3,2,1,0:T(8,128)}), f32[32,8,8,256]{3,2,1,0:T(8,128)}, u32[]{:S(2)}, u32[]{:S(2)}) async-start(f32[32,8,8,256]{3,2,1,0:T(8,128)} %bitcast.19), calls=%async_computation.3 | async-start | bytes 4194304 | tf_op jit(solution)/shard_map/all_to_all | solution.py:308
  192.4 25.7 %collective-permute-start = (f32[8,32,256]{2,1,0:T(8,128)S(1)}, f32[8,32,256]{2,1,0:T(8,128)S(1)}, u32[]{:S(2)}, u32[]{:S(2)}) collective-permute-start(f32[8,32,256]{2,1,0:T(8,128)S(1)} %get-tuple-element.38), channel_id=1, source_target_pairs={{0,224},{32,0},{64,32},{96,64},{128,96},{160,128},{192,160},{224,1... | collective-permute-start | bytes 786440 | tf_op jit(solution)/shard_map/ppermute | solution.py:312
  197.0 40.1 %collective-permute-start.1 = (f32[8,32,256]{2,1,0:T(8,128)S(1)}, f32[8,32,256]{2,1,0:T(8,128)S(1)}, u32[]{:S(2)}, u32[]{:S(2)}) collective-permute-start(f32[8,32,256]{2,1,0:T(8,128)S(1)} %get-tuple-element.41), channel_id=1, source_target_pairs={{0,32},{32,64},{64,96},{96,128},{128,160},{160,192},{192,224},{224... | collective-permute-start | bytes 786440 | tf_op jit(solution)/shard_map/ppermute | solution.py:312
  197.0 40.1 %collective-permute-start.2 = (f32[8,32,256]{2,1,0:T(8,128)S(1)}, f32[8,32,256]{2,1,0:T(8,128)S(1)}, u32[]{:S(2)}, u32[]{:S(2)}) collective-permute-start(f32[8,32,256]{2,1,0:T(8,128)S(1)} %get-tuple-element.42), channel_id=1, source_target_pairs={{0,64},{32,96},{64,128},{96,160},{128,192},{160,224},{192,0},{224,... | collective-permute-start | bytes 786440 | tf_op jit(solution)/shard_map/ppermute | solution.py:312
  197.6 39.5 %collective-permute-start.3 = (f32[8,32,256]{2,1,0:T(8,128)S(1)}, f32[8,32,256]{2,1,0:T(8,128)S(1)}, u32[]{:S(2)}, u32[]{:S(2)}) collective-permute-start(f32[8,32,256]{2,1,0:T(8,128)S(1)} %get-tuple-element.43), channel_id=1, source_target_pairs={{0,96},{32,128},{64,160},{96,192},{128,224},{160,0},{192,32},{224,... | collective-permute-start | bytes 786440 | tf_op jit(solution)/shard_map/ppermute | solution.py:312
  201.7 35.4 %collective-permute-start.4 = (f32[8,32,256]{2,1,0:T(8,128)S(1)}, f32[8,32,256]{2,1,0:T(8,128)S(1)}, u32[]{:S(2)}, u32[]{:S(2)}) collective-permute-start(f32[8,32,256]{2,1,0:T(8,128)S(1)} %get-tuple-element.44), channel_id=1, source_target_pairs={{0,128},{32,160},{64,192},{96,224},{128,0},{160,32},{192,64},{224,... | collective-permute-start | bytes 786440 | tf_op jit(solution)/shard_map/ppermute | solution.py:312
  218.2 22.8 %collective-permute-start.5 = (f32[8,32,256]{2,1,0:T(8,128)S(1)}, f32[8,32,256]{2,1,0:T(8,128)S(1)}, u32[]{:S(2)}, u32[]{:S(2)}) collective-permute-start(f32[8,32,256]{2,1,0:T(8,128)S(1)} %get-tuple-element.45), channel_id=1, source_target_pairs={{0,160},{32,192},{64,224},{96,0},{128,32},{160,64},{192,96},{224,1... | collective-permute-start | bytes 786440 | tf_op jit(solution)/shard_map/ppermute | solution.py:312
  237.1 6.4 %collective-permute-start.6 = (f32[8,32,256]{2,1,0:T(8,128)S(1)}, f32[8,32,256]{2,1,0:T(8,128)S(1)}, u32[]{:S(2)}, u32[]{:S(2)}) collective-permute-start(f32[8,32,256]{2,1,0:T(8,128)S(1)} %get-tuple-element.46), channel_id=1, source_target_pairs={{0,192},{32,224},{64,0},{96,32},{128,64},{160,96},{192,128},{224,1... | collective-permute-start | bytes 786440 | tf_op jit(solution)/shard_map/ppermute | solution.py:312
  243.5 19.3 %copy-start = (bf16[3,8,256,256]{3,2,1,0:T(8,128)(2,1)S(1)}, bf16[3,8,256,256]{3,2,1,0:T(8,128)(2,1)}, u32[]{:S(2)}) copy-start(bf16[3,8,256,256]{3,2,1,0:T(8,128)(2,1)} %shift_ref.19) | copy-start | bytes 9437188
  243.5 19.3 %copy-start.1 = (bf16[2,8,256,256]{3,2,1,0:T(8,128)(2,1)S(1)}, bf16[2,8,256,256]{3,2,1,0:T(8,128)(2,1)}, u32[]{:S(2)}) copy-start(bf16[2,8,256,256]{3,2,1,0:T(8,128)(2,1)} %rho_ref.19) | copy-start | bytes 6291460
  243.5 19.3 %copy-start.2 = (s32[8,256,256]{2,1,0:T(8,128)S(1)}, s32[8,256,256]{2,1,0:T(8,128)}, u32[]{:S(2)}) copy-start(s32[8,256,256]{2,1,0:T(8,128)} %support_ref.19) | copy-start | bytes 6291460
  243.5 19.3 %copy-start.3 = (bf16[512,512]{1,0:T(8,128)(2,1)S(1)}, bf16[512,512]{1,0:T(8,128)(2,1)}, u32[]{:S(2)}) copy-start(bf16[512,512]{1,0:T(8,128)(2,1)} %constant.18.clone.refs_2_) | copy-start | bytes 1572868
  243.5 19.3 %copy-start.4 = (bf16[512,512]{1,0:T(8,128)(2,1)S(1)}, bf16[512,512]{1,0:T(8,128)(2,1)}, u32[]{:S(2)}) copy-start(bf16[512,512]{1,0:T(8,128)(2,1)} %constant.19.clone.refs_3_) | copy-start | bytes 1572868
  243.5 19.3 %copy-start.5 = (s32[8,3]{0,1:T(4,128)S(1)}, s32[8,3]{0,1:T(4,128)}, u32[]{:S(2)}) copy-start(s32[8,3]{0,1:T(4,128)} %param.16) | copy-start | bytes 292
  249.3 15.2 %collective-permute-start.13 = (f32[8,32,256]{2,1,0:T(8,128)S(1)}, f32[8,32,256]{2,1,0:T(8,128)S(1)}, u32[]{:S(2)}, u32[]{:S(2)}) collective-permute-start(f32[8,32,256]{2,1,0:T(8,128)S(1)} %get-tuple-element.54), channel_id=1, source_target_pairs={{0,128},{32,160},{64,192},{96,224},{128,0},{160,32},{192,64},{224,... | collective-permute-start | bytes 786440 | tf_op jit(solution)/shard_map/ppermute | solution.py:312
  253.6 15.8 %collective-permute-start.12 = (f32[8,32,256]{2,1,0:T(8,128)S(1)}, f32[8,32,256]{2,1,0:T(8,128)S(1)}, u32[]{:S(2)}, u32[]{:S(2)}) collective-permute-start(f32[8,32,256]{2,1,0:T(8,128)S(1)} %get-tuple-element.53), channel_id=1, source_target_pairs={{0,96},{32,128},{64,160},{96,192},{128,224},{160,0},{192,32},{224,... | collective-permute-start | bytes 786440 | tf_op jit(solution)/shard_map/ppermute | solution.py:312
  255.4 18.3 %collective-permute-start.11 = (f32[8,32,256]{2,1,0:T(8,128)S(1)}, f32[8,32,256]{2,1,0:T(8,128)S(1)}, u32[]{:S(2)}, u32[]{:S(2)}) collective-permute-start(f32[8,32,256]{2,1,0:T(8,128)S(1)} %get-tuple-element.52), channel_id=1, source_target_pairs={{0,160},{32,192},{64,224},{96,0},{128,32},{160,64},{192,96},{224,1... | collective-permute-start | bytes 786440 | tf_op jit(solution)/shard_map/ppermute | solution.py:312
  259.5 16.0 %collective-permute-start.10 = (f32[8,32,256]{2,1,0:T(8,128)S(1)}, f32[8,32,256]{2,1,0:T(8,128)S(1)}, u32[]{:S(2)}, u32[]{:S(2)}) collective-permute-start(f32[8,32,256]{2,1,0:T(8,128)S(1)} %get-tuple-element.51), channel_id=1, source_target_pairs={{0,64},{32,96},{64,128},{96,160},{128,192},{160,224},{192,0},{224,... | collective-permute-start | bytes 786440 | tf_op jit(solution)/shard_map/ppermute | solution.py:312
  259.5 17.8 %collective-permute-start.9 = (f32[8,32,256]{2,1,0:T(8,128)S(1)}, f32[8,32,256]{2,1,0:T(8,128)S(1)}, u32[]{:S(2)}, u32[]{:S(2)}) collective-permute-start(f32[8,32,256]{2,1,0:T(8,128)S(1)} %get-tuple-element.50), channel_id=1, source_target_pairs={{0,192},{32,224},{64,0},{96,32},{128,64},{160,96},{192,128},{224,1... | collective-permute-start | bytes 786440 | tf_op jit(solution)/shard_map/ppermute | solution.py:312
  264.5 16.0 %collective-permute-start.8 = (f32[8,32,256]{2,1,0:T(8,128)S(1)}, f32[8,32,256]{2,1,0:T(8,128)S(1)}, u32[]{:S(2)}, u32[]{:S(2)}) collective-permute-start(f32[8,32,256]{2,1,0:T(8,128)S(1)} %get-tuple-element.49), channel_id=1, source_target_pairs={{0,32},{32,64},{64,96},{96,128},{128,160},{160,192},{192,224},{224... | collective-permute-start | bytes 786440 | tf_op jit(solution)/shard_map/ppermute | solution.py:312
  269.4 12.8 %collective-permute-start.7 = (f32[8,32,256]{2,1,0:T(8,128)S(1)}, f32[8,32,256]{2,1,0:T(8,128)S(1)}, u32[]{:S(2)}, u32[]{:S(2)}) collective-permute-start(f32[8,32,256]{2,1,0:T(8,128)S(1)} %get-tuple-element.48), channel_id=1, source_target_pairs={{0,224},{32,0},{64,32},{96,64},{128,96},{160,128},{192,160},{224,1... | collective-permute-start | bytes 786440 | tf_op jit(solution)/shard_map/ppermute | solution.py:312

commit v4 on v3

--- a/solution.py
+++ b/solution.py
@@ -17,7 +17,7 @@
 XL = 8
 NREF = 8
 HEAD_ROWS = 32
-R_ORDER = (4, 3, 5, 2, 6, 1, 7)
+R_ORDER = (5, 4, 1, 3, 7, 2, 6)
 BF = jnp.bfloat16
 F32 = jnp.float32
 
@@ -169,25 +169,29 @@
         copy.wait()
 
 
+def partner(r, s, sign):
+    return lax.rem(r // 2 + NREF // 2 + sign * (s // 2), NREF // 2) * 2 + lax.rem(r + s, 2)
+
+
 def y_inverse_kernel(idx_ref, in_ref, table_ref, *refs):
-    outs, (u_ref, t_ref, sems) = refs[:NREF], refs[NREF:]
+    outs, t_ref = refs[:NREF], refs[NREF]
     r = idx_ref[0]
-    copies = [pltpu.make_async_copy(in_ref.at[:, x], u_ref.at[x], sems.at[x]) for x in range(XL)]
-    for copy in copies:
-        copy.start()
-    for x in range(XL):
-        copies[x].wait()
-        t_ref[...] = left_multiply(table_ref[...], u_ref[x].reshape(N, 2 * KC))
+
+    def step(x, carry):
+        t_ref[...] = left_multiply(table_ref[...], in_ref[:, x].reshape(N, 2 * KC))
         for s in range(NREF):
-            start = pl.multiple_of(lax.rem(r + s, NREF) * 32, 32)
+            start = pl.multiple_of(partner(r, s, 1) * 32, 32)
             outs[s][x] = t_ref[pl.ds(start, 32), :]
+        return carry
+
+    lax.fori_loop(0, XL, step, 0)
 
 
 def gradient_kernel(shift_by, idx_ref, miller_ref, rho_ref, shift_ref, support_ref, *refs):
     ins, high_ref, low_ref = refs[:CH], refs[CH], refs[CH + 1]
     sums = refs[CH + 2 : -3]
     rho_out, shift_out, back_ref = refs[-3:]
-    g = lax.rem(idx_ref[0] + NREF - shift_by, NREF)
+    g = partner(idx_ref[0], shift_by, -1)
     h, k, l = (miller_ref[c, g].astype(F32) for c in range(3))
     high, low = split(jnp.concatenate([ref[...].reshape(N, 2 * KC) for ref in ins], 1))
     dot = functools.partial(jnp.dot, preferred_element_type=F32)
@@ -291,24 +295,20 @@
     def y_inverse(c, part):
         return pl.pallas_call(
             y_inverse_kernel,
-            in_specs=[SMEM, HBM, VMEM],
+            in_specs=[SMEM, VMEM, VMEM],
             out_specs=[VMEM] * NREF,
             out_shape=[f32(XL, 32, 2 * KC)] * NREF,
-            scratch_shapes=[
-                pltpu.VMEM((XL, SLABS, XL, 2 * KC), F32),
-                pltpu.VMEM((N, 2 * KC), F32),
-                pltpu.SemaphoreType.DMA((XL,)),
-            ],
+            scratch_shapes=[pltpu.VMEM((N, 2 * KC), F32)],
             compiler_params=params(24),
             cost_estimate=cost(3.2e9, 12e6),
             name=f"y_inverse_{c}",
-        )(idx, in_hbm(part), inverse)
+        )(idx, part, inverse)
 
     def over_grid(part):
         return lax.all_to_all(part, "grid", 0, 0, tiled=True)
 
     def over_refl(parts):
-        ring = lambda s: [(i, (i + s) % NREF) for i in range(NREF)]
+        ring = lambda s: [(i, (i // 2 + s // 2) % (NREF // 2) * 2 + (i + s) % 2) for i in range(NREF)]
         moved = {s: lax.ppermute(parts[s], "refl", ring(s)) for s in R_ORDER}
         return [parts[0]] + [moved[s] for s in range(1, NREF)]
 
@@ -344,7 +344,7 @@
     f1 = over_grid(after(head(1, millers, density, displacement, support), f0))
     b0 = over_grid(after(x_both(0, f0), f1))
     b1 = over_grid(after(x_both(1, f1), b0))
-    r0 = over_refl(y_inverse(0, b0))
+    r0 = over_refl(y_inverse(0, in_hbm(b0)))
     r1 = over_refl(y_inverse(1, after(b1, *r0)))
     sums = ()
     for s in (0,) + R_ORDER:

time: 289 us -> 286 us (0.990)
  Pallas kernels: 72.5 us -> 68.9 us
  local copies, waits for them, and re-layouts: 2.3 us -> 5.55 us
    pallas_call x2, Pallas kernels: 11.4 us -> 7.93 us  [y_inverse(): pl.pallas_call(y_inverse_kernel, in_specs=[SMEM, VMEM, VMEM], out_specs=[...]
    unnamed x20 -> x34, local copies, waits for them, and re-layouts: 2.3 us -> 5.55 us
  transfers between devices with their start and end apart: 18 -> 18, of which waited for: 7 -> 6; matrix products, arithmetic and copies ran while one was open for 0% -> 0% of each run, Pallas kernels for 19% -> 18%
where the time goes in v4:
time: 286 us; the launch traced here: 283 us
  waiting for transfers between devices  135 us (47%)
  starting transfers between devices  72.1 us (25%)
  Pallas kernels  68.9 us (24%)
  local copies, waits for them, and re-layouts  5.55 us (2%)
    all_to_all x4, waiting for transfers between devices, over_grid(): return lax.all_to_all(part, 'grid', 0, 0, tiled=True)  113 us
    ppermute x14, starting transfers between devices, over_refl(): moved = {s: lax.ppermute(parts[s], 'refl', ring(s)) for s in R_ORDER}  47.8 us
    all_to_all x4, starting transfers between devices, over_grid(): return lax.all_to_all(part, 'grid', 0, 0, tiled=True)  24.3 us
    pallas_call x2, Pallas kernels, x_both(): pl.pallas_call(x_kernel, grid=(1,), in_specs=[HBM, pl.BlockSpec((N * XL,...  24.2 us
    pallas_call x2, Pallas kernels, head(): pl.pallas_call(head_kernel, grid=(XL + 2,), in_specs=[SMEM, pl.BlockSpec(...  21.8 us
    ppermute x14, waiting for transfers between devices, over_refl(): moved = {s: lax.ppermute(parts[s], 'refl', ring(s)) for s in R_ORDER}  21.6 us
    pallas_call x8, Pallas kernels, gradient(): pl.pallas_call(functools.partial(gradient_kernel, s), grid_spec=pltpu.Pre...  15 us
    pallas_call x2, Pallas kernels, y_inverse(): pl.pallas_call(y_inverse_kernel, in_specs=[SMEM, VMEM, VMEM], out_specs=[...  7.93 us
  transfers between devices with their start and end apart: 18, of which 6 were waited for; matrix products, arithmetic and copies ran while one was open for 0% of the time, Pallas kernels for 18%

profile of v4, /device:TPU:8, one launch (start us, length us, event | category | flops | bytes accessed | tf_op | source)
XLA Modules:
  0.0 282.6 jit_solution(331803468571836080)
XLA Ops:
  0.6 10.9 %head_0.1 = f32[32,8,8,256]{3,2,1,0:T(8,128)} custom-call(s32[3,8]{1,0:T(4,128)} %bitcast.7, bf16[2,8,256,256]{3,2,1,0:T(8,128)(2,1)} %rho_ref.19, bf16[3,8,256,256]{3,2,1,0:T(8,128)(2,1)} %shift_ref.19, s32[8,256,256]{2,1,0:T(8,128)} %support_ref.19, bf16[1536,512]{1,0:T(8,128)(2,1)} %constant.20.clone.table_ref, ...), custom_call_target="tpu_custom_call" | custom-call | flops 6400000000 | bytes 16000000 | tf_op jit(solution)/shard_map/head_0/pallas_call | solution.py:254
  11.6 10.1 %all-to-all-start = ((f32[32,8,8,256]{3,2,1,0:T(8,128)}), f32[32,8,8,256]{3,2,1,0:T(8,128)}, u32[]{:S(2)}, u32[]{:S(2)}) async-start(f32[32,8,8,256]{3,2,1,0:T(8,128)} %head_0.1), calls=%async_computation | async-start | bytes 4194304 | tf_op jit(solution)/shard_map/all_to_all | solution.py:308
  21.7 10.9 %head_1.1 = f32[32,8,8,256]{3,2,1,0:T(8,128)} custom-call(s32[3,8]{1,0:T(4,128)} %bitcast.8, bf16[2,8,256,256]{3,2,1,0:T(8,128)(2,1)} %rho_ref.19, bf16[3,8,256,256]{3,2,1,0:T(8,128)(2,1)} %shift_ref.19, s32[8,256,256]{2,1,0:T(8,128)} %support_ref.19, bf16[1536,512]{1,0:T(8,128)(2,1)} %constant.20.clone.table_ref, ...), custom_call_target="tpu_custom_call" | custom-call | flops 6400000000 | bytes 16000000 | tf_op jit(solution)/shard_map/head_1/pallas_call | solution.py:254
  32.6 39.4 %all-to-all-done = f32[32,8,8,256]{3,2,1,0:T(8,128)} async-done(((f32[32,8,8,256]{3,2,1,0:T(8,128)}), f32[32,8,8,256]{3,2,1,0:T(8,128)}, u32[]{:S(2)}, u32[]{:S(2)}) %all-to-all-start) | async-done | bytes 2097184 | tf_op jit(solution)/shard_map/all_to_all | solution.py:308
  72.0 4.7 %all-to-all-start.1 = ((f32[32,8,8,256]{3,2,1,0:T(8,128)}), f32[32,8,8,256]{3,2,1,0:T(8,128)}, u32[]{:S(2)}, u32[]{:S(2)}) async-start(f32[32,8,8,256]{3,2,1,0:T(8,128)} %head_1.1), calls=%async_computation.1 | async-start | bytes 4194304 | tf_op jit(solution)/shard_map/all_to_all | solution.py:308
  76.7 0.0 copy-start.15
  76.8 1.1 copy-done.15
  77.9 12.1 %x_0.1 = f32[2048,256]{1,0:T(8,128)} custom-call(f32[2048,256]{1,0:T(8,128)} %bitcast.2.in_ref, f32[2048,256]{1,0:T(8,128)S(1)} %bitcast.17, bf16[512,768]{1,0:T(8,128)(2,1)S(1)} %copy-done.15, bf16[512,768]{1,0:T(8,128)(2,1)S(1)} %copy-done.13), custom_call_target="tpu_custom_call" | custom-call | flops 6400000000 | bytes 24000000 | tf_op jit(solution)/shard_map/x_0/pallas_call | solution.py:283
  90.0 37.0 %all-to-all-done.1 = f32[32,8,8,256]{3,2,1,0:T(8,128)} async-done(((f32[32,8,8,256]{3,2,1,0:T(8,128)}), f32[32,8,8,256]{3,2,1,0:T(8,128)}, u32[]{:S(2)}, u32[]{:S(2)}) %all-to-all-start.1) | async-done | bytes 2097184 | tf_op jit(solution)/shard_map/all_to_all | solution.py:308
  127.0 4.7 %all-to-all-start.2 = ((f32[32,8,8,256]{3,2,1,0:T(8,128)}), f32[32,8,8,256]{3,2,1,0:T(8,128)}, u32[]{:S(2)}, u32[]{:S(2)}) async-start(f32[32,8,8,256]{3,2,1,0:T(8,128)} %bitcast.20), calls=%async_computation.2 | async-start | bytes 4194304 | tf_op jit(solution)/shard_map/all_to_all | solution.py:308
  131.8 0.0 copy-start.16
  131.8 1.1 copy-done.16
  132.9 12.1 %x_1.1 = f32[2048,256]{1,0:T(8,128)} custom-call(f32[2048,256]{1,0:T(8,128)} %bitcast.5.in_ref, f32[2048,256]{1,0:T(8,128)S(1)} %bitcast.18, bf16[512,768]{1,0:T(8,128)(2,1)S(1)} %copy-done.16, bf16[512,768]{1,0:T(8,128)(2,1)S(1)} %copy-done.13), custom_call_target="tpu_custom_call" | custom-call | flops 6400000000 | bytes 24000000 | tf_op jit(solution)/shard_map/x_1/pallas_call | solution.py:283
  145.0 37.0 %all-to-all-done.2.in_ref = f32[32,8,8,256]{3,2,1,0:T(8,128)} async-done(((f32[32,8,8,256]{3,2,1,0:T(8,128)}), f32[32,8,8,256]{3,2,1,0:T(8,128)}, u32[]{:S(2)}, u32[]{:S(2)}) %all-to-all-start.2) | async-done | bytes 2097184 | tf_op jit(solution)/shard_map/all_to_all | solution.py:308
  182.1 4.7 %all-to-all-start.3 = ((f32[32,8,8,256]{3,2,1,0:T(8,128)}), f32[32,8,8,256]{3,2,1,0:T(8,128)S(1)}, u32[]{:S(2)}, u32[]{:S(2)}) async-start(f32[32,8,8,256]{3,2,1,0:T(8,128)} %bitcast.19), calls=%async_computation.3 | async-start | bytes 4194304 | tf_op jit(solution)/shard_map/all_to_all | solution.py:308
  186.8 4.7 %y_inverse_0.1 = (f32[8,32,256]{2,1,0:T(8,128)S(1)}, f32[8,32,256]{2,1,0:T(8,128)S(1)}, f32[8,32,256]{2,1,0:T(8,128)S(1)}, f32[8,32,256]{2,1,0:T(8,128)S(1)}, f3...) custom-call(s32[1]{0:T(128)} %bitcast.idx_ref, ...), custom_call_target="tpu_custom_call" | custom-call | flops 3200000000 | bytes 12000000 | tf_op jit(solution)/shard_map/y_inverse_0/pallas_call | solution.py:296
  191.5 0.0 copy-start.7
  191.5 0.7 copy-done.7
  192.2 2.8 collective-permute-start
  195.0 2.3 collective-permute-start.1
  197.3 0.0 collective-permute-start.2
  197.3 1.4 collective-permute-start.3
  198.7 3.9 %collective-permute-start.4 = (f32[8,32,256]{2,1,0:T(8,128)S(1)}, f32[8,32,256]{2,1,0:T(8,128)S(1)}, u32[]{:S(2)}, u32[]{:S(2)}) collective-permute-start(f32[8,32,256]{2,1,0:T(8,128)S(1)} %get-tuple-element.44), channel_id=1, source_target_pairs={{0,128},{32,160},{64,192},{96,224},{128,0},{160,32},{192,64},{224,... | collective-permute-start | bytes 786440 | tf_op jit(solution)/shard_map/ppermute | solution.py:312
  202.7 0.0 collective-permute-done.refs_0_
  202.7 2.7 collective-permute-start.5
  205.4 13.7 %collective-permute-done.1.refs_0_ = f32[8,32,256]{2,1,0:T(8,128)S(1)} collective-permute-done((f32[8,32,256]{2,1,0:T(8,128)S(1)}, f32[8,32,256]{2,1,0:T(8,128)S(1)}, u32[]{:S(2)}, u32[]{:S(2)}) %collective-permute-start.1) | collective-permute-done | bytes 262176 | tf_op jit(solution)/shard_map/ppermute | solution.py:312
  219.0 15.9 %collective-permute-start.6 = (f32[8,32,256]{2,1,0:T(8,128)S(1)}, f32[8,32,256]{2,1,0:T(8,128)S(1)}, u32[]{:S(2)}, u32[]{:S(2)}) collective-permute-start(f32[8,32,256]{2,1,0:T(8,128)S(1)} %get-tuple-element.46), channel_id=1, source_target_pairs={{0,224},{32,192},{64,32},{96,0},{128,96},{160,64},{192,160},{224,1... | collective-permute-start | bytes 786440 | tf_op jit(solution)/shard_map/ppermute | solution.py:312
  234.9 0.0 collective-permute-done.2.refs_0_
  234.9 0.0 collective-permute-done.3.refs_0_
  234.9 0.0 collective-permute-done.4.refs_0_
  234.9 0.0 copy-start.5
  234.9 0.7 copy-done.5
  235.6 0.0 collective-permute-done.5.refs_0_
  235.6 0.7 copy-done.9
  236.3 4.3 %collective-permute-done.6.refs_0_ = f32[8,32,256]{2,1,0:T(8,128)S(1)} collective-permute-done((f32[8,32,256]{2,1,0:T(8,128)S(1)}, f32[8,32,256]{2,1,0:T(8,128)S(1)}, u32[]{:S(2)}, u32[]{:S(2)}) %collective-permute-start.6) | collective-permute-done | bytes 262176 | tf_op jit(solution)/shard_map/ppermute | solution.py:312
  240.6 0.0 all-to-all-done.3.in_ref
  240.6 1.1 copy-done.14
  241.8 0.0 copy-start.4
  241.8 0.0 copy-start.11
  241.8 3.2 %y_inverse_1.1 = (f32[8,32,256]{2,1,0:T(8,128)S(1)}, f32[8,32,256]{2,1,0:T(8,128)S(1)}, f32[8,32,256]{2,1,0:T(8,128)S(1)}, f32[8,32,256]{2,1,0:T(8,128)S(1)}, f3...) custom-call(s32[1]{0:T(128)} %bitcast.idx_ref, ...), custom_call_target="tpu_custom_call" | custom-call | flops 3200000000 | bytes 12000000 | tf_op jit(solution)/shard_map/y_inverse_1/pallas_call | solution.py:296
  245.0 2.3 collective-permute-start.13
  247.3 0.9 collective-permute-start.12
  248.2 3.4 %collective-permute-start.11 = (f32[8,32,256]{2,1,0:T(8,128)S(1)}, f32[8,32,256]{2,1,0:T(8,128)S(1)}, u32[]{:S(2)}, u32[]{:S(2)}) collective-permute-start(f32[8,32,256]{2,1,0:T(8,128)S(1)} %get-tuple-element.52), channel_id=1, source_target_pairs={{0,32},{32,0},{64,96},{96,64},{128,160},{160,128},{192,224},{224,1... | collective-permute-start | bytes 786440 | tf_op jit(solution)/shard_map/ppermute | solution.py:312
  251.6 3.0 %collective-permute-start.10 = (f32[8,32,256]{2,1,0:T(8,128)S(1)}, f32[8,32,256]{2,1,0:T(8,128)S(1)}, u32[]{:S(2)}, u32[]{:S(2)}) collective-permute-start(f32[8,32,256]{2,1,0:T(8,128)S(1)} %get-tuple-element.51), channel_id=1, source_target_pairs={{0,96},{32,64},{64,160},{96,128},{128,224},{160,192},{192,32},{224... | collective-permute-start | bytes 786440 | tf_op jit(solution)/shard_map/ppermute | solution.py:312
  254.6 2.7 collective-permute-start.9
  257.3 0.0 copy-start.10
  257.3 1.7 gradient_0.1
  259.1 0.0 collective-permute-done.13.refs_1_
  259.1 0.1 collective-permute-start.8
  259.2 0.0 copy-start.6
  259.2 1.7 gradient_5.1
  260.9 0.0 collective-permute-done.12.refs_1_
  260.9 6.4 %collective-permute-start.7 = (f32[8,32,256]{2,1,0:T(8,128)S(1)}, f32[8,32,256]{2,1,0:T(8,128)S(1)}, u32[]{:S(2)}, u32[]{:S(2)}) collective-permute-start(f32[8,32,256]{2,1,0:T(8,128)S(1)} %get-tuple-element.48), channel_id=1, source_target_pairs={{0,192},{32,224},{64,0},{96,32},{128,64},{160,96},{192,128},{224,1... | collective-permute-start | bytes 786440 | tf_op jit(solution)/shard_map/ppermute | solution.py:312
  267.4 1.7 gradient_4.1
  269.1 3.6 %collective-permute-done.11.refs_1_ = f32[8,32,256]{2,1,0:T(8,128)S(1)} collective-permute-done((f32[8,32,256]{2,1,0:T(8,128)S(1)}, f32[8,32,256]{2,1,0:T(8,128)S(1)}, u32[]{:S(2)}, u32[]{:S(2)}) %collective-permute-start.11) | collective-permute-done | bytes 262176 | tf_op jit(solution)/shard_map/ppermute | solution.py:312
  272.7 1.7 gradient_1.1
  274.5 0.0 collective-permute-done.10.refs_1_
  274.5 1.7 gradient_3.1
  276.2 0.0 collective-permute-done.9.refs_1_
  276.3 1.7 gradient_7.1
  278.0 0.0 collective-permute-done.8.refs_1_
  278.0 1.7 gradient_2.1
  279.8 0.0 collective-permute-done.7.refs_1_
  279.8 2.8 gradient_6.1
  (20 shorter events, 0.0 us)
Async XLA Ops:
  11.6 60.4 %all-to-all-start = ((f32[32,8,8,256]{3,2,1,0:T(8,128)}), f32[32,8,8,256]{3,2,1,0:T(8,128)}, u32[]{:S(2)}, u32[]{:S(2)}) async-start(f32[32,8,8,256]{3,2,1,0:T(8,128)} %head_0.1), calls=%async_computation | async-start | bytes 4194304 | tf_op jit(solution)/shard_map/all_to_all | solution.py:308
  32.6 44.1 %copy-start.12 = (f32[1,256,8,256]{3,2,1,0:T(8,128)S(1)}, f32[1,256,8,256]{3,2,1,0:T(8,128)}, u32[]{:S(2)}) copy-start(f32[1,256,8,256]{3,2,1,0:T(8,128)} %param.17) | copy-start | bytes 6291460
  32.6 44.1 %copy-start.13 = (bf16[512,768]{1,0:T(8,128)(2,1)S(1)}, bf16[512,768]{1,0:T(8,128)(2,1)}, u32[]{:S(2)}) copy-start(bf16[512,768]{1,0:T(8,128)(2,1)} %constant.17.clone.inverse_ref.table_ref) | copy-start | bytes 2359300
  72.0 55.0 %all-to-all-start.1 = ((f32[32,8,8,256]{3,2,1,0:T(8,128)}), f32[32,8,8,256]{3,2,1,0:T(8,128)}, u32[]{:S(2)}, u32[]{:S(2)}) async-start(f32[32,8,8,256]{3,2,1,0:T(8,128)} %head_1.1), calls=%async_computation.1 | async-start | bytes 4194304 | tf_op jit(solution)/shard_map/all_to_all | solution.py:308
  76.7 1.1 copy-start.15
  127.0 55.0 %all-to-all-start.2 = ((f32[32,8,8,256]{3,2,1,0:T(8,128)}), f32[32,8,8,256]{3,2,1,0:T(8,128)}, u32[]{:S(2)}, u32[]{:S(2)}) async-start(f32[32,8,8,256]{3,2,1,0:T(8,128)} %bitcast.20), calls=%async_computation.2 | async-start | bytes 4194304 | tf_op jit(solution)/shard_map/all_to_all | solution.py:308
  131.8 1.1 copy-start.16
  182.1 58.5 %all-to-all-start.3 = ((f32[32,8,8,256]{3,2,1,0:T(8,128)}), f32[32,8,8,256]{3,2,1,0:T(8,128)S(1)}, u32[]{:S(2)}, u32[]{:S(2)}) async-start(f32[32,8,8,256]{3,2,1,0:T(8,128)} %bitcast.19), calls=%async_computation.3 | async-start | bytes 4194304 | tf_op jit(solution)/shard_map/all_to_all | solution.py:308
  191.5 0.7 copy-start.7
  192.2 10.4 %collective-permute-start = (f32[8,32,256]{2,1,0:T(8,128)S(1)}, f32[8,32,256]{2,1,0:T(8,128)S(1)}, u32[]{:S(2)}, u32[]{:S(2)}) collective-permute-start(f32[8,32,256]{2,1,0:T(8,128)S(1)} %get-tuple-element.38), channel_id=1, source_target_pairs={{0,192},{32,224},{64,0},{96,32},{128,64},{160,96},{192,128},{224,1... | collective-permute-start | bytes 786440 | tf_op jit(solution)/shard_map/ppermute | solution.py:312
  195.0 24.0 %collective-permute-start.1 = (f32[8,32,256]{2,1,0:T(8,128)S(1)}, f32[8,32,256]{2,1,0:T(8,128)S(1)}, u32[]{:S(2)}, u32[]{:S(2)}) collective-permute-start(f32[8,32,256]{2,1,0:T(8,128)S(1)} %get-tuple-element.41), channel_id=1, source_target_pairs={{0,32},{32,0},{64,96},{96,64},{128,160},{160,128},{192,224},{224,1... | collective-permute-start | bytes 786440 | tf_op jit(solution)/shard_map/ppermute | solution.py:312
  197.3 37.6 %collective-permute-start.2 = (f32[8,32,256]{2,1,0:T(8,128)S(1)}, f32[8,32,256]{2,1,0:T(8,128)S(1)}, u32[]{:S(2)}, u32[]{:S(2)}) collective-permute-start(f32[8,32,256]{2,1,0:T(8,128)S(1)} %get-tuple-element.42), channel_id=1, source_target_pairs={{0,64},{32,96},{64,128},{96,160},{128,192},{160,224},{192,0},{224,... | collective-permute-start | bytes 786440 | tf_op jit(solution)/shard_map/ppermute | solution.py:312
  197.3 37.6 %collective-permute-start.3 = (f32[8,32,256]{2,1,0:T(8,128)S(1)}, f32[8,32,256]{2,1,0:T(8,128)S(1)}, u32[]{:S(2)}, u32[]{:S(2)}) collective-permute-start(f32[8,32,256]{2,1,0:T(8,128)S(1)} %get-tuple-element.43), channel_id=1, source_target_pairs={{0,96},{32,64},{64,160},{96,128},{128,224},{160,192},{192,32},{224... | collective-permute-start | bytes 786440 | tf_op jit(solution)/shard_map/ppermute | solution.py:312
  198.7 36.2 %collective-permute-start.4 = (f32[8,32,256]{2,1,0:T(8,128)S(1)}, f32[8,32,256]{2,1,0:T(8,128)S(1)}, u32[]{:S(2)}, u32[]{:S(2)}) collective-permute-start(f32[8,32,256]{2,1,0:T(8,128)S(1)} %get-tuple-element.44), channel_id=1, source_target_pairs={{0,128},{32,160},{64,192},{96,224},{128,0},{160,32},{192,64},{224,... | collective-permute-start | bytes 786440 | tf_op jit(solution)/shard_map/ppermute | solution.py:312
  202.7 32.9 %collective-permute-start.5 = (f32[8,32,256]{2,1,0:T(8,128)S(1)}, f32[8,32,256]{2,1,0:T(8,128)S(1)}, u32[]{:S(2)}, u32[]{:S(2)}) collective-permute-start(f32[8,32,256]{2,1,0:T(8,128)S(1)} %get-tuple-element.45), channel_id=1, source_target_pairs={{0,160},{32,128},{64,224},{96,192},{128,32},{160,0},{192,96},{224,... | collective-permute-start | bytes 786440 | tf_op jit(solution)/shard_map/ppermute | solution.py:312
  219.0 21.6 %collective-permute-start.6 = (f32[8,32,256]{2,1,0:T(8,128)S(1)}, f32[8,32,256]{2,1,0:T(8,128)S(1)}, u32[]{:S(2)}, u32[]{:S(2)}) collective-permute-start(f32[8,32,256]{2,1,0:T(8,128)S(1)} %get-tuple-element.46), channel_id=1, source_target_pairs={{0,224},{32,192},{64,32},{96,0},{128,96},{160,64},{192,160},{224,1... | collective-permute-start | bytes 786440 | tf_op jit(solution)/shard_map/ppermute | solution.py:312
  234.9 0.7 copy-start.5
  235.6 0.7 copy-start.9
  240.6 1.1 copy-start.14
  241.8 15.5 %copy-start = (bf16[3,8,256,256]{3,2,1,0:T(8,128)(2,1)S(1)}, bf16[3,8,256,256]{3,2,1,0:T(8,128)(2,1)}, u32[]{:S(2)}) copy-start(bf16[3,8,256,256]{3,2,1,0:T(8,128)(2,1)} %shift_ref.19) | copy-start | bytes 9437188
  241.8 15.5 %copy-start.1 = (bf16[2,8,256,256]{3,2,1,0:T(8,128)(2,1)S(1)}, bf16[2,8,256,256]{3,2,1,0:T(8,128)(2,1)}, u32[]{:S(2)}) copy-start(bf16[2,8,256,256]{3,2,1,0:T(8,128)(2,1)} %rho_ref.19) | copy-start | bytes 6291460
  241.8 15.5 %copy-start.2 = (s32[8,256,256]{2,1,0:T(8,128)S(1)}, s32[8,256,256]{2,1,0:T(8,128)}, u32[]{:S(2)}) copy-start(s32[8,256,256]{2,1,0:T(8,128)} %support_ref.19) | copy-start | bytes 6291460
  241.8 15.5 %copy-start.3 = (bf16[512,512]{1,0:T(8,128)(2,1)S(1)}, bf16[512,512]{1,0:T(8,128)(2,1)}, u32[]{:S(2)}) copy-start(bf16[512,512]{1,0:T(8,128)(2,1)} %constant.18.clone.refs_2_) | copy-start | bytes 1572868
  241.8 15.5 %copy-start.4 = (bf16[512,512]{1,0:T(8,128)(2,1)S(1)}, bf16[512,512]{1,0:T(8,128)(2,1)}, u32[]{:S(2)}) copy-start(bf16[512,512]{1,0:T(8,128)(2,1)} %constant.19.clone.refs_3_) | copy-start | bytes 1572868
  241.8 15.5 %copy-start.8 = (f32[8,32,256]{2,1,0:T(8,128)S(1)}, f32[8,32,256]{2,1,0:T(8,128)}, u32[]{:S(2)}) copy-start(f32[8,32,256]{2,1,0:T(8,128)} %copy-done.7) | copy-start | bytes 786436
  241.8 15.5 %copy-start.11 = (s32[8,3]{0,1:T(4,128)S(1)}, s32[8,3]{0,1:T(4,128)}, u32[]{:S(2)}) copy-start(s32[8,3]{0,1:T(4,128)} %param.16) | copy-start | bytes 292
  245.0 14.1 %collective-permute-start.13 = (f32[8,32,256]{2,1,0:T(8,128)S(1)}, f32[8,32,256]{2,1,0:T(8,128)S(1)}, u32[]{:S(2)}, u32[]{:S(2)}) collective-permute-start(f32[8,32,256]{2,1,0:T(8,128)S(1)} %get-tuple-element.54), channel_id=1, source_target_pairs={{0,160},{32,128},{64,224},{96,192},{128,32},{160,0},{192,96},{224,... | collective-permute-start | bytes 786440 | tf_op jit(solution)/shard_map/ppermute | solution.py:312
  247.3 13.6 %collective-permute-start.12 = (f32[8,32,256]{2,1,0:T(8,128)S(1)}, f32[8,32,256]{2,1,0:T(8,128)S(1)}, u32[]{:S(2)}, u32[]{:S(2)}) collective-permute-start(f32[8,32,256]{2,1,0:T(8,128)S(1)} %get-tuple-element.53), channel_id=1, source_target_pairs={{0,128},{32,160},{64,192},{96,224},{128,0},{160,32},{192,64},{224,... | collective-permute-start | bytes 786440 | tf_op jit(solution)/shard_map/ppermute | solution.py:312
  248.2 24.6 %collective-permute-start.11 = (f32[8,32,256]{2,1,0:T(8,128)S(1)}, f32[8,32,256]{2,1,0:T(8,128)S(1)}, u32[]{:S(2)}, u32[]{:S(2)}) collective-permute-start(f32[8,32,256]{2,1,0:T(8,128)S(1)} %get-tuple-element.52), channel_id=1, source_target_pairs={{0,32},{32,0},{64,96},{96,64},{128,160},{160,128},{192,224},{224,1... | collective-permute-start | bytes 786440 | tf_op jit(solution)/shard_map/ppermute | solution.py:312
  251.6 22.9 %collective-permute-start.10 = (f32[8,32,256]{2,1,0:T(8,128)S(1)}, f32[8,32,256]{2,1,0:T(8,128)S(1)}, u32[]{:S(2)}, u32[]{:S(2)}) collective-permute-start(f32[8,32,256]{2,1,0:T(8,128)S(1)} %get-tuple-element.51), channel_id=1, source_target_pairs={{0,96},{32,64},{64,160},{96,128},{128,224},{160,192},{192,32},{224... | collective-permute-start | bytes 786440 | tf_op jit(solution)/shard_map/ppermute | solution.py:312
  254.6 21.6 %collective-permute-start.9 = (f32[8,32,256]{2,1,0:T(8,128)S(1)}, f32[8,32,256]{2,1,0:T(8,128)S(1)}, u32[]{:S(2)}, u32[]{:S(2)}) collective-permute-start(f32[8,32,256]{2,1,0:T(8,128)S(1)} %get-tuple-element.50), channel_id=1, source_target_pairs={{0,224},{32,192},{64,32},{96,0},{128,96},{160,64},{192,160},{224,1... | collective-permute-start | bytes 786440 | tf_op jit(solution)/shard_map/ppermute | solution.py:312
  257.3 1.8 copy-start.10
  259.1 18.9 %collective-permute-start.8 = (f32[8,32,256]{2,1,0:T(8,128)S(1)}, f32[8,32,256]{2,1,0:T(8,128)S(1)}, u32[]{:S(2)}, u32[]{:S(2)}) collective-permute-start(f32[8,32,256]{2,1,0:T(8,128)S(1)} %get-tuple-element.49), channel_id=1, source_target_pairs={{0,64},{32,96},{64,128},{96,160},{128,192},{160,224},{192,0},{224,... | collective-permute-start | bytes 786440 | tf_op jit(solution)/shard_map/ppermute | solution.py:312
  259.2 8.2 %copy-start.6 = (f32[8,32,256]{2,1,0:T(8,128)S(1)}, f32[8,32,256]{2,1,0:T(8,128)}, u32[]{:S(2)}) copy-start(f32[8,32,256]{2,1,0:T(8,128)} %copy-done.5) | copy-start | bytes 786436
  260.9 18.8 %collective-permute-start.7 = (f32[8,32,256]{2,1,0:T(8,128)S(1)}, f32[8,32,256]{2,1,0:T(8,128)S(1)}, u32[]{:S(2)}, u32[]{:S(2)}) collective-permute-start(f32[8,32,256]{2,1,0:T(8,128)S(1)} %get-tuple-element.48), channel_id=1, source_target_pairs={{0,192},{32,224},{64,0},{96,32},{128,64},{160,96},{192,128},{224,1... | collective-permute-start | bytes 786440 | tf_op jit(solution)/shard_map/ppermute | solution.py:312

commit v5 on v4

--- a/solution.py
+++ b/solution.py
@@ -67,7 +67,8 @@
     table[real, N:] = -im
     table[imag, :N] = im
     table[imag, N:] = re
-    return split_np(table)
+    high, low = split_np(table)
+    return np.concatenate([high, high, low], 0)
 
 
 def sine_coefficients():
@@ -175,37 +176,35 @@
 
 def y_inverse_kernel(idx_ref, in_ref, table_ref, *refs):
     outs, t_ref = refs[:NREF], refs[NREF]
-    r = idx_ref[0]
-
-    def step(x, carry):
-        t_ref[...] = left_multiply(table_ref[...], in_ref[:, x].reshape(N, 2 * KC))
-        for s in range(NREF):
-            start = pl.multiple_of(partner(r, s, 1) * 32, 32)
-            outs[s][x] = t_ref[pl.ds(start, 32), :]
-        return carry
-
-    lax.fori_loop(0, XL, step, 0)
+    t_ref[...] = left_multiply(table_ref[...], in_ref[:, 0].reshape(N, 2 * KC))
+    for s in range(NREF):
+        start = pl.multiple_of(partner(idx_ref[0], s, 1) * 32, 32)
+        outs[s][0] = t_ref[pl.ds(start, 32), :]
 
 
 def gradient_kernel(shift_by, idx_ref, miller_ref, rho_ref, shift_ref, support_ref, *refs):
-    ins, high_ref, low_ref = refs[:CH], refs[CH], refs[CH + 1]
-    sums = refs[CH + 2 : -3]
-    rho_out, shift_out, back_ref = refs[-3:]
+    ins, table_ref, sums = refs[:CH], refs[CH], refs[CH + 1 : -2]
+    rho_out, shift_out = refs[-2:]
     g = partner(idx_ref[0], shift_by, -1)
     h, k, l = (miller_ref[c, g].astype(F32) for c in range(3))
-    high, low = split(jnp.concatenate([ref[...].reshape(N, 2 * KC) for ref in ins], 1))
-    dot = functools.partial(jnp.dot, preferred_element_type=F32)
-    back_ref[...] = dot(high, high_ref[...]) + dot(low, high_ref[...]) + dot(high, low_ref[...])
-
-    def step(x, carry):
-        at = pl.ds(pl.multiple_of(x * 32, 32), 32)
-        u = [shift_ref[c, x].astype(F32) for c in range(3)]
-        mask = support_ref[x].astype(F32) * (1.0 / NREF)
+    rows = pl.ds(pl.multiple_of(idx_ref[0] * 32, 32), 32)
+    half = XL // 2
+    backs = []
+    for first in (0, half):
+        packed = [ref[first : first + half].reshape(half * 32, 2 * KC) for ref in ins]
+        high, low = split(jnp.concatenate(packed, 1))
+        backs.append(
+            jnp.dot(jnp.concatenate([high, low, high], 1), table_ref[...], preferred_element_type=F32)
+        )
+    for x in range(XL):
+        back = backs[x // half][x % half * 32 : (x % half + 1) * 32]
+        u = [shift_ref[c, x, rows, :].astype(F32) for c in range(3)]
+        mask = support_ref[x, rows, :].astype(F32) * (1.0 / NREF)
         cosine, sine = cos_sin_turns(h * u[0] + k * u[1] + l * u[2])
-        real, imag = back_ref[at, :N], back_ref[at, N:]
+        real, imag = back[:, :N], back[:, N:]
         p = mask * (cosine * real + sine * imag)
         q = mask * (cosine * imag - sine * real)
-        twist = rho_ref[0, x].astype(F32) * q - rho_ref[1, x].astype(F32) * p
+        twist = rho_ref[0, x, rows, :].astype(F32) * q - rho_ref[1, x, rows, :].astype(F32) * p
         for out, old, n, value in (
             (rho_out, 0, 0, p),
             (rho_out, 0, 1, q),
@@ -214,9 +213,6 @@
             (shift_out, 1, 2, l * twist),
         ):
             out[n, x] = sums[old][n, x] + value if sums else value
-        return carry
-
-    lax.fori_loop(0, XL, step, 0)
 
 
 SMEM = pl.BlockSpec(memory_space=pltpu.SMEM)
@@ -275,7 +271,7 @@
     r = lax.axis_index("refl")
     idx = jnp.stack([r]).astype(jnp.int32)
     forward, inverse = jnp.asarray(left_table(False)), jnp.asarray(left_table(True))
-    high, low = (jnp.asarray(t) for t in right_inverse())
+    last_table = jnp.asarray(right_inverse())
     amp = amplitude.reshape(N * XL, N)
     millers = millers.T
 
@@ -295,14 +291,19 @@
     def y_inverse(c, part):
         return pl.pallas_call(
             y_inverse_kernel,
-            in_specs=[SMEM, VMEM, VMEM],
-            out_specs=[VMEM] * NREF,
+            grid=(XL,),
+            in_specs=[
+                SMEM,
+                pl.BlockSpec((SLABS, 1, XL, 2 * KC), lambda x: (0, x, 0, 0)),
+                pl.BlockSpec((2 * N, 3 * N), lambda x: (0, 0)),
+            ],
+            out_specs=[pl.BlockSpec((1, 32, 2 * KC), lambda x: (x, 0, 0))] * NREF,
             out_shape=[f32(XL, 32, 2 * KC)] * NREF,
             scratch_shapes=[pltpu.VMEM((N, 2 * KC), F32)],
             compiler_params=params(24),
             cost_estimate=cost(3.2e9, 12e6),
             name=f"y_inverse_{c}",
-        )(idx, part, inverse)
+        )(idx, in_hbm(part), inverse)
 
     def over_grid(part):
         return lax.all_to_all(part, "grid", 0, 0, tiled=True)
@@ -313,38 +314,23 @@
         return [parts[0]] + [moved[s] for s in range(1, NREF)]
 
     def gradient(s, parts, sums):
-        out_block = lambda n: pl.BlockSpec((n, XL, 32, N), lambda i, idx: (0, 0, 0, 0))
-        whole = lambda i, idx: (0, 0)
         return tuple(
             pl.pallas_call(
                 functools.partial(gradient_kernel, s),
-                grid_spec=pltpu.PrefetchScalarGridSpec(
-                    num_scalar_prefetch=1,
-                    grid=(1,),
-                    in_specs=[
-                        SMEM,
-                        pl.BlockSpec((2, XL, 32, N), lambda i, idx: (0, 0, idx[0], 0)),
-                        pl.BlockSpec((3, XL, 32, N), lambda i, idx: (0, 0, idx[0], 0)),
-                        pl.BlockSpec((XL, 32, N), lambda i, idx: (0, idx[0], 0)),
-                    ]
-                    + [pl.BlockSpec((XL, 32, 2 * KC), lambda i, idx: (0, 0, 0))] * CH
-                    + [pl.BlockSpec((2 * N, 2 * N), whole)] * 2
-                    + ([out_block(2), out_block(3)] if sums else []),
-                    out_specs=[out_block(2), out_block(3)],
-                    scratch_shapes=[pltpu.VMEM((N, 2 * N), F32)],
-                ),
+                in_specs=[SMEM, SMEM] + [VMEM] * (3 + CH + 1 + len(sums)),
+                out_specs=[VMEM] * 2,
                 out_shape=[f32(2, XL, 32, N), f32(3, XL, 32, N)],
-                compiler_params=params(24),
+                compiler_params=params(16),
                 cost_estimate=cost(0.8e9, 5e6),
                 name=f"gradient_{s}",
-            )(idx, millers, density, displacement, support, *parts, high, low, *sums)
+            )(idx, millers, density, displacement, support, *parts, last_table, *sums)
         )
 
     f0 = over_grid(head(0, millers, density, displacement, support))
     f1 = over_grid(after(head(1, millers, density, displacement, support), f0))
     b0 = over_grid(after(x_both(0, f0), f1))
     b1 = over_grid(after(x_both(1, f1), b0))
-    r0 = over_refl(y_inverse(0, in_hbm(b0)))
+    r0 = over_refl(y_inverse(0, b0))
     r1 = over_refl(y_inverse(1, after(b1, *r0)))
     sums = ()
     for s in (0,) + R_ORDER:

time: 286 us -> 289 us (1.010)
  local copies, waits for them, and re-layouts: 5.55 us -> 2.29 us
  Pallas kernels: 68.9 us -> 72 us
    unnamed x34 -> x18, local copies, waits for them, and re-layouts: 5.55 us -> 2.29 us
    pallas_call x10, Pallas kernels: 22.9 us -> 25.9 us  [the longest x8 13.1 us: gradient(): pl.pallas_call(functools.partial(gradient_kernel, s), in_specs=[SMEM, SME...]
where the time goes in v5:
time: 289 us; the launch traced here: 284 us
  waiting for transfers between devices  136 us (47%)
  starting transfers between devices  73.7 us (26%)
  Pallas kernels  72 us (25%)
    all_to_all x4, waiting for transfers between devices, over_grid(): return lax.all_to_all(part, 'grid', 0, 0, tiled=True)  113 us
    ppermute x14, starting transfers between devices, over_refl(): moved = {s: lax.ppermute(parts[s], 'refl', ring(s)) for s in R_ORDER}  49.3 us
    all_to_all x4, starting transfers between devices, over_grid(): return lax.all_to_all(part, 'grid', 0, 0, tiled=True)  24.3 us
    pallas_call x2, Pallas kernels, x_both(): pl.pallas_call(x_kernel, grid=(1,), in_specs=[HBM, pl.BlockSpec((N * XL,...  24.3 us
    ppermute x14, waiting for transfers between devices, over_refl(): moved = {s: lax.ppermute(parts[s], 'refl', ring(s)) for s in R_ORDER}  22.2 us
    pallas_call x2, Pallas kernels, head(): pl.pallas_call(head_kernel, grid=(XL + 2,), in_specs=[SMEM, pl.BlockSpec(...  21.8 us
    pallas_call x8, Pallas kernels, gradient(): pl.pallas_call(functools.partial(gradient_kernel, s), in_specs=[SMEM, SME...  13.1 us
    pallas_call x2, Pallas kernels, y_inverse(): pl.pallas_call(y_inverse_kernel, grid=(XL,), in_specs=[SMEM, pl.BlockSpec...  12.7 us
  transfers between devices with their start and end apart: 18, of which 6 were waited for; matrix products, arithmetic and copies ran while one was open for 0% of the time, Pallas kernels for 18%

profile of v5, /device:TPU:8, one launch (start us, length us, event | category | flops | bytes accessed | tf_op | source)
XLA Modules:
  0.0 284.4 jit_solution(17814994129850411234)
XLA Ops:
  0.6 10.9 %head_0.1 = f32[32,8,8,256]{3,2,1,0:T(8,128)} custom-call(s32[3,8]{1,0:T(4,128)} %bitcast.7, bf16[2,8,256,256]{3,2,1,0:T(8,128)(2,1)} %rho_ref.19, bf16[3,8,256,256]{3,2,1,0:T(8,128)(2,1)} %shift_ref.19, s32[8,256,256]{2,1,0:T(8,128)} %support_ref.19, bf16[1536,512]{1,0:T(8,128)(2,1)} %constant.17.clone.table_ref, ...), custom_call_target="tpu_custom_call" | custom-call | flops 6400000000 | bytes 16000000 | tf_op jit(solution)/shard_map/head_0/pallas_call | solution.py:250
  11.5 10.1 %all-to-all-start = ((f32[32,8,8,256]{3,2,1,0:T(8,128)}), f32[32,8,8,256]{3,2,1,0:T(8,128)}, u32[]{:S(2)}, u32[]{:S(2)}) async-start(f32[32,8,8,256]{3,2,1,0:T(8,128)} %head_0.1), calls=%async_computation | async-start | bytes 4194304 | tf_op jit(solution)/shard_map/all_to_all | solution.py:309
  21.7 10.9 %head_1.1 = f32[32,8,8,256]{3,2,1,0:T(8,128)} custom-call(s32[3,8]{1,0:T(4,128)} %bitcast.8, bf16[2,8,256,256]{3,2,1,0:T(8,128)(2,1)} %rho_ref.19, bf16[3,8,256,256]{3,2,1,0:T(8,128)(2,1)} %shift_ref.19, s32[8,256,256]{2,1,0:T(8,128)} %support_ref.19, bf16[1536,512]{1,0:T(8,128)(2,1)} %constant.17.clone.table_ref, ...), custom_call_target="tpu_custom_call" | custom-call | flops 6400000000 | bytes 16000000 | tf_op jit(solution)/shard_map/head_1/pallas_call | solution.py:250
  32.6 0.0 copy-start.5
  32.6 39.4 %all-to-all-done = f32[32,8,8,256]{3,2,1,0:T(8,128)} async-done(((f32[32,8,8,256]{3,2,1,0:T(8,128)}), f32[32,8,8,256]{3,2,1,0:T(8,128)}, u32[]{:S(2)}, u32[]{:S(2)}) %all-to-all-start) | async-done | bytes 2097184 | tf_op jit(solution)/shard_map/all_to_all | solution.py:309
  72.0 4.7 %all-to-all-start.1 = ((f32[32,8,8,256]{3,2,1,0:T(8,128)}), f32[32,8,8,256]{3,2,1,0:T(8,128)}, u32[]{:S(2)}, u32[]{:S(2)}) async-start(f32[32,8,8,256]{3,2,1,0:T(8,128)} %head_1.1), calls=%async_computation.1 | async-start | bytes 4194304 | tf_op jit(solution)/shard_map/all_to_all | solution.py:309
  76.7 0.0 copy-done.5
  76.7 0.0 copy-done.6
  76.7 0.0 copy-start.7
  76.7 1.1 copy-done.7
  77.9 12.1 %x_0.1 = f32[2048,256]{1,0:T(8,128)} custom-call(f32[2048,256]{1,0:T(8,128)} %bitcast.2.in_ref, f32[2048,256]{1,0:T(8,128)S(1)} %bitcast.17, bf16[512,768]{1,0:T(8,128)(2,1)S(1)} %copy-done.7, bf16[512,768]{1,0:T(8,128)(2,1)S(1)} %copy-done.6), custom_call_target="tpu_custom_call" | custom-call | flops 6400000000 | bytes 24000000 | tf_op jit(solution)/shard_map/x_0/pallas_call | solution.py:279
  90.0 37.0 %all-to-all-done.1 = f32[32,8,8,256]{3,2,1,0:T(8,128)} async-done(((f32[32,8,8,256]{3,2,1,0:T(8,128)}), f32[32,8,8,256]{3,2,1,0:T(8,128)}, u32[]{:S(2)}, u32[]{:S(2)}) %all-to-all-start.1) | async-done | bytes 2097184 | tf_op jit(solution)/shard_map/all_to_all | solution.py:309
  127.0 4.7 %all-to-all-start.2 = ((f32[32,8,8,256]{3,2,1,0:T(8,128)}), f32[32,8,8,256]{3,2,1,0:T(8,128)}, u32[]{:S(2)}, u32[]{:S(2)}) async-start(f32[32,8,8,256]{3,2,1,0:T(8,128)} %bitcast.20), calls=%async_computation.2 | async-start | bytes 4194304 | tf_op jit(solution)/shard_map/all_to_all | solution.py:309
  131.7 0.0 copy-start.8
  131.8 1.1 copy-done.8
  132.9 12.1 %x_1.1 = f32[2048,256]{1,0:T(8,128)} custom-call(f32[2048,256]{1,0:T(8,128)} %bitcast.5.in_ref, f32[2048,256]{1,0:T(8,128)S(1)} %bitcast.18, bf16[512,768]{1,0:T(8,128)(2,1)S(1)} %copy-done.8, bf16[512,768]{1,0:T(8,128)(2,1)S(1)} %copy-done.6), custom_call_target="tpu_custom_call" | custom-call | flops 6400000000 | bytes 24000000 | tf_op jit(solution)/shard_map/x_1/pallas_call | solution.py:279
  145.0 37.0 %all-to-all-done.2.in_ref = f32[32,8,8,256]{3,2,1,0:T(8,128)} async-done(((f32[32,8,8,256]{3,2,1,0:T(8,128)}), f32[32,8,8,256]{3,2,1,0:T(8,128)}, u32[]{:S(2)}, u32[]{:S(2)}) %all-to-all-start.2) | async-done | bytes 2097184 | tf_op jit(solution)/shard_map/all_to_all | solution.py:309
  182.0 4.7 %all-to-all-start.3 = ((f32[32,8,8,256]{3,2,1,0:T(8,128)}), f32[32,8,8,256]{3,2,1,0:T(8,128)}, u32[]{:S(2)}, u32[]{:S(2)}) async-start(f32[32,8,8,256]{3,2,1,0:T(8,128)} %bitcast.19), calls=%async_computation.3 | async-start | bytes 4194304 | tf_op jit(solution)/shard_map/all_to_all | solution.py:309
  186.8 5.9 %y_inverse_0.1 = (f32[8,32,256]{2,1,0:T(8,128)S(1)}, f32[8,32,256]{2,1,0:T(8,128)S(1)}, f32[8,32,256]{2,1,0:T(8,128)S(1)}, f32[8,32,256]{2,1,0:T(8,128)S(1)}, f3...) custom-call(s32[1]{0:T(128)} %bitcast.idx_ref, ...), custom_call_target="tpu_custom_call" | custom-call | flops 3200000000 | bytes 12000000 | tf_op jit(solution)/shard_map/y_inverse_0/pallas_call | solution.py:292
  192.7 2.8 collective-permute-start
  195.5 2.3 collective-permute-start.1
  197.9 0.0 collective-permute-start.2
  197.9 1.4 collective-permute-start.3
  199.3 3.9 %collective-permute-start.4 = (f32[8,32,256]{2,1,0:T(8,128)S(1)}, f32[8,32,256]{2,1,0:T(8,128)S(1)}, u32[]{:S(2)}, u32[]{:S(2)}) collective-permute-start(f32[8,32,256]{2,1,0:T(8,128)S(1)} %get-tuple-element.44), channel_id=1, source_target_pairs={{0,128},{32,160},{64,192},{96,224},{128,0},{160,32},{192,64},{224,... | collective-permute-start | bytes 786440 | tf_op jit(solution)/shard_map/ppermute | solution.py:313
  203.2 0.0 collective-permute-done.refs_0_
  203.2 2.7 collective-permute-start.5
  205.9 13.2 %collective-permute-done.1.refs_0_ = f32[8,32,256]{2,1,0:T(8,128)S(1)} collective-permute-done((f32[8,32,256]{2,1,0:T(8,128)S(1)}, f32[8,32,256]{2,1,0:T(8,128)S(1)}, u32[]{:S(2)}, u32[]{:S(2)}) %collective-permute-start.1) | collective-permute-done | bytes 262176 | tf_op jit(solution)/shard_map/ppermute | solution.py:313
  219.1 16.3 %collective-permute-start.6 = (f32[8,32,256]{2,1,0:T(8,128)S(1)}, f32[8,32,256]{2,1,0:T(8,128)S(1)}, u32[]{:S(2)}, u32[]{:S(2)}) collective-permute-start(f32[8,32,256]{2,1,0:T(8,128)S(1)} %get-tuple-element.46), channel_id=1, source_target_pairs={{0,224},{32,192},{64,32},{96,0},{128,96},{160,64},{192,160},{224,1... | collective-permute-start | bytes 786440 | tf_op jit(solution)/shard_map/ppermute | solution.py:313
  235.5 0.0 collective-permute-done.2.refs_0_
  235.5 0.0 collective-permute-done.3.refs_0_
  235.5 0.0 collective-permute-done.4.refs_0_
  235.5 0.0 collective-permute-done.5.refs_0_
  235.5 5.4 %collective-permute-done.6.refs_0_ = f32[8,32,256]{2,1,0:T(8,128)S(1)} collective-permute-done((f32[8,32,256]{2,1,0:T(8,128)S(1)}, f32[8,32,256]{2,1,0:T(8,128)S(1)}, u32[]{:S(2)}, u32[]{:S(2)}) %collective-permute-start.6) | collective-permute-done | bytes 262176 | tf_op jit(solution)/shard_map/ppermute | solution.py:313
  240.9 0.0 all-to-all-done.3.in_ref
  240.9 0.0 copy-start.3
  240.9 0.0 copy-start.4
  240.9 6.8 %y_inverse_1.1 = (f32[8,32,256]{2,1,0:T(8,128)S(1)}, f32[8,32,256]{2,1,0:T(8,128)S(1)}, f32[8,32,256]{2,1,0:T(8,128)S(1)}, f32[8,32,256]{2,1,0:T(8,128)S(1)}, f3...) custom-call(s32[1]{0:T(128)} %bitcast.idx_ref, ...), custom_call_target="tpu_custom_call" | custom-call | flops 3200000000 | bytes 12000000 | tf_op jit(solution)/shard_map/y_inverse_1/pallas_call | solution.py:292
  247.8 3.3 %collective-permute-start.13 = (f32[8,32,256]{2,1,0:T(8,128)S(1)}, f32[8,32,256]{2,1,0:T(8,128)S(1)}, u32[]{:S(2)}, u32[]{:S(2)}) collective-permute-start(f32[8,32,256]{2,1,0:T(8,128)S(1)} %get-tuple-element.54), channel_id=1, source_target_pairs={{0,160},{32,128},{64,224},{96,192},{128,32},{160,0},{192,96},{224,... | collective-permute-start | bytes 786440 | tf_op jit(solution)/shard_map/ppermute | solution.py:313
  251.1 0.2 collective-permute-start.12
  251.3 3.0 %collective-permute-start.11 = (f32[8,32,256]{2,1,0:T(8,128)S(1)}, f32[8,32,256]{2,1,0:T(8,128)S(1)}, u32[]{:S(2)}, u32[]{:S(2)}) collective-permute-start(f32[8,32,256]{2,1,0:T(8,128)S(1)} %get-tuple-element.52), channel_id=1, source_target_pairs={{0,32},{32,0},{64,96},{96,64},{128,160},{160,128},{192,224},{224,1... | collective-permute-start | bytes 786440 | tf_op jit(solution)/shard_map/ppermute | solution.py:313
  254.4 3.4 %collective-permute-start.10 = (f32[8,32,256]{2,1,0:T(8,128)S(1)}, f32[8,32,256]{2,1,0:T(8,128)S(1)}, u32[]{:S(2)}, u32[]{:S(2)}) collective-permute-start(f32[8,32,256]{2,1,0:T(8,128)S(1)} %get-tuple-element.51), channel_id=1, source_target_pairs={{0,96},{32,64},{64,160},{96,128},{128,224},{160,192},{192,32},{224... | collective-permute-start | bytes 786440 | tf_op jit(solution)/shard_map/ppermute | solution.py:313
  257.8 2.7 collective-permute-start.9
  260.5 0.0 copy-done
  260.5 0.0 copy-done.1
  260.5 0.0 copy-done.2
  260.5 0.0 copy-done.3
  260.5 0.0 copy-done.4
  260.5 1.5 gradient_0.1
  262.0 0.0 collective-permute-done.13.refs_1_
  262.0 0.2 collective-permute-start.8
  262.2 1.5 gradient_5.1
  263.7 0.0 collective-permute-done.12.refs_1_
  263.7 6.9 %collective-permute-start.7 = (f32[8,32,256]{2,1,0:T(8,128)S(1)}, f32[8,32,256]{2,1,0:T(8,128)S(1)}, u32[]{:S(2)}, u32[]{:S(2)}) collective-permute-start(f32[8,32,256]{2,1,0:T(8,128)S(1)} %get-tuple-element.48), channel_id=1, source_target_pairs={{0,192},{32,224},{64,0},{96,32},{128,64},{160,96},{192,128},{224,1... | collective-permute-start | bytes 786440 | tf_op jit(solution)/shard_map/ppermute | solution.py:313
  270.6 1.5 gradient_4.1
  272.1 3.5 %collective-permute-done.11.refs_1_ = f32[8,32,256]{2,1,0:T(8,128)S(1)} collective-permute-done((f32[8,32,256]{2,1,0:T(8,128)S(1)}, f32[8,32,256]{2,1,0:T(8,128)S(1)}, u32[]{:S(2)}, u32[]{:S(2)}) %collective-permute-start.11) | collective-permute-done | bytes 262176 | tf_op jit(solution)/shard_map/ppermute | solution.py:313
  275.7 1.5 gradient_1.1
  277.2 0.0 collective-permute-done.10.refs_1_
  277.2 1.5 gradient_3.1
  278.7 0.0 collective-permute-done.9.refs_1_
  278.7 1.5 gradient_7.1
  280.3 0.0 collective-permute-done.8.refs_1_
  280.3 1.5 gradient_2.1
  281.8 0.0 collective-permute-done.7.refs_1_
  281.8 2.6 gradient_6.1
  (4 shorter events, 0.0 us)
Async XLA Ops:
  11.5 60.4 %all-to-all-start = ((f32[32,8,8,256]{3,2,1,0:T(8,128)}), f32[32,8,8,256]{3,2,1,0:T(8,128)}, u32[]{:S(2)}, u32[]{:S(2)}) async-start(f32[32,8,8,256]{3,2,1,0:T(8,128)} %head_0.1), calls=%async_computation | async-start | bytes 4194304 | tf_op jit(solution)/shard_map/all_to_all | solution.py:309
  32.6 44.1 %copy-start.5 = (f32[1,256,8,256]{3,2,1,0:T(8,128)S(1)}, f32[1,256,8,256]{3,2,1,0:T(8,128)}, u32[]{:S(2)}) copy-start(f32[1,256,8,256]{3,2,1,0:T(8,128)} %param.16) | copy-start | bytes 6291460
  32.6 44.1 %copy-start.6 = (bf16[512,768]{1,0:T(8,128)(2,1)S(1)}, bf16[512,768]{1,0:T(8,128)(2,1)}, u32[]{:S(2)}) copy-start(bf16[512,768]{1,0:T(8,128)(2,1)} %constant.15.clone.inverse_ref.table_ref) | copy-start | bytes 2359300
  72.0 55.0 %all-to-all-start.1 = ((f32[32,8,8,256]{3,2,1,0:T(8,128)}), f32[32,8,8,256]{3,2,1,0:T(8,128)}, u32[]{:S(2)}, u32[]{:S(2)}) async-start(f32[32,8,8,256]{3,2,1,0:T(8,128)} %head_1.1), calls=%async_computation.1 | async-start | bytes 4194304 | tf_op jit(solution)/shard_map/all_to_all | solution.py:309
  76.7 1.1 copy-start.7
  127.0 55.0 %all-to-all-start.2 = ((f32[32,8,8,256]{3,2,1,0:T(8,128)}), f32[32,8,8,256]{3,2,1,0:T(8,128)}, u32[]{:S(2)}, u32[]{:S(2)}) async-start(f32[32,8,8,256]{3,2,1,0:T(8,128)} %bitcast.20), calls=%async_computation.2 | async-start | bytes 4194304 | tf_op jit(solution)/shard_map/all_to_all | solution.py:309
  131.7 1.1 copy-start.8
  182.0 58.9 %all-to-all-start.3 = ((f32[32,8,8,256]{3,2,1,0:T(8,128)}), f32[32,8,8,256]{3,2,1,0:T(8,128)}, u32[]{:S(2)}, u32[]{:S(2)}) async-start(f32[32,8,8,256]{3,2,1,0:T(8,128)} %bitcast.19), calls=%async_computation.3 | async-start | bytes 4194304 | tf_op jit(solution)/shard_map/all_to_all | solution.py:309
  192.7 10.5 %collective-permute-start = (f32[8,32,256]{2,1,0:T(8,128)S(1)}, f32[8,32,256]{2,1,0:T(8,128)S(1)}, u32[]{:S(2)}, u32[]{:S(2)}) collective-permute-start(f32[8,32,256]{2,1,0:T(8,128)S(1)} %get-tuple-element.38), channel_id=1, source_target_pairs={{0,192},{32,224},{64,0},{96,32},{128,64},{160,96},{192,128},{224,1... | collective-permute-start | bytes 786440 | tf_op jit(solution)/shard_map/ppermute | solution.py:313
  195.5 23.6 %collective-permute-start.1 = (f32[8,32,256]{2,1,0:T(8,128)S(1)}, f32[8,32,256]{2,1,0:T(8,128)S(1)}, u32[]{:S(2)}, u32[]{:S(2)}) collective-permute-start(f32[8,32,256]{2,1,0:T(8,128)S(1)} %get-tuple-element.41), channel_id=1, source_target_pairs={{0,32},{32,0},{64,96},{96,64},{128,160},{160,128},{192,224},{224,1... | collective-permute-start | bytes 786440 | tf_op jit(solution)/shard_map/ppermute | solution.py:313
  197.9 37.6 %collective-permute-start.2 = (f32[8,32,256]{2,1,0:T(8,128)S(1)}, f32[8,32,256]{2,1,0:T(8,128)S(1)}, u32[]{:S(2)}, u32[]{:S(2)}) collective-permute-start(f32[8,32,256]{2,1,0:T(8,128)S(1)} %get-tuple-element.42), channel_id=1, source_target_pairs={{0,64},{32,96},{64,128},{96,160},{128,192},{160,224},{192,0},{224,... | collective-permute-start | bytes 786440 | tf_op jit(solution)/shard_map/ppermute | solution.py:313
  197.9 37.6 %collective-permute-start.3 = (f32[8,32,256]{2,1,0:T(8,128)S(1)}, f32[8,32,256]{2,1,0:T(8,128)S(1)}, u32[]{:S(2)}, u32[]{:S(2)}) collective-permute-start(f32[8,32,256]{2,1,0:T(8,128)S(1)} %get-tuple-element.43), channel_id=1, source_target_pairs={{0,96},{32,64},{64,160},{96,128},{128,224},{160,192},{192,32},{224... | collective-permute-start | bytes 786440 | tf_op jit(solution)/shard_map/ppermute | solution.py:313
  199.3 36.2 %collective-permute-start.4 = (f32[8,32,256]{2,1,0:T(8,128)S(1)}, f32[8,32,256]{2,1,0:T(8,128)S(1)}, u32[]{:S(2)}, u32[]{:S(2)}) collective-permute-start(f32[8,32,256]{2,1,0:T(8,128)S(1)} %get-tuple-element.44), channel_id=1, source_target_pairs={{0,128},{32,160},{64,192},{96,224},{128,0},{160,32},{192,64},{224,... | collective-permute-start | bytes 786440 | tf_op jit(solution)/shard_map/ppermute | solution.py:313
  203.2 32.3 %collective-permute-start.5 = (f32[8,32,256]{2,1,0:T(8,128)S(1)}, f32[8,32,256]{2,1,0:T(8,128)S(1)}, u32[]{:S(2)}, u32[]{:S(2)}) collective-permute-start(f32[8,32,256]{2,1,0:T(8,128)S(1)} %get-tuple-element.45), channel_id=1, source_target_pairs={{0,160},{32,128},{64,224},{96,192},{128,32},{160,0},{192,96},{224,... | collective-permute-start | bytes 786440 | tf_op jit(solution)/shard_map/ppermute | solution.py:313
  219.1 21.8 %collective-permute-start.6 = (f32[8,32,256]{2,1,0:T(8,128)S(1)}, f32[8,32,256]{2,1,0:T(8,128)S(1)}, u32[]{:S(2)}, u32[]{:S(2)}) collective-permute-start(f32[8,32,256]{2,1,0:T(8,128)S(1)} %get-tuple-element.46), channel_id=1, source_target_pairs={{0,224},{32,192},{64,32},{96,0},{128,96},{160,64},{192,160},{224,1... | collective-permute-start | bytes 786440 | tf_op jit(solution)/shard_map/ppermute | solution.py:313
  240.9 19.6 %copy-start = (bf16[3,8,256,256]{3,2,1,0:T(8,128)(2,1)S(1)}, bf16[3,8,256,256]{3,2,1,0:T(8,128)(2,1)}, u32[]{:S(2)}) copy-start(bf16[3,8,256,256]{3,2,1,0:T(8,128)(2,1)} %shift_ref.19) | copy-start | bytes 9437188
  240.9 19.6 %copy-start.1 = (bf16[2,8,256,256]{3,2,1,0:T(8,128)(2,1)S(1)}, bf16[2,8,256,256]{3,2,1,0:T(8,128)(2,1)}, u32[]{:S(2)}) copy-start(bf16[2,8,256,256]{3,2,1,0:T(8,128)(2,1)} %rho_ref.19) | copy-start | bytes 6291460
  240.9 19.6 %copy-start.2 = (s32[8,256,256]{2,1,0:T(8,128)S(1)}, s32[8,256,256]{2,1,0:T(8,128)}, u32[]{:S(2)}) copy-start(s32[8,256,256]{2,1,0:T(8,128)} %support_ref.19) | copy-start | bytes 6291460
  240.9 19.6 %copy-start.3 = (bf16[1536,512]{1,0:T(8,128)(2,1)S(1)}, bf16[1536,512]{1,0:T(8,128)(2,1)}, u32[]{:S(2)}) copy-start(bf16[1536,512]{1,0:T(8,128)(2,1)} %constant.16.clone.refs_2_) | copy-start | bytes 4718596
  240.9 19.6 %copy-start.4 = (s32[8,3]{0,1:T(4,128)S(1)}, s32[8,3]{0,1:T(4,128)}, u32[]{:S(2)}) copy-start(s32[8,3]{0,1:T(4,128)} %param.15) | copy-start | bytes 292
  247.8 14.2 %collective-permute-start.13 = (f32[8,32,256]{2,1,0:T(8,128)S(1)}, f32[8,32,256]{2,1,0:T(8,128)S(1)}, u32[]{:S(2)}, u32[]{:S(2)}) collective-permute-start(f32[8,32,256]{2,1,0:T(8,128)S(1)} %get-tuple-element.54), channel_id=1, source_target_pairs={{0,160},{32,128},{64,224},{96,192},{128,32},{160,0},{192,96},{224,... | collective-permute-start | bytes 786440 | tf_op jit(solution)/shard_map/ppermute | solution.py:313
  251.1 12.6 %collective-permute-start.12 = (f32[8,32,256]{2,1,0:T(8,128)S(1)}, f32[8,32,256]{2,1,0:T(8,128)S(1)}, u32[]{:S(2)}, u32[]{:S(2)}) collective-permute-start(f32[8,32,256]{2,1,0:T(8,128)S(1)} %get-tuple-element.53), channel_id=1, source_target_pairs={{0,128},{32,160},{64,192},{96,224},{128,0},{160,32},{192,64},{224,... | collective-permute-start | bytes 786440 | tf_op jit(solution)/shard_map/ppermute | solution.py:313
  251.3 24.3 %collective-permute-start.11 = (f32[8,32,256]{2,1,0:T(8,128)S(1)}, f32[8,32,256]{2,1,0:T(8,128)S(1)}, u32[]{:S(2)}, u32[]{:S(2)}) collective-permute-start(f32[8,32,256]{2,1,0:T(8,128)S(1)} %get-tuple-element.52), channel_id=1, source_target_pairs={{0,32},{32,0},{64,96},{96,64},{128,160},{160,128},{192,224},{224,1... | collective-permute-start | bytes 786440 | tf_op jit(solution)/shard_map/ppermute | solution.py:313
  254.4 22.8 %collective-permute-start.10 = (f32[8,32,256]{2,1,0:T(8,128)S(1)}, f32[8,32,256]{2,1,0:T(8,128)S(1)}, u32[]{:S(2)}, u32[]{:S(2)}) collective-permute-start(f32[8,32,256]{2,1,0:T(8,128)S(1)} %get-tuple-element.51), channel_id=1, source_target_pairs={{0,96},{32,64},{64,160},{96,128},{128,224},{160,192},{192,32},{224... | collective-permute-start | bytes 786440 | tf_op jit(solution)/shard_map/ppermute | solution.py:313
  257.8 20.9 %collective-permute-start.9 = (f32[8,32,256]{2,1,0:T(8,128)S(1)}, f32[8,32,256]{2,1,0:T(8,128)S(1)}, u32[]{:S(2)}, u32[]{:S(2)}) collective-permute-start(f32[8,32,256]{2,1,0:T(8,128)S(1)} %get-tuple-element.50), channel_id=1, source_target_pairs={{0,224},{32,192},{64,32},{96,0},{128,96},{160,64},{192,160},{224,1... | collective-permute-start | bytes 786440 | tf_op jit(solution)/shard_map/ppermute | solution.py:313
  262.0 18.3 %collective-permute-start.8 = (f32[8,32,256]{2,1,0:T(8,128)S(1)}, f32[8,32,256]{2,1,0:T(8,128)S(1)}, u32[]{:S(2)}, u32[]{:S(2)}) collective-permute-start(f32[8,32,256]{2,1,0:T(8,128)S(1)} %get-tuple-element.49), channel_id=1, source_target_pairs={{0,64},{32,96},{64,128},{96,160},{128,192},{160,224},{192,0},{224,... | collective-permute-start | bytes 786440 | tf_op jit(solution)/shard_map/ppermute | solution.py:313
  263.7 18.1 %collective-permute-start.7 = (f32[8,32,256]{2,1,0:T(8,128)S(1)}, f32[8,32,256]{2,1,0:T(8,128)S(1)}, u32[]{:S(2)}, u32[]{:S(2)}) collective-permute-start(f32[8,32,256]{2,1,0:T(8,128)S(1)} %get-tuple-element.48), channel_id=1, source_target_pairs={{0,192},{32,224},{64,0},{96,32},{128,64},{160,96},{192,128},{224,1... | collective-permute-start | bytes 786440 | tf_op jit(solution)/shard_map/ppermute | solution.py:313

commit v6 on v5

--- a/solution.py
+++ b/solution.py
@@ -17,7 +17,7 @@
 XL = 8
 NREF = 8
 HEAD_ROWS = 32
-R_ORDER = (5, 4, 1, 3, 7, 2, 6)
+R_ORDER = (4, 5, 3, 2, 7, 6, 1)
 BF = jnp.bfloat16
 F32 = jnp.float32
 
@@ -176,10 +176,16 @@
 
 def y_inverse_kernel(idx_ref, in_ref, table_ref, *refs):
     outs, t_ref = refs[:NREF], refs[NREF]
-    t_ref[...] = left_multiply(table_ref[...], in_ref[:, 0].reshape(N, 2 * KC))
-    for s in range(NREF):
-        start = pl.multiple_of(partner(idx_ref[0], s, 1) * 32, 32)
-        outs[s][0] = t_ref[pl.ds(start, 32), :]
+    r = idx_ref[0]
+
+    def step(x, carry):
+        t_ref[...] = left_multiply(table_ref[...], in_ref[:, x].reshape(N, 2 * KC))
+        for s in range(NREF):
+            start = pl.multiple_of(partner(r, s, 1) * 32, 32)
+            outs[s][x] = t_ref[pl.ds(start, 32), :]
+        return carry
+
+    lax.fori_loop(0, XL, step, 0)
 
 
 def gradient_kernel(shift_by, idx_ref, miller_ref, rho_ref, shift_ref, support_ref, *refs):
@@ -291,26 +297,21 @@
     def y_inverse(c, part):
         return pl.pallas_call(
             y_inverse_kernel,
-            grid=(XL,),
-            in_specs=[
-                SMEM,
-                pl.BlockSpec((SLABS, 1, XL, 2 * KC), lambda x: (0, x, 0, 0)),
-                pl.BlockSpec((2 * N, 3 * N), lambda x: (0, 0)),
-            ],
-            out_specs=[pl.BlockSpec((1, 32, 2 * KC), lambda x: (x, 0, 0))] * NREF,
+            in_specs=[SMEM, VMEM, VMEM],
+            out_specs=[VMEM] * NREF,
             out_shape=[f32(XL, 32, 2 * KC)] * NREF,
             scratch_shapes=[pltpu.VMEM((N, 2 * KC), F32)],
             compiler_params=params(24),
             cost_estimate=cost(3.2e9, 12e6),
             name=f"y_inverse_{c}",
-        )(idx, in_hbm(part), inverse)
+        )(idx, part, in_hbm(inverse))
 
     def over_grid(part):
         return lax.all_to_all(part, "grid", 0, 0, tiled=True)
 
-    def over_refl(parts):
+    def over_refl(parts, order):
         ring = lambda s: [(i, (i // 2 + s // 2) % (NREF // 2) * 2 + (i + s) % 2) for i in range(NREF)]
-        moved = {s: lax.ppermute(parts[s], "refl", ring(s)) for s in R_ORDER}
+        moved = {s: lax.ppermute(parts[s], "refl", ring(s)) for s in order}
         return [parts[0]] + [moved[s] for s in range(1, NREF)]
 
     def gradient(s, parts, sums):
@@ -330,8 +331,8 @@
     f1 = over_grid(after(head(1, millers, density, displacement, support), f0))
     b0 = over_grid(after(x_both(0, f0), f1))
     b1 = over_grid(after(x_both(1, f1), b0))
-    r0 = over_refl(y_inverse(0, b0))
-    r1 = over_refl(y_inverse(1, after(b1, *r0)))
+    r0 = over_refl(y_inverse(0, in_hbm(b0)), (5, 4, 1, 3, 7, 2, 6))
+    r1 = over_refl(y_inverse(1, after(b1, *r0)), R_ORDER)
     sums = ()
     for s in (0,) + R_ORDER:
         sums = gradient(s, (r0[s], r1[s]), sums)

time: 289 us -> 288 us (level)
  waiting for transfers between devices: 136 us -> 142 us
  starting transfers between devices: 73.7 us -> 69.1 us
  Pallas kernels: 72 us -> 68.6 us
    ppermute x14, waiting for transfers between devices: 22.2 us -> 28.8 us  [over_refl(): moved = {s: lax.ppermute(parts[s], 'refl', ring(s)) for s in order}]
    ppermute x14, starting transfers between devices: 49.3 us -> 44.8 us  [over_refl(): moved = {s: lax.ppermute(parts[s], 'refl', ring(s)) for s in order}]
    pallas_call x2, Pallas kernels: 12.7 us -> 9.38 us  [y_inverse(): pl.pallas_call(y_inverse_kernel, in_specs=[SMEM, VMEM, VMEM], out_specs=[...]
  transfers between devices with their start and end apart: 18 -> 18, of which waited for: 6 -> 9; matrix products, arithmetic and copies ran while one was open for 0% -> 0% of each run, Pallas kernels for 18% -> 18%
where the time goes in v6:
time: 288 us; the launch traced here: 285 us
  waiting for transfers between devices  142 us (49%)
  starting transfers between devices  69.1 us (24%)
  Pallas kernels  68.6 us (24%)
  local copies, waits for them, and re-layouts  4.4 us (2%)
    all_to_all x4, waiting for transfers between devices, over_grid(): return lax.all_to_all(part, 'grid', 0, 0, tiled=True)  113 us
    ppermute x14, starting transfers between devices, over_refl(): moved = {s: lax.ppermute(parts[s], 'refl', ring(s)) for s in order}  44.8 us
    ppermute x14, waiting for transfers between devices, over_refl(): moved = {s: lax.ppermute(parts[s], 'refl', ring(s)) for s in order}  28.8 us
    all_to_all x4, starting transfers between devices, over_grid(): return lax.all_to_all(part, 'grid', 0, 0, tiled=True)  24.3 us
    pallas_call x2, Pallas kernels, x_both(): pl.pallas_call(x_kernel, grid=(1,), in_specs=[HBM, pl.BlockSpec((N * XL,...  24.2 us
    pallas_call x2, Pallas kernels, head(): pl.pallas_call(head_kernel, grid=(XL + 2,), in_specs=[SMEM, pl.BlockSpec(...  21.9 us
    pallas_call x8, Pallas kernels, gradient(): pl.pallas_call(functools.partial(gradient_kernel, s), in_specs=[SMEM, SME...  13.1 us
    pallas_call x2, Pallas kernels, y_inverse(): pl.pallas_call(y_inverse_kernel, in_specs=[SMEM, VMEM, VMEM], out_specs=[...  9.38 us
  transfers between devices with their start and end apart: 18, of which 9 were waited for; matrix products, arithmetic and copies ran while one was open for 0% of the time, Pallas kernels for 18%

profile of v6, /device:TPU:8, one launch (start us, length us, event | category | flops | bytes accessed | tf_op | source)
XLA Modules:
  0.0 285.2 jit_solution(8901311602744873844)
XLA Ops:
  0.6 10.9 %head_0.1 = f32[32,8,8,256]{3,2,1,0:T(8,128)} custom-call(s32[3,8]{1,0:T(4,128)} %bitcast.7, bf16[2,8,256,256]{3,2,1,0:T(8,128)(2,1)} %rho_ref.19, bf16[3,8,256,256]{3,2,1,0:T(8,128)(2,1)} %shift_ref.19, s32[8,256,256]{2,1,0:T(8,128)} %support_ref.19, bf16[1536,512]{1,0:T(8,128)(2,1)} %constant.17.clone.table_ref, ...), custom_call_target="tpu_custom_call" | custom-call | flops 6400000000 | bytes 16000000 | tf_op jit(solution)/shard_map/head_0/pallas_call | solution.py:256
  11.6 10.1 %all-to-all-start = ((f32[32,8,8,256]{3,2,1,0:T(8,128)}), f32[32,8,8,256]{3,2,1,0:T(8,128)}, u32[]{:S(2)}, u32[]{:S(2)}) async-start(f32[32,8,8,256]{3,2,1,0:T(8,128)} %head_0.1), calls=%async_computation | async-start | bytes 4194304 | tf_op jit(solution)/shard_map/all_to_all | solution.py:310
  21.7 10.9 %head_1.1 = f32[32,8,8,256]{3,2,1,0:T(8,128)} custom-call(s32[3,8]{1,0:T(4,128)} %bitcast.8, bf16[2,8,256,256]{3,2,1,0:T(8,128)(2,1)} %rho_ref.19, bf16[3,8,256,256]{3,2,1,0:T(8,128)(2,1)} %shift_ref.19, s32[8,256,256]{2,1,0:T(8,128)} %support_ref.19, bf16[1536,512]{1,0:T(8,128)(2,1)} %constant.17.clone.table_ref, ...), custom_call_target="tpu_custom_call" | custom-call | flops 6400000000 | bytes 16000000 | tf_op jit(solution)/shard_map/head_1/pallas_call | solution.py:256
  32.6 39.4 %all-to-all-done = f32[32,8,8,256]{3,2,1,0:T(8,128)} async-done(((f32[32,8,8,256]{3,2,1,0:T(8,128)}), f32[32,8,8,256]{3,2,1,0:T(8,128)}, u32[]{:S(2)}, u32[]{:S(2)}) %all-to-all-start) | async-done | bytes 2097184 | tf_op jit(solution)/shard_map/all_to_all | solution.py:310
  72.0 4.7 %all-to-all-start.1 = ((f32[32,8,8,256]{3,2,1,0:T(8,128)}), f32[32,8,8,256]{3,2,1,0:T(8,128)}, u32[]{:S(2)}, u32[]{:S(2)}) async-start(f32[32,8,8,256]{3,2,1,0:T(8,128)} %head_1.1), calls=%async_computation.1 | async-start | bytes 4194304 | tf_op jit(solution)/shard_map/all_to_all | solution.py:310
  76.7 0.0 copy-done.11
  76.7 0.0 copy-done.12
  76.8 0.0 copy-start.13
  76.8 1.1 copy-done.13
  77.9 12.1 %x_0.1 = f32[2048,256]{1,0:T(8,128)} custom-call(f32[2048,256]{1,0:T(8,128)} %bitcast.2.in_ref, f32[2048,256]{1,0:T(8,128)S(1)} %bitcast.17, bf16[512,768]{1,0:T(8,128)(2,1)S(1)} %copy-done.13, bf16[512,768]{1,0:T(8,128)(2,1)S(1)} %copy-done.12), custom_call_target="tpu_custom_call" | custom-call | flops 6400000000 | bytes 24000000 | tf_op jit(solution)/shard_map/x_0/pallas_call | solution.py:285
  90.0 37.0 %all-to-all-done.1 = f32[32,8,8,256]{3,2,1,0:T(8,128)} async-done(((f32[32,8,8,256]{3,2,1,0:T(8,128)}), f32[32,8,8,256]{3,2,1,0:T(8,128)}, u32[]{:S(2)}, u32[]{:S(2)}) %all-to-all-start.1) | async-done | bytes 2097184 | tf_op jit(solution)/shard_map/all_to_all | solution.py:310
  127.0 4.7 %all-to-all-start.2 = ((f32[32,8,8,256]{3,2,1,0:T(8,128)}), f32[32,8,8,256]{3,2,1,0:T(8,128)}, u32[]{:S(2)}, u32[]{:S(2)}) async-start(f32[32,8,8,256]{3,2,1,0:T(8,128)} %bitcast.20), calls=%async_computation.2 | async-start | bytes 4194304 | tf_op jit(solution)/shard_map/all_to_all | solution.py:310
  131.8 0.0 copy-start.14
  131.8 1.1 copy-done.14
  132.9 12.1 %x_1.1 = f32[2048,256]{1,0:T(8,128)} custom-call(f32[2048,256]{1,0:T(8,128)} %bitcast.5.in_ref, f32[2048,256]{1,0:T(8,128)S(1)} %bitcast.18, bf16[512,768]{1,0:T(8,128)(2,1)S(1)} %copy-done.14, bf16[512,768]{1,0:T(8,128)(2,1)S(1)} %copy-done.12), custom_call_target="tpu_custom_call" | custom-call | flops 6400000000 | bytes 24000000 | tf_op jit(solution)/shard_map/x_1/pallas_call | solution.py:285
  145.0 37.0 %all-to-all-done.2.in_ref = f32[32,8,8,256]{3,2,1,0:T(8,128)} async-done(((f32[32,8,8,256]{3,2,1,0:T(8,128)}), f32[32,8,8,256]{3,2,1,0:T(8,128)}, u32[]{:S(2)}, u32[]{:S(2)}) %all-to-all-start.2) | async-done | bytes 2097184 | tf_op jit(solution)/shard_map/all_to_all | solution.py:310
  182.1 4.7 %all-to-all-start.3 = ((f32[32,8,8,256]{3,2,1,0:T(8,128)}), f32[32,8,8,256]{3,2,1,0:T(8,128)S(1)}, u32[]{:S(2)}, u32[]{:S(2)}) async-start(f32[32,8,8,256]{3,2,1,0:T(8,128)} %bitcast.19), calls=%async_computation.3 | async-start | bytes 4194304 | tf_op jit(solution)/shard_map/all_to_all | solution.py:310
  186.8 4.9 %y_inverse_0.1 = (f32[8,32,256]{2,1,0:T(8,128)S(1)}, f32[8,32,256]{2,1,0:T(8,128)S(1)}, f32[8,32,256]{2,1,0:T(8,128)S(1)}, f32[8,32,256]{2,1,0:T(8,128)S(1)}, f3...) custom-call(s32[1]{0:T(128)} %bitcast.idx_ref, ...), custom_call_target="tpu_custom_call" | custom-call | flops 3200000000 | bytes 12000000 | tf_op jit(solution)/shard_map/y_inverse_0/pallas_call | solution.py:298
  191.7 0.7 copy-done.6
  192.4 2.3 collective-permute-start
  194.7 1.5 collective-permute-start.1
  196.2 2.1 collective-permute-start.2
  198.4 1.7 collective-permute-start.3
  200.1 3.6 %collective-permute-start.4 = (f32[8,32,256]{2,1,0:T(8,128)S(1)}, f32[8,32,256]{2,1,0:T(8,128)S(1)}, u32[]{:S(2)}, u32[]{:S(2)}) collective-permute-start(f32[8,32,256]{2,1,0:T(8,128)S(1)} %get-tuple-element.44), channel_id=1, source_target_pairs={{0,160},{32,128},{64,224},{96,192},{128,32},{160,0},{192,96},{224,... | collective-permute-start | bytes 786440 | tf_op jit(solution)/shard_map/ppermute | solution.py:314
  203.6 14.5 %collective-permute-done.refs_0_ = f32[8,32,256]{2,1,0:T(8,128)S(1)} collective-permute-done((f32[8,32,256]{2,1,0:T(8,128)S(1)}, f32[8,32,256]{2,1,0:T(8,128)S(1)}, u32[]{:S(2)}, u32[]{:S(2)}) %collective-permute-start) | collective-permute-done | bytes 262176 | tf_op jit(solution)/shard_map/ppermute | solution.py:314
  218.1 13.6 %collective-permute-start.5 = (f32[8,32,256]{2,1,0:T(8,128)S(1)}, f32[8,32,256]{2,1,0:T(8,128)S(1)}, u32[]{:S(2)}, u32[]{:S(2)}) collective-permute-start(f32[8,32,256]{2,1,0:T(8,128)S(1)} %get-tuple-element.45), channel_id=1, source_target_pairs={{0,192},{32,224},{64,0},{96,32},{128,64},{160,96},{192,128},{224,1... | collective-permute-start | bytes 786440 | tf_op jit(solution)/shard_map/ppermute | solution.py:314
  231.8 0.0 collective-permute-done.1.refs_0_
  231.8 2.7 collective-permute-start.6
  234.5 0.0 collective-permute-done.2.refs_0_
  234.5 0.0 collective-permute-done.3.refs_0_
  234.5 0.7 copy-done.8
  235.2 0.0 collective-permute-done.4.refs_0_
  235.2 0.7 copy-done.4
  235.9 2.6 collective-permute-done.5.refs_0_
  238.5 6.2 %collective-permute-done.6.refs_0_ = f32[8,32,256]{2,1,0:T(8,128)S(1)} collective-permute-done((f32[8,32,256]{2,1,0:T(8,128)S(1)}, f32[8,32,256]{2,1,0:T(8,128)S(1)}, u32[]{:S(2)}, u32[]{:S(2)}) %collective-permute-start.6) | collective-permute-done | bytes 262176 | tf_op jit(solution)/shard_map/ppermute | solution.py:314
  244.8 0.0 all-to-all-done.3.in_ref
  244.8 0.0 copy-start.3
  244.8 0.0 copy-start.10
  244.8 4.4 %y_inverse_1.1 = (f32[8,32,256]{2,1,0:T(8,128)S(1)}, f32[8,32,256]{2,1,0:T(8,128)S(1)}, f32[8,32,256]{2,1,0:T(8,128)S(1)}, f32[8,32,256]{2,1,0:T(8,128)S(1)}, f3...) custom-call(s32[1]{0:T(128)} %bitcast.idx_ref, ...), custom_call_target="tpu_custom_call" | custom-call | flops 3200000000 | bytes 12000000 | tf_op jit(solution)/shard_map/y_inverse_1/pallas_call | solution.py:298
  249.3 2.7 collective-permute-start.13
  252.0 1.3 collective-permute-start.12
  253.3 3.7 %collective-permute-start.11 = (f32[8,32,256]{2,1,0:T(8,128)S(1)}, f32[8,32,256]{2,1,0:T(8,128)S(1)}, u32[]{:S(2)}, u32[]{:S(2)}) collective-permute-start(f32[8,32,256]{2,1,0:T(8,128)S(1)} %get-tuple-element.52), channel_id=1, source_target_pairs={{0,96},{32,64},{64,160},{96,128},{128,224},{160,192},{192,32},{224... | collective-permute-start | bytes 786440 | tf_op jit(solution)/shard_map/ppermute | solution.py:314
  257.0 0.8 collective-permute-start.10
  257.9 2.2 collective-permute-start.9
  260.1 0.0 copy-done.2
  260.1 0.0 copy-start.9
  260.1 1.5 gradient_0.1
  261.6 0.0 collective-permute-done.13.refs_1_
  261.6 2.7 collective-permute-start.8
  264.3 1.5 gradient_4.1
  265.8 0.7 collective-permute-done.12.refs_1_
  266.6 3.6 %collective-permute-start.7 = (f32[8,32,256]{2,1,0:T(8,128)S(1)}, f32[8,32,256]{2,1,0:T(8,128)S(1)}, u32[]{:S(2)}, u32[]{:S(2)}) collective-permute-start(f32[8,32,256]{2,1,0:T(8,128)S(1)} %get-tuple-element.48), channel_id=1, source_target_pairs={{0,32},{32,0},{64,96},{96,64},{128,160},{160,128},{192,224},{224,1... | collective-permute-start | bytes 786440 | tf_op jit(solution)/shard_map/ppermute | solution.py:314
  270.2 0.0 copy-done.5
  270.2 1.5 gradient_5.1
  271.7 2.2 collective-permute-done.11.refs_1_
  273.9 1.5 gradient_3.1
  275.4 2.6 collective-permute-done.10.refs_1_
  278.0 1.5 gradient_2.1
  279.5 0.0 collective-permute-done.9.refs_1_
  279.5 1.5 gradient_7.1
  281.0 0.0 collective-permute-done.8.refs_1_
  281.1 1.5 gradient_6.1
  282.6 0.0 collective-permute-done.7.refs_1_
  282.6 2.6 gradient_1.1
  (16 shorter events, 0.0 us)
Async XLA Ops:
  11.6 60.4 %all-to-all-start = ((f32[32,8,8,256]{3,2,1,0:T(8,128)}), f32[32,8,8,256]{3,2,1,0:T(8,128)}, u32[]{:S(2)}, u32[]{:S(2)}) async-start(f32[32,8,8,256]{3,2,1,0:T(8,128)} %head_0.1), calls=%async_computation | async-start | bytes 4194304 | tf_op jit(solution)/shard_map/all_to_all | solution.py:310
  32.6 44.1 %copy-start.11 = (f32[1,256,8,256]{3,2,1,0:T(8,128)S(1)}, f32[1,256,8,256]{3,2,1,0:T(8,128)}, u32[]{:S(2)}) copy-start(f32[1,256,8,256]{3,2,1,0:T(8,128)} %param.16) | copy-start | bytes 6291460
  32.6 44.1 %copy-start.12 = (bf16[512,768]{1,0:T(8,128)(2,1)S(1)}, bf16[512,768]{1,0:T(8,128)(2,1)}, u32[]{:S(2)}) copy-start(bf16[512,768]{1,0:T(8,128)(2,1)} %constant.15.clone.inverse_ref.table_ref) | copy-start | bytes 2359300
  72.0 55.0 %all-to-all-start.1 = ((f32[32,8,8,256]{3,2,1,0:T(8,128)}), f32[32,8,8,256]{3,2,1,0:T(8,128)}, u32[]{:S(2)}, u32[]{:S(2)}) async-start(f32[32,8,8,256]{3,2,1,0:T(8,128)} %head_1.1), calls=%async_computation.1 | async-start | bytes 4194304 | tf_op jit(solution)/shard_map/all_to_all | solution.py:310
  76.8 1.1 copy-start.13
  127.0 55.0 %all-to-all-start.2 = ((f32[32,8,8,256]{3,2,1,0:T(8,128)}), f32[32,8,8,256]{3,2,1,0:T(8,128)}, u32[]{:S(2)}, u32[]{:S(2)}) async-start(f32[32,8,8,256]{3,2,1,0:T(8,128)} %bitcast.20), calls=%async_computation.2 | async-start | bytes 4194304 | tf_op jit(solution)/shard_map/all_to_all | solution.py:310
  131.8 1.1 copy-start.14
  182.1 62.7 %all-to-all-start.3 = ((f32[32,8,8,256]{3,2,1,0:T(8,128)}), f32[32,8,8,256]{3,2,1,0:T(8,128)S(1)}, u32[]{:S(2)}, u32[]{:S(2)}) async-start(f32[32,8,8,256]{3,2,1,0:T(8,128)} %bitcast.19), calls=%async_computation.3 | async-start | bytes 4194304 | tf_op jit(solution)/shard_map/all_to_all | solution.py:310
  191.7 0.7 copy-start.6
  192.4 25.7 %collective-permute-start = (f32[8,32,256]{2,1,0:T(8,128)S(1)}, f32[8,32,256]{2,1,0:T(8,128)S(1)}, u32[]{:S(2)}, u32[]{:S(2)}) collective-permute-start(f32[8,32,256]{2,1,0:T(8,128)S(1)} %get-tuple-element.38), channel_id=1, source_target_pairs={{0,32},{32,0},{64,96},{96,64},{128,160},{160,128},{192,224},{224,1... | collective-permute-start | bytes 786440 | tf_op jit(solution)/shard_map/ppermute | solution.py:314
  194.7 37.1 %collective-permute-start.1 = (f32[8,32,256]{2,1,0:T(8,128)S(1)}, f32[8,32,256]{2,1,0:T(8,128)S(1)}, u32[]{:S(2)}, u32[]{:S(2)}) collective-permute-start(f32[8,32,256]{2,1,0:T(8,128)S(1)} %get-tuple-element.41), channel_id=1, source_target_pairs={{0,64},{32,96},{64,128},{96,160},{128,192},{160,224},{192,0},{224,... | collective-permute-start | bytes 786440 | tf_op jit(solution)/shard_map/ppermute | solution.py:314
  196.2 38.3 %collective-permute-start.2 = (f32[8,32,256]{2,1,0:T(8,128)S(1)}, f32[8,32,256]{2,1,0:T(8,128)S(1)}, u32[]{:S(2)}, u32[]{:S(2)}) collective-permute-start(f32[8,32,256]{2,1,0:T(8,128)S(1)} %get-tuple-element.42), channel_id=1, source_target_pairs={{0,96},{32,64},{64,160},{96,128},{128,224},{160,192},{192,32},{224... | collective-permute-start | bytes 786440 | tf_op jit(solution)/shard_map/ppermute | solution.py:314
  198.4 36.2 %collective-permute-start.3 = (f32[8,32,256]{2,1,0:T(8,128)S(1)}, f32[8,32,256]{2,1,0:T(8,128)S(1)}, u32[]{:S(2)}, u32[]{:S(2)}) collective-permute-start(f32[8,32,256]{2,1,0:T(8,128)S(1)} %get-tuple-element.43), channel_id=1, source_target_pairs={{0,128},{32,160},{64,192},{96,224},{128,0},{160,32},{192,64},{224,... | collective-permute-start | bytes 786440 | tf_op jit(solution)/shard_map/ppermute | solution.py:314
  200.1 35.2 %collective-permute-start.4 = (f32[8,32,256]{2,1,0:T(8,128)S(1)}, f32[8,32,256]{2,1,0:T(8,128)S(1)}, u32[]{:S(2)}, u32[]{:S(2)}) collective-permute-start(f32[8,32,256]{2,1,0:T(8,128)S(1)} %get-tuple-element.44), channel_id=1, source_target_pairs={{0,160},{32,128},{64,224},{96,192},{128,32},{160,0},{192,96},{224,... | collective-permute-start | bytes 786440 | tf_op jit(solution)/shard_map/ppermute | solution.py:314
  218.1 20.4 %collective-permute-start.5 = (f32[8,32,256]{2,1,0:T(8,128)S(1)}, f32[8,32,256]{2,1,0:T(8,128)S(1)}, u32[]{:S(2)}, u32[]{:S(2)}) collective-permute-start(f32[8,32,256]{2,1,0:T(8,128)S(1)} %get-tuple-element.45), channel_id=1, source_target_pairs={{0,192},{32,224},{64,0},{96,32},{128,64},{160,96},{192,128},{224,1... | collective-permute-start | bytes 786440 | tf_op jit(solution)/shard_map/ppermute | solution.py:314
  231.8 13.0 %collective-permute-start.6 = (f32[8,32,256]{2,1,0:T(8,128)S(1)}, f32[8,32,256]{2,1,0:T(8,128)S(1)}, u32[]{:S(2)}, u32[]{:S(2)}) collective-permute-start(f32[8,32,256]{2,1,0:T(8,128)S(1)} %get-tuple-element.46), channel_id=1, source_target_pairs={{0,224},{32,192},{64,32},{96,0},{128,96},{160,64},{192,160},{224,1... | collective-permute-start | bytes 786440 | tf_op jit(solution)/shard_map/ppermute | solution.py:314
  234.5 0.7 copy-start.8
  235.2 0.7 copy-start.4
  244.8 15.3 %copy-start = (bf16[3,8,256,256]{3,2,1,0:T(8,128)(2,1)S(1)}, bf16[3,8,256,256]{3,2,1,0:T(8,128)(2,1)}, u32[]{:S(2)}) copy-start(bf16[3,8,256,256]{3,2,1,0:T(8,128)(2,1)} %shift_ref.19) | copy-start | bytes 9437188
  244.8 15.3 %copy-start.1 = (bf16[2,8,256,256]{3,2,1,0:T(8,128)(2,1)S(1)}, bf16[2,8,256,256]{3,2,1,0:T(8,128)(2,1)}, u32[]{:S(2)}) copy-start(bf16[2,8,256,256]{3,2,1,0:T(8,128)(2,1)} %rho_ref.19) | copy-start | bytes 6291460
  244.8 15.3 %copy-start.2 = (s32[8,256,256]{2,1,0:T(8,128)S(1)}, s32[8,256,256]{2,1,0:T(8,128)}, u32[]{:S(2)}) copy-start(s32[8,256,256]{2,1,0:T(8,128)} %support_ref.19) | copy-start | bytes 6291460
  244.8 15.3 %copy-start.3 = (bf16[1536,512]{1,0:T(8,128)(2,1)S(1)}, bf16[1536,512]{1,0:T(8,128)(2,1)}, u32[]{:S(2)}) copy-start(bf16[1536,512]{1,0:T(8,128)(2,1)} %constant.16.clone.refs_2_) | copy-start | bytes 4718596
  244.8 15.3 %copy-start.7 = (f32[8,32,256]{2,1,0:T(8,128)S(1)}, f32[8,32,256]{2,1,0:T(8,128)}, u32[]{:S(2)}) copy-start(f32[8,32,256]{2,1,0:T(8,128)} %copy-done.6) | copy-start | bytes 786436
  244.8 15.3 %copy-start.10 = (s32[8,3]{0,1:T(4,128)S(1)}, s32[8,3]{0,1:T(4,128)}, u32[]{:S(2)}) copy-start(s32[8,3]{0,1:T(4,128)} %param.15) | copy-start | bytes 292
  249.3 12.3 %collective-permute-start.13 = (f32[8,32,256]{2,1,0:T(8,128)S(1)}, f32[8,32,256]{2,1,0:T(8,128)S(1)}, u32[]{:S(2)}, u32[]{:S(2)}) collective-permute-start(f32[8,32,256]{2,1,0:T(8,128)S(1)} %get-tuple-element.54), channel_id=1, source_target_pairs={{0,128},{32,160},{64,192},{96,224},{128,0},{160,32},{192,64},{224,... | collective-permute-start | bytes 786440 | tf_op jit(solution)/shard_map/ppermute | solution.py:314
  252.0 14.6 %collective-permute-start.12 = (f32[8,32,256]{2,1,0:T(8,128)S(1)}, f32[8,32,256]{2,1,0:T(8,128)S(1)}, u32[]{:S(2)}, u32[]{:S(2)}) collective-permute-start(f32[8,32,256]{2,1,0:T(8,128)S(1)} %get-tuple-element.53), channel_id=1, source_target_pairs={{0,160},{32,128},{64,224},{96,192},{128,32},{160,0},{192,96},{224,... | collective-permute-start | bytes 786440 | tf_op jit(solution)/shard_map/ppermute | solution.py:314
  253.3 20.6 %collective-permute-start.11 = (f32[8,32,256]{2,1,0:T(8,128)S(1)}, f32[8,32,256]{2,1,0:T(8,128)S(1)}, u32[]{:S(2)}, u32[]{:S(2)}) collective-permute-start(f32[8,32,256]{2,1,0:T(8,128)S(1)} %get-tuple-element.52), channel_id=1, source_target_pairs={{0,96},{32,64},{64,160},{96,128},{128,224},{160,192},{192,32},{224... | collective-permute-start | bytes 786440 | tf_op jit(solution)/shard_map/ppermute | solution.py:314
  257.0 21.0 %collective-permute-start.10 = (f32[8,32,256]{2,1,0:T(8,128)S(1)}, f32[8,32,256]{2,1,0:T(8,128)S(1)}, u32[]{:S(2)}, u32[]{:S(2)}) collective-permute-start(f32[8,32,256]{2,1,0:T(8,128)S(1)} %get-tuple-element.51), channel_id=1, source_target_pairs={{0,64},{32,96},{64,128},{96,160},{128,192},{160,224},{192,0},{224,... | collective-permute-start | bytes 786440 | tf_op jit(solution)/shard_map/ppermute | solution.py:314
  257.9 21.7 %collective-permute-start.9 = (f32[8,32,256]{2,1,0:T(8,128)S(1)}, f32[8,32,256]{2,1,0:T(8,128)S(1)}, u32[]{:S(2)}, u32[]{:S(2)}) collective-permute-start(f32[8,32,256]{2,1,0:T(8,128)S(1)} %get-tuple-element.50), channel_id=1, source_target_pairs={{0,224},{32,192},{64,32},{96,0},{128,96},{160,64},{192,160},{224,1... | collective-permute-start | bytes 786440 | tf_op jit(solution)/shard_map/ppermute | solution.py:314
  260.1 4.2 %copy-start.9 = (f32[8,32,256]{2,1,0:T(8,128)S(1)}, f32[8,32,256]{2,1,0:T(8,128)}, u32[]{:S(2)}) copy-start(f32[8,32,256]{2,1,0:T(8,128)} %copy-done.8) | copy-start | bytes 786436
  261.6 19.4 %collective-permute-start.8 = (f32[8,32,256]{2,1,0:T(8,128)S(1)}, f32[8,32,256]{2,1,0:T(8,128)S(1)}, u32[]{:S(2)}, u32[]{:S(2)}) collective-permute-start(f32[8,32,256]{2,1,0:T(8,128)S(1)} %get-tuple-element.49), channel_id=1, source_target_pairs={{0,192},{32,224},{64,0},{96,32},{128,64},{160,96},{192,128},{224,1... | collective-permute-start | bytes 786440 | tf_op jit(solution)/shard_map/ppermute | solution.py:314
  264.3 5.9 %copy-start.5 = (f32[8,32,256]{2,1,0:T(8,128)S(1)}, f32[8,32,256]{2,1,0:T(8,128)}, u32[]{:S(2)}) copy-start(f32[8,32,256]{2,1,0:T(8,128)} %copy-done.4) | copy-start | bytes 786436
  266.6 16.0 %collective-permute-start.7 = (f32[8,32,256]{2,1,0:T(8,128)S(1)}, f32[8,32,256]{2,1,0:T(8,128)S(1)}, u32[]{:S(2)}, u32[]{:S(2)}) collective-permute-start(f32[8,32,256]{2,1,0:T(8,128)S(1)} %get-tuple-element.48), channel_id=1, source_target_pairs={{0,32},{32,0},{64,96},{96,64},{128,160},{160,128},{192,224},{224,1... | collective-permute-start | bytes 786440 | tf_op jit(solution)/shard_map/ppermute | solution.py:314

commit v7 on v6

--- a/solution.py
+++ b/solution.py
@@ -17,7 +17,7 @@
 XL = 8
 NREF = 8
 HEAD_ROWS = 32
-R_ORDER = (4, 5, 3, 2, 7, 6, 1)
+R_ORDER = (5, 4, 1, 3, 7, 2, 6)
 BF = jnp.bfloat16
 F32 = jnp.float32
 
@@ -304,14 +304,14 @@
             compiler_params=params(24),
             cost_estimate=cost(3.2e9, 12e6),
             name=f"y_inverse_{c}",
-        )(idx, part, in_hbm(inverse))
+        )(idx, part, inverse)
 
     def over_grid(part):
         return lax.all_to_all(part, "grid", 0, 0, tiled=True)
 
-    def over_refl(parts, order):
+    def over_refl(parts):
         ring = lambda s: [(i, (i // 2 + s // 2) % (NREF // 2) * 2 + (i + s) % 2) for i in range(NREF)]
-        moved = {s: lax.ppermute(parts[s], "refl", ring(s)) for s in order}
+        moved = {s: lax.ppermute(parts[s], "refl", ring(s)) for s in R_ORDER}
         return [parts[0]] + [moved[s] for s in range(1, NREF)]
 
     def gradient(s, parts, sums):
@@ -331,8 +331,9 @@
     f1 = over_grid(after(head(1, millers, density, displacement, support), f0))
     b0 = over_grid(after(x_both(0, f0), f1))
     b1 = over_grid(after(x_both(1, f1), b0))
-    r0 = over_refl(y_inverse(0, in_hbm(b0)), (5, 4, 1, 3, 7, 2, 6))
-    r1 = over_refl(y_inverse(1, after(b1, *r0)), R_ORDER)
+    r0 = over_refl(y_inverse(0, in_hbm(b0)))
+    parts = y_inverse(1, after(b1, *(r0[s] for s in R_ORDER[:5])))
+    r1 = over_refl(after(parts, *r0))
     sums = ()
     for s in (0,) + R_ORDER:
         sums = gradient(s, (r0[s], r1[s]), sums)

time: 288 us -> 285 us (0.990)
  starting transfers between devices: 69.1 us -> 56.8 us
  waiting for transfers between devices: 142 us -> 150 us
    ppermute x14, starting transfers between devices: 44.8 us -> 32.5 us  [over_refl(): moved = {s: lax.ppermute(parts[s], 'refl', ring(s)) for s in R_ORDER}]
    ppermute x14, waiting for transfers between devices: 28.8 us -> 36.2 us  [over_refl(): moved = {s: lax.ppermute(parts[s], 'refl', ring(s)) for s in R_ORDER}]
  transfers between devices with their start and end apart: 18 -> 18, of which waited for: 9 -> 9; matrix products, arithmetic and copies ran while one was open for 0% -> 0% of each run, Pallas kernels for 18% -> 20%
where the time goes in v7:
time: 285 us; the launch traced here: 283 us
  waiting for transfers between devices  150 us (53%)
  Pallas kernels  69.7 us (24%)
  starting transfers between devices  56.8 us (20%)
  local copies, waits for them, and re-layouts  5.58 us (2%)
    all_to_all x4, waiting for transfers between devices, over_grid(): return lax.all_to_all(part, 'grid', 0, 0, tiled=True)  114 us
    ppermute x14, waiting for transfers between devices, over_refl(): moved = {s: lax.ppermute(parts[s], 'refl', ring(s)) for s in R_ORDER}  36.2 us
    ppermute x14, starting transfers between devices, over_refl(): moved = {s: lax.ppermute(parts[s], 'refl', ring(s)) for s in R_ORDER}  32.5 us
    all_to_all x4, starting transfers between devices, over_grid(): return lax.all_to_all(part, 'grid', 0, 0, tiled=True)  24.3 us
    pallas_call x2, Pallas kernels, x_both(): pl.pallas_call(x_kernel, grid=(1,), in_specs=[HBM, pl.BlockSpec((N * XL,...  24.3 us
    pallas_call x2, Pallas kernels, head(): pl.pallas_call(head_kernel, grid=(XL + 2,), in_specs=[SMEM, pl.BlockSpec(...  21.9 us
    pallas_call x8, Pallas kernels, gradient(): pl.pallas_call(functools.partial(gradient_kernel, s), in_specs=[SMEM, SME...  13.1 us
    pallas_call x2, Pallas kernels, y_inverse(): pl.pallas_call(y_inverse_kernel, in_specs=[SMEM, VMEM, VMEM], out_specs=[...  10.4 us
  transfers between devices with their start and end apart: 18, of which 9 were waited for; matrix products, arithmetic and copies ran while one was open for 0% of the time, Pallas kernels for 20%

profile of v7, /device:TPU:8, one launch (start us, length us, event | category | flops | bytes accessed | tf_op | source)
XLA Modules:
  0.0 283.1 jit_solution(8332548353043604534)
XLA Ops:
  0.6 10.9 %head_0.1 = f32[32,8,8,256]{3,2,1,0:T(8,128)} custom-call(s32[3,8]{1,0:T(4,128)} %bitcast.7, bf16[2,8,256,256]{3,2,1,0:T(8,128)(2,1)} %rho_ref.19, bf16[3,8,256,256]{3,2,1,0:T(8,128)(2,1)} %shift_ref.19, s32[8,256,256]{2,1,0:T(8,128)} %support_ref.19, bf16[1536,512]{1,0:T(8,128)(2,1)} %constant.17.clone.table_ref, ...), custom_call_target="tpu_custom_call" | custom-call | flops 6400000000 | bytes 16000000 | tf_op jit(solution)/shard_map/head_0/pallas_call | solution.py:256
  11.5 10.1 %all-to-all-start = ((f32[32,8,8,256]{3,2,1,0:T(8,128)}), f32[32,8,8,256]{3,2,1,0:T(8,128)}, u32[]{:S(2)}, u32[]{:S(2)}) async-start(f32[32,8,8,256]{3,2,1,0:T(8,128)} %head_0.1), calls=%async_computation | async-start | bytes 4194304 | tf_op jit(solution)/shard_map/all_to_all | solution.py:310
  21.7 11.0 %head_1.1 = f32[32,8,8,256]{3,2,1,0:T(8,128)} custom-call(s32[3,8]{1,0:T(4,128)} %bitcast.8, bf16[2,8,256,256]{3,2,1,0:T(8,128)(2,1)} %rho_ref.19, bf16[3,8,256,256]{3,2,1,0:T(8,128)(2,1)} %shift_ref.19, s32[8,256,256]{2,1,0:T(8,128)} %support_ref.19, bf16[1536,512]{1,0:T(8,128)(2,1)} %constant.17.clone.table_ref, ...), custom_call_target="tpu_custom_call" | custom-call | flops 6400000000 | bytes 16000000 | tf_op jit(solution)/shard_map/head_1/pallas_call | solution.py:256
  32.6 39.3 %all-to-all-done = f32[32,8,8,256]{3,2,1,0:T(8,128)} async-done(((f32[32,8,8,256]{3,2,1,0:T(8,128)}), f32[32,8,8,256]{3,2,1,0:T(8,128)}, u32[]{:S(2)}, u32[]{:S(2)}) %all-to-all-start) | async-done | bytes 2097184 | tf_op jit(solution)/shard_map/all_to_all | solution.py:310
  72.0 4.7 %all-to-all-start.1 = ((f32[32,8,8,256]{3,2,1,0:T(8,128)}), f32[32,8,8,256]{3,2,1,0:T(8,128)}, u32[]{:S(2)}, u32[]{:S(2)}) async-start(f32[32,8,8,256]{3,2,1,0:T(8,128)} %head_1.1), calls=%async_computation.1 | async-start | bytes 4194304 | tf_op jit(solution)/shard_map/all_to_all | solution.py:310
  76.7 0.0 copy-done.11
  76.7 0.0 copy-done.12
  76.7 0.0 copy-start.14
  76.7 1.1 copy-done.14
  77.9 12.1 %x_0.1 = f32[2048,256]{1,0:T(8,128)} custom-call(f32[2048,256]{1,0:T(8,128)} %bitcast.2.in_ref, f32[2048,256]{1,0:T(8,128)S(1)} %bitcast.17, bf16[512,768]{1,0:T(8,128)(2,1)S(1)} %copy-done.14, bf16[512,768]{1,0:T(8,128)(2,1)S(1)} %copy-done.12), custom_call_target="tpu_custom_call" | custom-call | flops 6400000000 | bytes 24000000 | tf_op jit(solution)/shard_map/x_0/pallas_call | solution.py:285
  90.0 37.0 %all-to-all-done.1 = f32[32,8,8,256]{3,2,1,0:T(8,128)} async-done(((f32[32,8,8,256]{3,2,1,0:T(8,128)}), f32[32,8,8,256]{3,2,1,0:T(8,128)}, u32[]{:S(2)}, u32[]{:S(2)}) %all-to-all-start.1) | async-done | bytes 2097184 | tf_op jit(solution)/shard_map/all_to_all | solution.py:310
  127.0 4.7 %all-to-all-start.2 = ((f32[32,8,8,256]{3,2,1,0:T(8,128)}), f32[32,8,8,256]{3,2,1,0:T(8,128)}, u32[]{:S(2)}, u32[]{:S(2)}) async-start(f32[32,8,8,256]{3,2,1,0:T(8,128)} %bitcast.20), calls=%async_computation.2 | async-start | bytes 4194304 | tf_op jit(solution)/shard_map/all_to_all | solution.py:310
  131.8 0.0 copy-start.15
  131.8 1.1 copy-done.15
  132.9 12.1 %x_1.1 = f32[2048,256]{1,0:T(8,128)} custom-call(f32[2048,256]{1,0:T(8,128)} %bitcast.5.in_ref, f32[2048,256]{1,0:T(8,128)S(1)} %bitcast.18, bf16[512,768]{1,0:T(8,128)(2,1)S(1)} %copy-done.15, bf16[512,768]{1,0:T(8,128)(2,1)S(1)} %copy-done.12), custom_call_target="tpu_custom_call" | custom-call | flops 6400000000 | bytes 24000000 | tf_op jit(solution)/shard_map/x_1/pallas_call | solution.py:285
  145.0 37.0 %all-to-all-done.2.in_ref = f32[32,8,8,256]{3,2,1,0:T(8,128)} async-done(((f32[32,8,8,256]{3,2,1,0:T(8,128)}), f32[32,8,8,256]{3,2,1,0:T(8,128)}, u32[]{:S(2)}, u32[]{:S(2)}) %all-to-all-start.2) | async-done | bytes 2097184 | tf_op jit(solution)/shard_map/all_to_all | solution.py:310
  182.1 4.7 %all-to-all-start.3 = ((f32[32,8,8,256]{3,2,1,0:T(8,128)}), f32[32,8,8,256]{3,2,1,0:T(8,128)}, u32[]{:S(2)}, u32[]{:S(2)}) async-start(f32[32,8,8,256]{3,2,1,0:T(8,128)} %bitcast.19), calls=%async_computation.3 | async-start | bytes 4194304 | tf_op jit(solution)/shard_map/all_to_all | solution.py:310
  186.8 5.5 %y_inverse_0.1 = (f32[8,32,256]{2,1,0:T(8,128)S(1)}, f32[8,32,256]{2,1,0:T(8,128)S(1)}, f32[8,32,256]{2,1,0:T(8,128)}, f32[8,32,256]{2,1,0:T(8,128)S(1)}, f32[8,...) custom-call(s32[1]{0:T(128)} %bitcast.idx_ref, ...), custom_call_target="tpu_custom_call" | custom-call | flops 3200000000 | bytes 12000000 | tf_op jit(solution)/shard_map/y_inverse_0/pallas_call | solution.py:298
  192.3 0.7 copy-done.8
  193.1 4.8 %collective-permute-start.1 = (f32[8,32,256]{2,1,0:T(8,128)S(1)}, f32[8,32,256]{2,1,0:T(8,128)S(1)}, u32[]{:S(2)}, u32[]{:S(2)}) collective-permute-start(f32[8,32,256]{2,1,0:T(8,128)S(1)} %get-tuple-element.48), channel_id=1, source_target_pairs={{0,160},{32,128},{64,224},{96,192},{128,32},{160,0},{192,96},{224,... | collective-permute-start | bytes 786440 | tf_op jit(solution)/shard_map/ppermute | solution.py:314
  197.8 0.5 collective-permute-start.2
  198.3 1.2 collective-permute-start.3
  199.6 3.2 %collective-permute-start.4 = (f32[8,32,256]{2,1,0:T(8,128)S(1)}, f32[8,32,256]{2,1,0:T(8,128)S(1)}, u32[]{:S(2)}, u32[]{:S(2)}) collective-permute-start(f32[8,32,256]{2,1,0:T(8,128)S(1)} %get-tuple-element.51), channel_id=1, source_target_pairs={{0,96},{32,64},{64,160},{96,128},{128,224},{160,192},{192,32},{224... | collective-permute-start | bytes 786440 | tf_op jit(solution)/shard_map/ppermute | solution.py:314
  202.8 2.4 collective-permute-start.5
  205.2 5.1 %collective-permute-done.1.refs_0_ = f32[8,32,256]{2,1,0:T(8,128)S(1)} collective-permute-done((f32[8,32,256]{2,1,0:T(8,128)S(1)}, f32[8,32,256]{2,1,0:T(8,128)S(1)}, u32[]{:S(2)}, u32[]{:S(2)}) %collective-permute-start.1) | collective-permute-done | bytes 262176 | tf_op jit(solution)/shard_map/ppermute | solution.py:314
  210.3 0.7 copy-done.6
  211.0 2.7 collective-permute-start
  213.7 1.1 collective-permute-done.2.refs_0_
  214.8 0.7 copy-done.4
  215.5 2.1 collective-permute-start.6
  217.6 21.2 %collective-permute-done.3.refs_0_ = f32[8,32,256]{2,1,0:T(8,128)S(1)} collective-permute-done((f32[8,32,256]{2,1,0:T(8,128)S(1)}, f32[8,32,256]{2,1,0:T(8,128)S(1)}, u32[]{:S(2)}, u32[]{:S(2)}) %collective-permute-start.3) | collective-permute-done | bytes 262176 | tf_op jit(solution)/shard_map/ppermute | solution.py:314
  238.8 0.0 collective-permute-done.4.refs_0_
  238.8 0.0 collective-permute-done.5.refs_0_
  238.8 0.6 all-to-all-done.3.in_ref
  239.4 1.1 copy-done.13
  240.6 4.9 %y_inverse_1.1 = (f32[8,32,256]{2,1,0:T(8,128)S(1)}, f32[8,32,256]{2,1,0:T(8,128)S(1)}, f32[8,32,256]{2,1,0:T(8,128)S(1)}, f32[8,32,256]{2,1,0:T(8,128)S(1)}, f3...) custom-call(s32[1]{0:T(128)} %bitcast.idx_ref, ...), custom_call_target="tpu_custom_call" | custom-call | flops 3200000000 | bytes 12000000 | tf_op jit(solution)/shard_map/y_inverse_1/pallas_call | solution.py:298
  245.5 0.0 collective-permute-done.refs_0_
  245.5 0.0 collective-permute-done.6.refs_0_
  245.5 0.0 copy-start.7
  245.5 4.8 %collective-permute-start.13 = (f32[8,32,256]{2,1,0:T(8,128)S(1)}, f32[8,32,256]{2,1,0:T(8,128)S(1)}, u32[]{:S(2)}, u32[]{:S(2)}) collective-permute-start(f32[8,32,256]{2,1,0:T(8,128)S(1)} %get-tuple-element.70), channel_id=1, source_target_pairs={{0,160},{32,128},{64,224},{96,192},{128,32},{160,0},{192,96},{224,... | collective-permute-start | bytes 786440 | tf_op jit(solution)/shard_map/ppermute | solution.py:314
  250.3 1.2 collective-permute-start.12
  251.5 0.6 collective-permute-start.11
  252.1 2.8 collective-permute-start.10
  254.9 2.8 %collective-permute-start.9 = (f32[8,32,256]{2,1,0:T(8,128)S(1)}, f32[8,32,256]{2,1,0:T(8,128)S(1)}, u32[]{:S(2)}, u32[]{:S(2)}) collective-permute-start(f32[8,32,256]{2,1,0:T(8,128)S(1)} %get-tuple-element.66), channel_id=1, source_target_pairs={{0,224},{32,192},{64,32},{96,0},{128,96},{160,64},{192,160},{224,1... | collective-permute-start | bytes 786440 | tf_op jit(solution)/shard_map/ppermute | solution.py:314
  257.7 0.0 copy-done.1
  257.7 0.0 copy-done.10
  257.7 0.0 copy-done
  257.8 1.5 gradient_0.1
  259.2 0.0 collective-permute-done.13.refs_1_
  259.3 0.3 collective-permute-start.8
  259.6 1.5 gradient_5.1
  261.1 3.2 %collective-permute-done.12.refs_1_ = f32[8,32,256]{2,1,0:T(8,128)S(1)} collective-permute-done((f32[8,32,256]{2,1,0:T(8,128)S(1)}, f32[8,32,256]{2,1,0:T(8,128)S(1)}, u32[]{:S(2)}, u32[]{:S(2)}) %collective-permute-start.12) | collective-permute-done | bytes 262176 | tf_op jit(solution)/shard_map/ppermute | solution.py:314
  264.3 3.0 %collective-permute-start.7 = (f32[8,32,256]{2,1,0:T(8,128)S(1)}, f32[8,32,256]{2,1,0:T(8,128)S(1)}, u32[]{:S(2)}, u32[]{:S(2)}) collective-permute-start(f32[8,32,256]{2,1,0:T(8,128)S(1)} %get-tuple-element.64), channel_id=1, source_target_pairs={{0,192},{32,224},{64,0},{96,32},{128,64},{160,96},{192,128},{224,1... | collective-permute-start | bytes 786440 | tf_op jit(solution)/shard_map/ppermute | solution.py:314
  267.3 1.5 gradient_4.1
  268.8 5.7 %collective-permute-done.11.refs_1_ = f32[8,32,256]{2,1,0:T(8,128)S(1)} collective-permute-done((f32[8,32,256]{2,1,0:T(8,128)S(1)}, f32[8,32,256]{2,1,0:T(8,128)S(1)}, u32[]{:S(2)}, u32[]{:S(2)}) %collective-permute-start.11) | collective-permute-done | bytes 262176 | tf_op jit(solution)/shard_map/ppermute | solution.py:314
  274.4 1.5 gradient_1.1
  275.9 0.0 collective-permute-done.10.refs_1_
  276.0 1.5 gradient_3.1
  277.5 0.0 collective-permute-done.9.refs_1_
  277.5 1.5 gradient_7.1
  279.0 0.0 collective-permute-done.8.refs_1_
  279.0 1.5 gradient_2.1
  280.5 0.0 collective-permute-done.7.refs_1_
  280.5 2.6 gradient_6.1
  (18 shorter events, 0.0 us)
Async XLA Ops:
  11.5 60.4 %all-to-all-start = ((f32[32,8,8,256]{3,2,1,0:T(8,128)}), f32[32,8,8,256]{3,2,1,0:T(8,128)}, u32[]{:S(2)}, u32[]{:S(2)}) async-start(f32[32,8,8,256]{3,2,1,0:T(8,128)} %head_0.1), calls=%async_computation | async-start | bytes 4194304 | tf_op jit(solution)/shard_map/all_to_all | solution.py:310
  32.6 44.1 %copy-start.11 = (f32[1,256,8,256]{3,2,1,0:T(8,128)S(1)}, f32[1,256,8,256]{3,2,1,0:T(8,128)}, u32[]{:S(2)}) copy-start(f32[1,256,8,256]{3,2,1,0:T(8,128)} %param.16) | copy-start | bytes 6291460
  32.6 44.1 %copy-start.12 = (bf16[512,768]{1,0:T(8,128)(2,1)S(1)}, bf16[512,768]{1,0:T(8,128)(2,1)}, u32[]{:S(2)}) copy-start(bf16[512,768]{1,0:T(8,128)(2,1)} %constant.15.clone.inverse_ref.table_ref) | copy-start | bytes 2359300
  72.0 55.0 %all-to-all-start.1 = ((f32[32,8,8,256]{3,2,1,0:T(8,128)}), f32[32,8,8,256]{3,2,1,0:T(8,128)}, u32[]{:S(2)}, u32[]{:S(2)}) async-start(f32[32,8,8,256]{3,2,1,0:T(8,128)} %head_1.1), calls=%async_computation.1 | async-start | bytes 4194304 | tf_op jit(solution)/shard_map/all_to_all | solution.py:310
  76.7 1.1 copy-start.14
  127.0 55.1 %all-to-all-start.2 = ((f32[32,8,8,256]{3,2,1,0:T(8,128)}), f32[32,8,8,256]{3,2,1,0:T(8,128)}, u32[]{:S(2)}, u32[]{:S(2)}) async-start(f32[32,8,8,256]{3,2,1,0:T(8,128)} %bitcast.20), calls=%async_computation.2 | async-start | bytes 4194304 | tf_op jit(solution)/shard_map/all_to_all | solution.py:310
  131.8 1.1 copy-start.15
  182.1 57.4 %all-to-all-start.3 = ((f32[32,8,8,256]{3,2,1,0:T(8,128)}), f32[32,8,8,256]{3,2,1,0:T(8,128)}, u32[]{:S(2)}, u32[]{:S(2)}) async-start(f32[32,8,8,256]{3,2,1,0:T(8,128)} %bitcast.19), calls=%async_computation.3 | async-start | bytes 4194304 | tf_op jit(solution)/shard_map/all_to_all | solution.py:310
  192.3 0.7 copy-start.8
  193.1 17.3 %collective-permute-start.1 = (f32[8,32,256]{2,1,0:T(8,128)S(1)}, f32[8,32,256]{2,1,0:T(8,128)S(1)}, u32[]{:S(2)}, u32[]{:S(2)}) collective-permute-start(f32[8,32,256]{2,1,0:T(8,128)S(1)} %get-tuple-element.48), channel_id=1, source_target_pairs={{0,160},{32,128},{64,224},{96,192},{128,32},{160,0},{192,96},{224,... | collective-permute-start | bytes 786440 | tf_op jit(solution)/shard_map/ppermute | solution.py:314
  197.8 17.0 %collective-permute-start.2 = (f32[8,32,256]{2,1,0:T(8,128)S(1)}, f32[8,32,256]{2,1,0:T(8,128)S(1)}, u32[]{:S(2)}, u32[]{:S(2)}) collective-permute-start(f32[8,32,256]{2,1,0:T(8,128)S(1)} %get-tuple-element.49), channel_id=1, source_target_pairs={{0,128},{32,160},{64,192},{96,224},{128,0},{160,32},{192,64},{224,... | collective-permute-start | bytes 786440 | tf_op jit(solution)/shard_map/ppermute | solution.py:314
  198.3 40.5 %collective-permute-start.3 = (f32[8,32,256]{2,1,0:T(8,128)S(1)}, f32[8,32,256]{2,1,0:T(8,128)S(1)}, u32[]{:S(2)}, u32[]{:S(2)}) collective-permute-start(f32[8,32,256]{2,1,0:T(8,128)S(1)} %get-tuple-element.50), channel_id=1, source_target_pairs={{0,32},{32,0},{64,96},{96,64},{128,160},{160,128},{192,224},{224,1... | collective-permute-start | bytes 786440 | tf_op jit(solution)/shard_map/ppermute | solution.py:314
  199.6 39.3 %collective-permute-start.4 = (f32[8,32,256]{2,1,0:T(8,128)S(1)}, f32[8,32,256]{2,1,0:T(8,128)S(1)}, u32[]{:S(2)}, u32[]{:S(2)}) collective-permute-start(f32[8,32,256]{2,1,0:T(8,128)S(1)} %get-tuple-element.51), channel_id=1, source_target_pairs={{0,96},{32,64},{64,160},{96,128},{128,224},{160,192},{192,32},{224... | collective-permute-start | bytes 786440 | tf_op jit(solution)/shard_map/ppermute | solution.py:314
  202.8 36.0 %collective-permute-start.5 = (f32[8,32,256]{2,1,0:T(8,128)S(1)}, f32[8,32,256]{2,1,0:T(8,128)S(1)}, u32[]{:S(2)}, u32[]{:S(2)}) collective-permute-start(f32[8,32,256]{2,1,0:T(8,128)S(1)} %get-tuple-element.52), channel_id=1, source_target_pairs={{0,224},{32,192},{64,32},{96,0},{128,96},{160,64},{192,160},{224,1... | collective-permute-start | bytes 786440 | tf_op jit(solution)/shard_map/ppermute | solution.py:314
  210.3 0.7 copy-start.6
  211.0 34.5 %collective-permute-start = (f32[8,32,256]{2,1,0:T(8,128)}, f32[8,32,256]{2,1,0:T(8,128)S(1)}, u32[]{:S(2)}, u32[]{:S(2)}) collective-permute-start(f32[8,32,256]{2,1,0:T(8,128)} %get-tuple-element.46), channel_id=1, source_target_pairs={{0,192},{32,224},{64,0},{96,32},{128,64},{160,96},{192,128},{224,1... | collective-permute-start | bytes 786440 | tf_op jit(solution)/shard_map/ppermute | solution.py:314
  214.8 0.7 copy-start.4
  215.5 42.2 %copy-start.1 = (bf16[2,8,256,256]{3,2,1,0:T(8,128)(2,1)S(1)}, bf16[2,8,256,256]{3,2,1,0:T(8,128)(2,1)}, u32[]{:S(2)}) copy-start(bf16[2,8,256,256]{3,2,1,0:T(8,128)(2,1)} %rho_ref.19) | copy-start | bytes 6291460
  215.5 42.2 %copy-start.10 = (s32[8,3]{0,1:T(4,128)S(1)}, s32[8,3]{0,1:T(4,128)}, u32[]{:S(2)}) copy-start(s32[8,3]{0,1:T(4,128)} %param.15) | copy-start | bytes 292
  215.5 30.0 %collective-permute-start.6 = (f32[8,32,256]{2,1,0:T(8,128)}, f32[8,32,256]{2,1,0:T(8,128)S(1)}, u32[]{:S(2)}, u32[]{:S(2)}) collective-permute-start(f32[8,32,256]{2,1,0:T(8,128)} %get-tuple-element.63), channel_id=1, source_target_pairs={{0,64},{32,96},{64,128},{96,160},{128,192},{160,224},{192,0},{224,... | collective-permute-start | bytes 786440 | tf_op jit(solution)/shard_map/ppermute | solution.py:314
  239.4 1.1 copy-start.13
  240.6 17.2 %copy-start = (bf16[3,8,256,256]{3,2,1,0:T(8,128)(2,1)S(1)}, bf16[3,8,256,256]{3,2,1,0:T(8,128)(2,1)}, u32[]{:S(2)}) copy-start(bf16[3,8,256,256]{3,2,1,0:T(8,128)(2,1)} %shift_ref.19) | copy-start | bytes 9437188
  240.6 17.2 %copy-start.2 = (s32[8,256,256]{2,1,0:T(8,128)S(1)}, s32[8,256,256]{2,1,0:T(8,128)}, u32[]{:S(2)}) copy-start(s32[8,256,256]{2,1,0:T(8,128)} %support_ref.19) | copy-start | bytes 6291460
  240.6 17.2 %copy-start.3 = (bf16[1536,512]{1,0:T(8,128)(2,1)S(1)}, bf16[1536,512]{1,0:T(8,128)(2,1)}, u32[]{:S(2)}) copy-start(bf16[1536,512]{1,0:T(8,128)(2,1)} %constant.16.clone.refs_2_) | copy-start | bytes 4718596
  240.6 17.2 %copy-start.9 = (f32[8,32,256]{2,1,0:T(8,128)S(1)}, f32[8,32,256]{2,1,0:T(8,128)}, u32[]{:S(2)}) copy-start(f32[8,32,256]{2,1,0:T(8,128)} %copy-done.8) | copy-start | bytes 786436
  245.5 14.1 %copy-start.7 = (f32[8,32,256]{2,1,0:T(8,128)S(1)}, f32[8,32,256]{2,1,0:T(8,128)}, u32[]{:S(2)}) copy-start(f32[8,32,256]{2,1,0:T(8,128)} %copy-done.6) | copy-start | bytes 786436
  245.5 13.7 %collective-permute-start.13 = (f32[8,32,256]{2,1,0:T(8,128)S(1)}, f32[8,32,256]{2,1,0:T(8,128)S(1)}, u32[]{:S(2)}, u32[]{:S(2)}) collective-permute-start(f32[8,32,256]{2,1,0:T(8,128)S(1)} %get-tuple-element.70), channel_id=1, source_target_pairs={{0,160},{32,128},{64,224},{96,192},{128,32},{160,0},{192,96},{224,... | collective-permute-start | bytes 786440 | tf_op jit(solution)/shard_map/ppermute | solution.py:314
  250.3 14.0 %collective-permute-start.12 = (f32[8,32,256]{2,1,0:T(8,128)S(1)}, f32[8,32,256]{2,1,0:T(8,128)S(1)}, u32[]{:S(2)}, u32[]{:S(2)}) collective-permute-start(f32[8,32,256]{2,1,0:T(8,128)S(1)} %get-tuple-element.69), channel_id=1, source_target_pairs={{0,128},{32,160},{64,192},{96,224},{128,0},{160,32},{192,64},{224,... | collective-permute-start | bytes 786440 | tf_op jit(solution)/shard_map/ppermute | solution.py:314
  251.5 23.0 %collective-permute-start.11 = (f32[8,32,256]{2,1,0:T(8,128)S(1)}, f32[8,32,256]{2,1,0:T(8,128)S(1)}, u32[]{:S(2)}, u32[]{:S(2)}) collective-permute-start(f32[8,32,256]{2,1,0:T(8,128)S(1)} %get-tuple-element.68), channel_id=1, source_target_pairs={{0,32},{32,0},{64,96},{96,64},{128,160},{160,128},{192,224},{224,1... | collective-permute-start | bytes 786440 | tf_op jit(solution)/shard_map/ppermute | solution.py:314
  252.1 23.9 %collective-permute-start.10 = (f32[8,32,256]{2,1,0:T(8,128)S(1)}, f32[8,32,256]{2,1,0:T(8,128)S(1)}, u32[]{:S(2)}, u32[]{:S(2)}) collective-permute-start(f32[8,32,256]{2,1,0:T(8,128)S(1)} %get-tuple-element.67), channel_id=1, source_target_pairs={{0,96},{32,64},{64,160},{96,128},{128,224},{160,192},{192,32},{224... | collective-permute-start | bytes 786440 | tf_op jit(solution)/shard_map/ppermute | solution.py:314
  254.9 22.6 %collective-permute-start.9 = (f32[8,32,256]{2,1,0:T(8,128)S(1)}, f32[8,32,256]{2,1,0:T(8,128)S(1)}, u32[]{:S(2)}, u32[]{:S(2)}) collective-permute-start(f32[8,32,256]{2,1,0:T(8,128)S(1)} %get-tuple-element.66), channel_id=1, source_target_pairs={{0,224},{32,192},{64,32},{96,0},{128,96},{160,64},{192,160},{224,1... | collective-permute-start | bytes 786440 | tf_op jit(solution)/shard_map/ppermute | solution.py:314
  259.3 19.8 %collective-permute-start.8 = (f32[8,32,256]{2,1,0:T(8,128)S(1)}, f32[8,32,256]{2,1,0:T(8,128)S(1)}, u32[]{:S(2)}, u32[]{:S(2)}) collective-permute-start(f32[8,32,256]{2,1,0:T(8,128)S(1)} %get-tuple-element.65), channel_id=1, source_target_pairs={{0,64},{32,96},{64,128},{96,160},{128,192},{160,224},{192,0},{224,... | collective-permute-start | bytes 786440 | tf_op jit(solution)/shard_map/ppermute | solution.py:314
  259.6 7.7 %copy-start.5 = (f32[8,32,256]{2,1,0:T(8,128)S(1)}, f32[8,32,256]{2,1,0:T(8,128)}, u32[]{:S(2)}) copy-start(f32[8,32,256]{2,1,0:T(8,128)} %copy-done.4) | copy-start | bytes 786436
  264.3 16.2 %collective-permute-start.7 = (f32[8,32,256]{2,1,0:T(8,128)S(1)}, f32[8,32,256]{2,1,0:T(8,128)S(1)}, u32[]{:S(2)}, u32[]{:S(2)}) collective-permute-start(f32[8,32,256]{2,1,0:T(8,128)S(1)} %get-tuple-element.64), channel_id=1, source_target_pairs={{0,192},{32,224},{64,0},{96,32},{128,64},{160,96},{192,128},{224,1... | collective-permute-start | bytes 786440 | tf_op jit(solution)/shard_map/ppermute | solution.py:314

commit v8 on v7

--- a/solution.py
+++ b/solution.py
@@ -221,6 +221,43 @@
             out[n, x] = sums[old][n, x] + value if sums else value
 
 
+def early_kernel(shift_by, idx_ref, miller_ref, shift_ref, support_ref, in_ref, table_ref, back_ref, phase_ref):
+    g = partner(idx_ref[0], shift_by, -1)
+    h, k, l = (miller_ref[c, g].astype(F32) for c in range(3))
+    rows = pl.ds(pl.multiple_of(idx_ref[0] * 32, 32), 32)
+    high, low = split(in_ref[...].reshape(N, 2 * KC))
+    back_ref[...] = jnp.dot(
+        jnp.concatenate([high, low, high], 1), table_ref[...], preferred_element_type=F32
+    )
+    for x in range(XL):
+        u = [shift_ref[c, x, rows, :].astype(F32) for c in range(3)]
+        mask = support_ref[x, rows, :].astype(F32) * (1.0 / NREF)
+        cosine, sine = cos_sin_turns(h * u[0] + k * u[1] + l * u[2])
+        phase_ref[0, x] = mask * cosine
+        phase_ref[1, x] = mask * sine
+
+
+def late_kernel(shift_by, idx_ref, miller_ref, rho_ref, in_ref, back_ref, phase_ref, table_ref, *refs):
+    sums, (rho_out, shift_out) = refs[:2], refs[2:]
+    g = partner(idx_ref[0], shift_by, -1)
+    hkl = [miller_ref[c, g].astype(F32) for c in range(3)]
+    rows = pl.ds(pl.multiple_of(idx_ref[0] * 32, 32), 32)
+    high, low = split(in_ref[...].reshape(N, 2 * KC))
+    rest = jnp.dot(jnp.concatenate([high, low, high], 1), table_ref[...], preferred_element_type=F32)
+    for x in range(XL):
+        at = slice(x * 32, (x + 1) * 32)
+        back = back_ref[at, :] + rest[at]
+        real, imag = back[:, :N], back[:, N:]
+        cosine, sine = phase_ref[0, x], phase_ref[1, x]
+        p = cosine * real + sine * imag
+        q = cosine * imag - sine * real
+        twist = rho_ref[0, x, rows, :].astype(F32) * q - rho_ref[1, x, rows, :].astype(F32) * p
+        rho_out[0, x] = sums[0][0, x] + p
+        rho_out[1, x] = sums[0][1, x] + q
+        for c in range(3):
+            shift_out[c, x] = sums[1][c, x] + hkl[c] * twist
+
+
 SMEM = pl.BlockSpec(memory_space=pltpu.SMEM)
 VMEM = pl.BlockSpec(memory_space=pltpu.VMEM)
 HBM = pl.BlockSpec(memory_space=pltpu.HBM)
@@ -278,6 +315,9 @@
     idx = jnp.stack([r]).astype(jnp.int32)
     forward, inverse = jnp.asarray(left_table(False)), jnp.asarray(left_table(True))
     last_table = jnp.asarray(right_inverse())
+    tables = [
+        jnp.asarray(right_inverse().reshape(3, CH, 2 * KC, 2 * N)[:, c].reshape(6 * KC, 2 * N)) for c in range(CH)
+    ]
     amp = amplitude.reshape(N * XL, N)
     millers = millers.T
 
@@ -327,6 +367,30 @@
             )(idx, millers, density, displacement, support, *parts, last_table, *sums)
         )
 
+    def early(s, part):
+        return pl.pallas_call(
+            functools.partial(early_kernel, s),
+            in_specs=[SMEM, SMEM] + [VMEM] * 4,
+            out_specs=[VMEM] * 2,
+            out_shape=[f32(N, 2 * N), f32(2, XL, 32, N)],
+            compiler_params=params(16),
+            cost_estimate=cost(0.8e9, 5e6),
+            name=f"early_{s}",
+        )(idx, millers, displacement, support, part, tables[0])
+
+    def late(s, part, known, sums):
+        return tuple(
+            pl.pallas_call(
+                functools.partial(late_kernel, s),
+                in_specs=[SMEM, SMEM] + [VMEM] * 7,
+                out_specs=[VMEM] * 2,
+                out_shape=[f32(2, XL, 32, N), f32(3, XL, 32, N)],
+                compiler_params=params(16),
+                cost_estimate=cost(0.4e9, 5e6),
+                name=f"late_{s}",
+            )(idx, millers, density, part, *known, tables[1], *sums)
+        )
+
     f0 = over_grid(head(0, millers, density, displacement, support))
     f1 = over_grid(after(head(1, millers, density, displacement, support), f0))
     b0 = over_grid(after(x_both(0, f0), f1))
@@ -335,8 +399,12 @@
     parts = y_inverse(1, after(b1, *(r0[s] for s in R_ORDER[:5])))
     r1 = over_refl(after(parts, *r0))
     sums = ()
-    for s in (0,) + R_ORDER:
+    for s in (0,) + R_ORDER[:2]:
         sums = gradient(s, (r0[s], r1[s]), sums)
+    known = {s: early(s, after(r0[s], r1[R_ORDER[0]])) for s in R_ORDER[2:]}
+    sums = after(sums, known)
+    for s in R_ORDER[2:]:
+        sums = late(s, r1[s], known[s], sums)
     return sums
 
 

time: 285 us -> 283 us (level)
  Pallas kernels: 69.7 us -> 74.7 us
  waiting for transfers between devices: 150 us -> 145 us
    pallas_call x0 -> x10, Pallas kernels: none -> 13.3 us  [the longest x5 6.92 us: early(): pl.pallas_call(functools.partial(early_kernel, s), in_specs=[SMEM, SMEM]...]
    pallas_call x8 -> x3, Pallas kernels: 13.1 us -> 4.56 us  [gradient(): pl.pallas_call(functools.partial(gradient_kernel, s), in_specs=[SMEM, SME...]
    ppermute x14, waiting for transfers between devices: 36.2 us -> 31.9 us  [over_refl(): moved = {s: lax.ppermute(parts[s], 'refl', ring(s)) for s in R_ORDER}]
  transfers between devices with their start and end apart: 18 -> 18, of which waited for: 9 -> 8; matrix products, arithmetic and copies ran while one was open for 0% -> 0% of each run, Pallas kernels for 20% -> 22%
where the time goes in v8:
time: 283 us; the launch traced here: 282 us
  waiting for transfers between devices  145 us (51%)
  Pallas kernels  74.7 us (26%)
  starting transfers between devices  56.2 us (20%)
  local copies, waits for them, and re-layouts  4.18 us (1%)
    all_to_all x4, waiting for transfers between devices, over_grid(): return lax.all_to_all(part, 'grid', 0, 0, tiled=True)  114 us
    ppermute x14, waiting for transfers between devices, over_refl(): moved = {s: lax.ppermute(parts[s], 'refl', ring(s)) for s in R_ORDER}  31.9 us
    ppermute x14, starting transfers between devices, over_refl(): moved = {s: lax.ppermute(parts[s], 'refl', ring(s)) for s in R_ORDER}  31.8 us
    all_to_all x4, starting transfers between devices, over_grid(): return lax.all_to_all(part, 'grid', 0, 0, tiled=True)  24.4 us
    pallas_call x2, Pallas kernels, x_both(): pl.pallas_call(x_kernel, grid=(1,), in_specs=[HBM, pl.BlockSpec((N * XL,...  24.3 us
    pallas_call x2, Pallas kernels, head(): pl.pallas_call(head_kernel, grid=(XL + 2,), in_specs=[SMEM, pl.BlockSpec(...  22.1 us
    pallas_call x2, Pallas kernels, y_inverse(): pl.pallas_call(y_inverse_kernel, in_specs=[SMEM, VMEM, VMEM], out_specs=[...  10.4 us
    pallas_call x5, Pallas kernels, early(): pl.pallas_call(functools.partial(early_kernel, s), in_specs=[SMEM, SMEM]...  6.92 us
  transfers between devices with their start and end apart: 18, of which 8 were waited for; matrix products, arithmetic and copies ran while one was open for 0% of the time, Pallas kernels for 22%

profile of v8, /device:TPU:8, one launch (start us, length us, event | category | flops | bytes accessed | tf_op | source)
XLA Modules:
  0.0 281.5 jit_solution(14934694526575985656)
XLA Ops:
  0.6 11.1 %head_0.1 = f32[32,8,8,256]{3,2,1,0:T(8,128)} custom-call(s32[3,8]{1,0:T(4,128)} %bitcast.7, bf16[2,8,256,256]{3,2,1,0:T(8,128)(2,1)} %rho_ref.19, bf16[3,8,256,256]{3,2,1,0:T(8,128)(2,1)} %shift_ref.19, s32[8,256,256]{2,1,0:T(8,128)} %support_ref.19, bf16[1536,512]{1,0:T(8,128)(2,1)} %constant.23.clone.table_ref, ...), custom_call_target="tpu_custom_call" | custom-call | flops 6400000000 | bytes 16000000 | tf_op jit(solution)/shard_map/head_0/pallas_call | solution.py:293
  11.7 10.1 %all-to-all-start = ((f32[32,8,8,256]{3,2,1,0:T(8,128)}), f32[32,8,8,256]{3,2,1,0:T(8,128)}, u32[]{:S(2)}, u32[]{:S(2)}) async-start(f32[32,8,8,256]{3,2,1,0:T(8,128)} %head_0.1), calls=%async_computation | async-start | bytes 4194304 | tf_op jit(solution)/shard_map/all_to_all | solution.py:350
  21.8 11.1 %head_1.1 = f32[32,8,8,256]{3,2,1,0:T(8,128)} custom-call(s32[3,8]{1,0:T(4,128)} %bitcast.8, bf16[2,8,256,256]{3,2,1,0:T(8,128)(2,1)} %rho_ref.19, bf16[3,8,256,256]{3,2,1,0:T(8,128)(2,1)} %shift_ref.19, s32[8,256,256]{2,1,0:T(8,128)} %support_ref.19, bf16[1536,512]{1,0:T(8,128)(2,1)} %constant.23.clone.table_ref, ...), custom_call_target="tpu_custom_call" | custom-call | flops 6400000000 | bytes 16000000 | tf_op jit(solution)/shard_map/head_1/pallas_call | solution.py:293
  32.9 39.2 %all-to-all-done = f32[32,8,8,256]{3,2,1,0:T(8,128)} async-done(((f32[32,8,8,256]{3,2,1,0:T(8,128)}), f32[32,8,8,256]{3,2,1,0:T(8,128)}, u32[]{:S(2)}, u32[]{:S(2)}) %all-to-all-start) | async-done | bytes 2097184 | tf_op jit(solution)/shard_map/all_to_all | solution.py:350
  72.1 4.7 %all-to-all-start.1 = ((f32[32,8,8,256]{3,2,1,0:T(8,128)}), f32[32,8,8,256]{3,2,1,0:T(8,128)}, u32[]{:S(2)}, u32[]{:S(2)}) async-start(f32[32,8,8,256]{3,2,1,0:T(8,128)} %head_1.1), calls=%async_computation.1 | async-start | bytes 4194304 | tf_op jit(solution)/shard_map/all_to_all | solution.py:350
  76.8 0.0 copy-done.9
  76.8 0.0 copy-start.13
  76.8 1.1 copy-done.13
  78.0 12.2 %x_0.1 = f32[2048,256]{1,0:T(8,128)} custom-call(f32[2048,256]{1,0:T(8,128)} %bitcast.5.in_ref, f32[2048,256]{1,0:T(8,128)S(1)} %bitcast.22, bf16[512,768]{1,0:T(8,128)(2,1)S(1)} %copy-done.13, bf16[512,768]{1,0:T(8,128)(2,1)S(1)} %copy-done.10), custom_call_target="tpu_custom_call" | custom-call | flops 6400000000 | bytes 24000000 | tf_op jit(solution)/shard_map/x_0/pallas_call | solution.py:325
  90.1 37.0 %all-to-all-done.1 = f32[32,8,8,256]{3,2,1,0:T(8,128)} async-done(((f32[32,8,8,256]{3,2,1,0:T(8,128)}), f32[32,8,8,256]{3,2,1,0:T(8,128)}, u32[]{:S(2)}, u32[]{:S(2)}) %all-to-all-start.1) | async-done | bytes 2097184 | tf_op jit(solution)/shard_map/all_to_all | solution.py:350
  127.1 4.7 %all-to-all-start.2 = ((f32[32,8,8,256]{3,2,1,0:T(8,128)}), f32[32,8,8,256]{3,2,1,0:T(8,128)}, u32[]{:S(2)}, u32[]{:S(2)}) async-start(f32[32,8,8,256]{3,2,1,0:T(8,128)} %bitcast.25), calls=%async_computation.2 | async-start | bytes 4194304 | tf_op jit(solution)/shard_map/all_to_all | solution.py:350
  131.9 0.0 copy-start.14
  131.9 1.1 copy-done.14
  133.0 12.1 %x_1.1 = f32[2048,256]{1,0:T(8,128)} custom-call(f32[2048,256]{1,0:T(8,128)} %bitcast.2.in_ref, f32[2048,256]{1,0:T(8,128)S(1)} %bitcast.23, bf16[512,768]{1,0:T(8,128)(2,1)S(1)} %copy-done.14, bf16[512,768]{1,0:T(8,128)(2,1)S(1)} %copy-done.10), custom_call_target="tpu_custom_call" | custom-call | flops 6400000000 | bytes 24000000 | tf_op jit(solution)/shard_map/x_1/pallas_call | solution.py:325
  145.1 37.0 %all-to-all-done.2.in_ref = f32[32,8,8,256]{3,2,1,0:T(8,128)} async-done(((f32[32,8,8,256]{3,2,1,0:T(8,128)}), f32[32,8,8,256]{3,2,1,0:T(8,128)}, u32[]{:S(2)}, u32[]{:S(2)}) %all-to-all-start.2) | async-done | bytes 2097184 | tf_op jit(solution)/shard_map/all_to_all | solution.py:350
  182.2 4.9 %all-to-all-start.3 = ((f32[32,8,8,256]{3,2,1,0:T(8,128)}), f32[32,8,8,256]{3,2,1,0:T(8,128)}, u32[]{:S(2)}, u32[]{:S(2)}) async-start(f32[32,8,8,256]{3,2,1,0:T(8,128)} %bitcast.24), calls=%async_computation.3 | async-start | bytes 4194304 | tf_op jit(solution)/shard_map/all_to_all | solution.py:350
  187.0 5.5 %y_inverse_0.1 = (f32[8,32,256]{2,1,0:T(8,128)S(1)}, f32[8,32,256]{2,1,0:T(8,128)S(1)}, f32[8,32,256]{2,1,0:T(8,128)}, f32[8,32,256]{2,1,0:T(8,128)S(1)}, f32[8,...) custom-call(s32[1]{0:T(128)} %bitcast.idx_ref, ...), custom_call_target="tpu_custom_call" | custom-call | flops 3200000000 | bytes 12000000 | tf_op jit(solution)/shard_map/y_inverse_0/pallas_call | solution.py:338
  192.6 4.8 %collective-permute-start = (f32[8,32,256]{2,1,0:T(8,128)S(1)}, f32[8,32,256]{2,1,0:T(8,128)S(1)}, u32[]{:S(2)}, u32[]{:S(2)}) collective-permute-start(f32[8,32,256]{2,1,0:T(8,128)S(1)} %get-tuple-element.64), channel_id=1, source_target_pairs={{0,160},{32,128},{64,224},{96,192},{128,32},{160,0},{192,96},{224,... | collective-permute-start | bytes 786440 | tf_op jit(solution)/shard_map/ppermute | solution.py:354
  197.4 0.5 collective-permute-start.1
  197.9 1.2 collective-permute-start.2
  199.1 3.3 %collective-permute-start.3 = (f32[8,32,256]{2,1,0:T(8,128)S(1)}, f32[8,32,256]{2,1,0:T(8,128)S(1)}, u32[]{:S(2)}, u32[]{:S(2)}) collective-permute-start(f32[8,32,256]{2,1,0:T(8,128)S(1)} %get-tuple-element.67), channel_id=1, source_target_pairs={{0,96},{32,64},{64,160},{96,128},{128,224},{160,192},{192,32},{224... | collective-permute-start | bytes 786440 | tf_op jit(solution)/shard_map/ppermute | solution.py:354
  202.3 2.4 collective-permute-start.4
  204.7 5.5 %collective-permute-done.refs_0_ = f32[8,32,256]{2,1,0:T(8,128)S(1)} collective-permute-done((f32[8,32,256]{2,1,0:T(8,128)S(1)}, f32[8,32,256]{2,1,0:T(8,128)S(1)}, u32[]{:S(2)}, u32[]{:S(2)}) %collective-permute-start) | collective-permute-done | bytes 262176 | tf_op jit(solution)/shard_map/ppermute | solution.py:354
  210.2 3.5 %collective-permute-start.5 = (f32[8,32,256]{2,1,0:T(8,128)}, f32[8,32,256]{2,1,0:T(8,128)}, u32[]{:S(2)}, u32[]{:S(2)}) collective-permute-start(f32[8,32,256]{2,1,0:T(8,128)} %get-tuple-element.79), channel_id=1, source_target_pairs={{0,64},{32,96},{64,128},{96,160},{128,192},{160,224},{192,0},{224,... | collective-permute-start | bytes 786440 | tf_op jit(solution)/shard_map/ppermute | solution.py:354
  213.7 0.8 collective-permute-done.1.refs_0_
  214.5 0.6 collective-permute-start.6
  215.1 23.9 %collective-permute-done.2.in_ref = f32[8,32,256]{2,1,0:T(8,128)S(1)} collective-permute-done((f32[8,32,256]{2,1,0:T(8,128)S(1)}, f32[8,32,256]{2,1,0:T(8,128)S(1)}, u32[]{:S(2)}, u32[]{:S(2)}) %collective-permute-start.2) | collective-permute-done | bytes 262176 | tf_op jit(solution)/shard_map/ppermute | solution.py:354
  239.0 0.0 collective-permute-done.3.in_ref
  239.0 0.0 collective-permute-done.4.in_ref
  239.0 0.7 copy-done.7
  239.7 0.4 all-to-all-done.3.in_ref
  240.1 1.1 copy-done.12
  241.2 4.9 %y_inverse_1.1 = (f32[8,32,256]{2,1,0:T(8,128)S(1)}, f32[8,32,256]{2,1,0:T(8,128)S(1)}, f32[8,32,256]{2,1,0:T(8,128)S(1)}, f32[8,32,256]{2,1,0:T(8,128)S(1)}, f3...) custom-call(s32[1]{0:T(128)} %bitcast.idx_ref, ...), custom_call_target="tpu_custom_call" | custom-call | flops 3200000000 | bytes 12000000 | tf_op jit(solution)/shard_map/y_inverse_1/pallas_call | solution.py:338
  246.1 0.0 collective-permute-done.5.in_ref
  246.1 0.0 collective-permute-done.6.in_ref
  246.1 0.0 copy-start.3
  246.1 4.5 %collective-permute-start.8 = (f32[8,32,256]{2,1,0:T(8,128)S(1)}, f32[8,32,256]{2,1,0:T(8,128)S(1)}, u32[]{:S(2)}, u32[]{:S(2)}) collective-permute-start(f32[8,32,256]{2,1,0:T(8,128)S(1)} %get-tuple-element.82), channel_id=1, source_target_pairs={{0,160},{32,128},{64,224},{96,192},{128,32},{160,0},{192,96},{224,... | collective-permute-start | bytes 786440 | tf_op jit(solution)/shard_map/ppermute | solution.py:354
  250.6 0.5 collective-permute-start.13
  251.1 1.6 collective-permute-start.12
  252.7 2.6 collective-permute-start.11
  255.4 3.0 %collective-permute-start.10 = (f32[8,32,256]{2,1,0:T(8,128)S(1)}, f32[8,32,256]{2,1,0:T(8,128)S(1)}, u32[]{:S(2)}, u32[]{:S(2)}) collective-permute-start(f32[8,32,256]{2,1,0:T(8,128)S(1)} %get-tuple-element.90), channel_id=1, source_target_pairs={{0,224},{32,192},{64,32},{96,0},{128,96},{160,64},{192,160},{224,1... | collective-permute-start | bytes 786440 | tf_op jit(solution)/shard_map/ppermute | solution.py:354
  258.4 1.5 gradient_0.1
  259.9 0.0 collective-permute-done.8.refs_1_
  259.9 0.6 collective-permute-start.9
  260.5 1.2 early_1.1
  261.7 1.2 early_3.1
  263.0 1.2 early_7.1
  264.2 1.6 early_2.1
  265.8 1.6 early_6.1
  267.5 0.0 collective-permute-done.13.refs_1_
  267.5 2.8 collective-permute-start.7
  270.3 1.5 gradient_5.1
  271.8 0.0 copy-start.4
  271.8 1.5 gradient_4.1
  273.4 1.7 collective-permute-done.12.in_ref
  275.1 1.1 late_1.1
  276.1 0.0 collective-permute-done.11.in_ref
  276.2 1.1 late_3.1
  277.2 0.0 collective-permute-done.10.in_ref
  277.2 1.1 late_7.1
  278.3 0.0 collective-permute-done.9.in_ref
  278.3 1.1 late_2.1
  279.4 0.0 collective-permute-done.7.in_ref
  279.4 2.1 late_6.1
  (21 shorter events, 0.0 us)
Async XLA Ops:
  11.7 60.4 %all-to-all-start = ((f32[32,8,8,256]{3,2,1,0:T(8,128)}), f32[32,8,8,256]{3,2,1,0:T(8,128)}, u32[]{:S(2)}, u32[]{:S(2)}) async-start(f32[32,8,8,256]{3,2,1,0:T(8,128)} %head_0.1), calls=%async_computation | async-start | bytes 4194304 | tf_op jit(solution)/shard_map/all_to_all | solution.py:350
  32.9 43.9 %copy-start.9 = (f32[1,256,8,256]{3,2,1,0:T(8,128)S(1)}, f32[1,256,8,256]{3,2,1,0:T(8,128)}, u32[]{:S(2)}) copy-start(f32[1,256,8,256]{3,2,1,0:T(8,128)} %param.18) | copy-start | bytes 6291460
  32.9 44.0 %copy-start.10 = (bf16[512,768]{1,0:T(8,128)(2,1)S(1)}, bf16[512,768]{1,0:T(8,128)(2,1)}, u32[]{:S(2)}) copy-start(bf16[512,768]{1,0:T(8,128)(2,1)} %constant.19.clone.inverse_ref.table_ref) | copy-start | bytes 2359300
  72.1 55.0 %all-to-all-start.1 = ((f32[32,8,8,256]{3,2,1,0:T(8,128)}), f32[32,8,8,256]{3,2,1,0:T(8,128)}, u32[]{:S(2)}, u32[]{:S(2)}) async-start(f32[32,8,8,256]{3,2,1,0:T(8,128)} %head_1.1), calls=%async_computation.1 | async-start | bytes 4194304 | tf_op jit(solution)/shard_map/all_to_all | solution.py:350
  76.8 1.1 copy-start.13
  127.1 55.0 %all-to-all-start.2 = ((f32[32,8,8,256]{3,2,1,0:T(8,128)}), f32[32,8,8,256]{3,2,1,0:T(8,128)}, u32[]{:S(2)}, u32[]{:S(2)}) async-start(f32[32,8,8,256]{3,2,1,0:T(8,128)} %bitcast.25), calls=%async_computation.2 | async-start | bytes 4194304 | tf_op jit(solution)/shard_map/all_to_all | solution.py:350
  131.9 1.1 copy-start.14
  182.2 4.9 %copy-start.11 = (bf16[512,768]{1,0:T(8,128)(2,1)S(1)}, bf16[512,768]{1,0:T(8,128)(2,1)}, u32[]{:S(2)}) copy-start(bf16[512,768]{1,0:T(8,128)(2,1)} %constant.19.clone.inverse_ref.table_ref) | copy-start | bytes 2359300
  182.2 57.9 %all-to-all-start.3 = ((f32[32,8,8,256]{3,2,1,0:T(8,128)}), f32[32,8,8,256]{3,2,1,0:T(8,128)}, u32[]{:S(2)}, u32[]{:S(2)}) async-start(f32[32,8,8,256]{3,2,1,0:T(8,128)} %bitcast.24), calls=%async_computation.3 | async-start | bytes 4194304 | tf_op jit(solution)/shard_map/all_to_all | solution.py:350
  192.6 17.6 %collective-permute-start = (f32[8,32,256]{2,1,0:T(8,128)S(1)}, f32[8,32,256]{2,1,0:T(8,128)S(1)}, u32[]{:S(2)}, u32[]{:S(2)}) collective-permute-start(f32[8,32,256]{2,1,0:T(8,128)S(1)} %get-tuple-element.64), channel_id=1, source_target_pairs={{0,160},{32,128},{64,224},{96,192},{128,32},{160,0},{192,96},{224,... | collective-permute-start | bytes 786440 | tf_op jit(solution)/shard_map/ppermute | solution.py:354
  197.4 17.1 %collective-permute-start.1 = (f32[8,32,256]{2,1,0:T(8,128)S(1)}, f32[8,32,256]{2,1,0:T(8,128)S(1)}, u32[]{:S(2)}, u32[]{:S(2)}) collective-permute-start(f32[8,32,256]{2,1,0:T(8,128)S(1)} %get-tuple-element.65), channel_id=1, source_target_pairs={{0,128},{32,160},{64,192},{96,224},{128,0},{160,32},{192,64},{224,... | collective-permute-start | bytes 786440 | tf_op jit(solution)/shard_map/ppermute | solution.py:354
  197.9 41.1 %collective-permute-start.2 = (f32[8,32,256]{2,1,0:T(8,128)S(1)}, f32[8,32,256]{2,1,0:T(8,128)S(1)}, u32[]{:S(2)}, u32[]{:S(2)}) collective-permute-start(f32[8,32,256]{2,1,0:T(8,128)S(1)} %get-tuple-element.66), channel_id=1, source_target_pairs={{0,32},{32,0},{64,96},{96,64},{128,160},{160,128},{192,224},{224,1... | collective-permute-start | bytes 786440 | tf_op jit(solution)/shard_map/ppermute | solution.py:354
  199.1 39.9 %collective-permute-start.3 = (f32[8,32,256]{2,1,0:T(8,128)S(1)}, f32[8,32,256]{2,1,0:T(8,128)S(1)}, u32[]{:S(2)}, u32[]{:S(2)}) collective-permute-start(f32[8,32,256]{2,1,0:T(8,128)S(1)} %get-tuple-element.67), channel_id=1, source_target_pairs={{0,96},{32,64},{64,160},{96,128},{128,224},{160,192},{192,32},{224... | collective-permute-start | bytes 786440 | tf_op jit(solution)/shard_map/ppermute | solution.py:354
  202.3 36.6 %collective-permute-start.4 = (f32[8,32,256]{2,1,0:T(8,128)S(1)}, f32[8,32,256]{2,1,0:T(8,128)S(1)}, u32[]{:S(2)}, u32[]{:S(2)}) collective-permute-start(f32[8,32,256]{2,1,0:T(8,128)S(1)} %get-tuple-element.68), channel_id=1, source_target_pairs={{0,224},{32,192},{64,32},{96,0},{128,96},{160,64},{192,160},{224,1... | collective-permute-start | bytes 786440 | tf_op jit(solution)/shard_map/ppermute | solution.py:354
  210.2 35.9 %collective-permute-start.5 = (f32[8,32,256]{2,1,0:T(8,128)}, f32[8,32,256]{2,1,0:T(8,128)}, u32[]{:S(2)}, u32[]{:S(2)}) collective-permute-start(f32[8,32,256]{2,1,0:T(8,128)} %get-tuple-element.79), channel_id=1, source_target_pairs={{0,64},{32,96},{64,128},{96,160},{128,192},{160,224},{192,0},{224,... | collective-permute-start | bytes 786440 | tf_op jit(solution)/shard_map/ppermute | solution.py:354
  214.5 43.9 %copy-start.1 = (s32[8,256,256]{2,1,0:T(8,128)S(1)}, s32[8,256,256]{2,1,0:T(8,128)}, u32[]{:S(2)}) copy-start(s32[8,256,256]{2,1,0:T(8,128)} %support_ref.19) | copy-start | bytes 6291460
  214.5 43.9 %copy-start.6 = (s32[8,3]{0,1:T(4,128)S(1)}, s32[8,3]{0,1:T(4,128)}, u32[]{:S(2)}) copy-start(s32[8,3]{0,1:T(4,128)} %param.17) | copy-start | bytes 292
  214.5 31.6 %collective-permute-start.6 = (f32[8,32,256]{2,1,0:T(8,128)}, f32[8,32,256]{2,1,0:T(8,128)}, u32[]{:S(2)}, u32[]{:S(2)}) collective-permute-start(f32[8,32,256]{2,1,0:T(8,128)} %get-tuple-element.80), channel_id=1, source_target_pairs={{0,192},{32,224},{64,0},{96,32},{128,64},{160,96},{192,128},{224,1... | collective-permute-start | bytes 786440 | tf_op jit(solution)/shard_map/ppermute | solution.py:354
  239.0 0.7 copy-start.7
  240.1 1.1 copy-start.12
  241.2 17.2 %copy-start = (bf16[3,8,256,256]{3,2,1,0:T(8,128)(2,1)S(1)}, bf16[3,8,256,256]{3,2,1,0:T(8,128)(2,1)}, u32[]{:S(2)}) copy-start(bf16[3,8,256,256]{3,2,1,0:T(8,128)(2,1)} %shift_ref.19) | copy-start | bytes 9437188
  241.2 17.2 %copy-start.2 = (bf16[2,8,256,256]{3,2,1,0:T(8,128)(2,1)S(1)}, bf16[2,8,256,256]{3,2,1,0:T(8,128)(2,1)}, u32[]{:S(2)}) copy-start(bf16[2,8,256,256]{3,2,1,0:T(8,128)(2,1)} %rho_ref.19) | copy-start | bytes 6291460
  241.2 17.2 %copy-start.5 = (bf16[1536,512]{1,0:T(8,128)(2,1)S(1)}, bf16[1536,512]{1,0:T(8,128)(2,1)}, u32[]{:S(2)}) copy-start(bf16[1536,512]{1,0:T(8,128)(2,1)} %constant.20.clone.refs_2_) | copy-start | bytes 4718596
  246.1 14.4 %copy-start.3 = (bf16[768,512]{1,0:T(8,128)(2,1)S(1)}, bf16[768,512]{1,0:T(8,128)(2,1)}, u32[]{:S(2)}) copy-start(bf16[768,512]{1,0:T(8,128)(2,1)} %constant.21.clone.table_ref) | copy-start | bytes 2359300
  246.1 13.7 %collective-permute-start.8 = (f32[8,32,256]{2,1,0:T(8,128)S(1)}, f32[8,32,256]{2,1,0:T(8,128)S(1)}, u32[]{:S(2)}, u32[]{:S(2)}) collective-permute-start(f32[8,32,256]{2,1,0:T(8,128)S(1)} %get-tuple-element.82), channel_id=1, source_target_pairs={{0,160},{32,128},{64,224},{96,192},{128,32},{160,0},{192,96},{224,... | collective-permute-start | bytes 786440 | tf_op jit(solution)/shard_map/ppermute | solution.py:354
  250.6 16.9 %collective-permute-start.13 = (f32[8,32,256]{2,1,0:T(8,128)S(1)}, f32[8,32,256]{2,1,0:T(8,128)S(1)}, u32[]{:S(2)}, u32[]{:S(2)}) collective-permute-start(f32[8,32,256]{2,1,0:T(8,128)S(1)} %get-tuple-element.102), channel_id=1, source_target_pairs={{0,128},{32,160},{64,192},{96,224},{128,0},{160,32},{192,64},{224,... | collective-permute-start | bytes 786440 | tf_op jit(solution)/shard_map/ppermute | solution.py:354
  251.1 24.0 %collective-permute-start.12 = (f32[8,32,256]{2,1,0:T(8,128)S(1)}, f32[8,32,256]{2,1,0:T(8,128)S(1)}, u32[]{:S(2)}, u32[]{:S(2)}) collective-permute-start(f32[8,32,256]{2,1,0:T(8,128)S(1)} %get-tuple-element.98), channel_id=1, source_target_pairs={{0,32},{32,0},{64,96},{96,64},{128,160},{160,128},{192,224},{224,1... | collective-permute-start | bytes 786440 | tf_op jit(solution)/shard_map/ppermute | solution.py:354
  252.7 23.4 %collective-permute-start.11 = (f32[8,32,256]{2,1,0:T(8,128)S(1)}, f32[8,32,256]{2,1,0:T(8,128)S(1)}, u32[]{:S(2)}, u32[]{:S(2)}) collective-permute-start(f32[8,32,256]{2,1,0:T(8,128)S(1)} %get-tuple-element.94), channel_id=1, source_target_pairs={{0,96},{32,64},{64,160},{96,128},{128,224},{160,192},{192,32},{224... | collective-permute-start | bytes 786440 | tf_op jit(solution)/shard_map/ppermute | solution.py:354
  255.4 21.9 %collective-permute-start.10 = (f32[8,32,256]{2,1,0:T(8,128)S(1)}, f32[8,32,256]{2,1,0:T(8,128)S(1)}, u32[]{:S(2)}, u32[]{:S(2)}) collective-permute-start(f32[8,32,256]{2,1,0:T(8,128)S(1)} %get-tuple-element.90), channel_id=1, source_target_pairs={{0,224},{32,192},{64,32},{96,0},{128,96},{160,64},{192,160},{224,1... | collective-permute-start | bytes 786440 | tf_op jit(solution)/shard_map/ppermute | solution.py:354
  259.9 18.4 %collective-permute-start.9 = (f32[8,32,256]{2,1,0:T(8,128)S(1)}, f32[8,32,256]{2,1,0:T(8,128)S(1)}, u32[]{:S(2)}, u32[]{:S(2)}) collective-permute-start(f32[8,32,256]{2,1,0:T(8,128)S(1)} %get-tuple-element.86), channel_id=1, source_target_pairs={{0,64},{32,96},{64,128},{96,160},{128,192},{160,224},{192,0},{224,... | collective-permute-start | bytes 786440 | tf_op jit(solution)/shard_map/ppermute | solution.py:354
  261.7 1.2 copy-start.8
  267.5 11.9 %collective-permute-start.7 = (f32[8,32,256]{2,1,0:T(8,128)S(1)}, f32[8,32,256]{2,1,0:T(8,128)S(1)}, u32[]{:S(2)}, u32[]{:S(2)}) collective-permute-start(f32[8,32,256]{2,1,0:T(8,128)S(1)} %get-tuple-element.81), channel_id=1, source_target_pairs={{0,192},{32,224},{64,0},{96,32},{128,64},{160,96},{192,128},{224,1... | collective-permute-start | bytes 786440 | tf_op jit(solution)/shard_map/ppermute | solution.py:354
  271.8 3.3 %copy-start.4 = (bf16[768,512]{1,0:T(8,128)(2,1)S(1)}, bf16[768,512]{1,0:T(8,128)(2,1)}, u32[]{:S(2)}) copy-start(bf16[768,512]{1,0:T(8,128)(2,1)} %constant.22.clone.table_ref) | copy-start | bytes 2359300

commit v9 on v8

--- a/solution.py
+++ b/solution.py
@@ -351,7 +351,10 @@
 
     def over_refl(parts):
         ring = lambda s: [(i, (i // 2 + s // 2) % (NREF // 2) * 2 + (i + s) % 2) for i in range(NREF)]
-        moved = {s: lax.ppermute(parts[s], "refl", ring(s)) for s in R_ORDER}
+        moved = {}
+        for s in R_ORDER:
+            part = after(parts[s], moved[R_ORDER[0]]) if s in R_ORDER[5:] else parts[s]
+            moved[s] = lax.ppermute(part, "refl", ring(s))
         return [parts[0]] + [moved[s] for s in range(1, NREF)]
 
     def gradient(s, parts, sums):
@@ -403,7 +406,7 @@
         sums = gradient(s, (r0[s], r1[s]), sums)
     known = {s: early(s, after(r0[s], r1[R_ORDER[0]])) for s in R_ORDER[2:]}
     sums = after(sums, known)
-    for s in R_ORDER[2:]:
+    for s in (2, 1, 3, 7, 6):
         sums = late(s, r1[s], known[s], sums)
     return sums
 

time: 283 us -> 288 us (1.018)
  waiting for transfers between devices: 145 us -> 151 us
    ppermute x14, waiting for transfers between devices: 31.9 us -> 38.1 us  [over_refl(): moved[s] = lax.ppermute(part, 'refl', ring(s))]
  transfers between devices with their start and end apart: 18 -> 18, of which waited for: 8 -> 8; matrix products, arithmetic and copies ran while one was open for 0% -> 0% of each run, Pallas kernels for 22% -> 21%
where the time goes in v9:
time: 288 us; the launch traced here: 287 us
  waiting for transfers between devices  151 us (52%)
  Pallas kernels  74.4 us (26%)
  starting transfers between devices  55.3 us (19%)
  local copies, waits for them, and re-layouts  4.85 us (2%)
    all_to_all x4, waiting for transfers between devices, over_grid(): return lax.all_to_all(part, 'grid', 0, 0, tiled=True)  113 us
    ppermute x14, waiting for transfers between devices, over_refl(): moved[s] = lax.ppermute(part, 'refl', ring(s))  38.1 us
    ppermute x14, starting transfers between devices, over_refl(): moved[s] = lax.ppermute(part, 'refl', ring(s))  31 us
    pallas_call x2, Pallas kernels, x_both(): pl.pallas_call(x_kernel, grid=(1,), in_specs=[HBM, pl.BlockSpec((N * XL,...  24.3 us
    all_to_all x4, starting transfers between devices, over_grid(): return lax.all_to_all(part, 'grid', 0, 0, tiled=True)  24.3 us
    pallas_call x2, Pallas kernels, head(): pl.pallas_call(head_kernel, grid=(XL + 2,), in_specs=[SMEM, pl.BlockSpec(...  22.1 us
    pallas_call x2, Pallas kernels, y_inverse(): pl.pallas_call(y_inverse_kernel, in_specs=[SMEM, VMEM, VMEM], out_specs=[...  10.4 us
    pallas_call x5, Pallas kernels, early(): pl.pallas_call(functools.partial(early_kernel, s), in_specs=[SMEM, SMEM]...  6.52 us
  transfers between devices with their start and end apart: 18, of which 8 were waited for; matrix products, arithmetic and copies ran while one was open for 0% of the time, Pallas kernels for 21%

profile of v9, /device:TPU:8, one launch (start us, length us, event | category | flops | bytes accessed | tf_op | source)
XLA Modules:
  0.0 286.8 jit_solution(15316616487446709814)
XLA Ops:
  0.6 11.1 %head_0.1 = f32[32,8,8,256]{3,2,1,0:T(8,128)} custom-call(s32[3,8]{1,0:T(4,128)} %bitcast.7, bf16[2,8,256,256]{3,2,1,0:T(8,128)(2,1)} %rho_ref.19, bf16[3,8,256,256]{3,2,1,0:T(8,128)(2,1)} %shift_ref.19, s32[8,256,256]{2,1,0:T(8,128)} %support_ref.19, bf16[1536,512]{1,0:T(8,128)(2,1)} %constant.23.clone.table_ref, ...), custom_call_target="tpu_custom_call" | custom-call | flops 6400000000 | bytes 16000000 | tf_op jit(solution)/shard_map/head_0/pallas_call | solution.py:293
  11.7 10.1 %all-to-all-start = ((f32[32,8,8,256]{3,2,1,0:T(8,128)}), f32[32,8,8,256]{3,2,1,0:T(8,128)}, u32[]{:S(2)}, u32[]{:S(2)}) async-start(f32[32,8,8,256]{3,2,1,0:T(8,128)} %head_0.1), calls=%async_computation | async-start | bytes 4194304 | tf_op jit(solution)/shard_map/all_to_all | solution.py:350
  21.8 11.1 %head_1.1 = f32[32,8,8,256]{3,2,1,0:T(8,128)} custom-call(s32[3,8]{1,0:T(4,128)} %bitcast.8, bf16[2,8,256,256]{3,2,1,0:T(8,128)(2,1)} %rho_ref.19, bf16[3,8,256,256]{3,2,1,0:T(8,128)(2,1)} %shift_ref.19, s32[8,256,256]{2,1,0:T(8,128)} %support_ref.19, bf16[1536,512]{1,0:T(8,128)(2,1)} %constant.23.clone.table_ref, ...), custom_call_target="tpu_custom_call" | custom-call | flops 6400000000 | bytes 16000000 | tf_op jit(solution)/shard_map/head_1/pallas_call | solution.py:293
  32.9 39.2 %all-to-all-done = f32[32,8,8,256]{3,2,1,0:T(8,128)} async-done(((f32[32,8,8,256]{3,2,1,0:T(8,128)}), f32[32,8,8,256]{3,2,1,0:T(8,128)}, u32[]{:S(2)}, u32[]{:S(2)}) %all-to-all-start) | async-done | bytes 2097184 | tf_op jit(solution)/shard_map/all_to_all | solution.py:350
  72.1 4.7 %all-to-all-start.1 = ((f32[32,8,8,256]{3,2,1,0:T(8,128)}), f32[32,8,8,256]{3,2,1,0:T(8,128)}, u32[]{:S(2)}, u32[]{:S(2)}) async-start(f32[32,8,8,256]{3,2,1,0:T(8,128)} %head_1.1), calls=%async_computation.1 | async-start | bytes 4194304 | tf_op jit(solution)/shard_map/all_to_all | solution.py:350
  76.8 0.0 copy-start.14
  76.8 1.1 copy-done.14
  78.0 12.2 %x_0.1 = f32[2048,256]{1,0:T(8,128)} custom-call(f32[2048,256]{1,0:T(8,128)} %bitcast.5.in_ref, f32[2048,256]{1,0:T(8,128)S(1)} %bitcast.22, bf16[512,768]{1,0:T(8,128)(2,1)S(1)} %copy-done.14, bf16[512,768]{1,0:T(8,128)(2,1)S(1)} %copy-done.12), custom_call_target="tpu_custom_call" | custom-call | flops 6400000000 | bytes 24000000 | tf_op jit(solution)/shard_map/x_0/pallas_call | solution.py:325
  90.1 37.0 %all-to-all-done.1 = f32[32,8,8,256]{3,2,1,0:T(8,128)} async-done(((f32[32,8,8,256]{3,2,1,0:T(8,128)}), f32[32,8,8,256]{3,2,1,0:T(8,128)}, u32[]{:S(2)}, u32[]{:S(2)}) %all-to-all-start.1) | async-done | bytes 2097184 | tf_op jit(solution)/shard_map/all_to_all | solution.py:350
  127.1 4.7 %all-to-all-start.2 = ((f32[32,8,8,256]{3,2,1,0:T(8,128)}), f32[32,8,8,256]{3,2,1,0:T(8,128)}, u32[]{:S(2)}, u32[]{:S(2)}) async-start(f32[32,8,8,256]{3,2,1,0:T(8,128)} %bitcast.25), calls=%async_computation.2 | async-start | bytes 4194304 | tf_op jit(solution)/shard_map/all_to_all | solution.py:350
  131.9 0.0 copy-start.15
  131.9 1.1 copy-done.15
  133.0 12.1 %x_1.1 = f32[2048,256]{1,0:T(8,128)} custom-call(f32[2048,256]{1,0:T(8,128)} %bitcast.2.in_ref, f32[2048,256]{1,0:T(8,128)S(1)} %bitcast.23, bf16[512,768]{1,0:T(8,128)(2,1)S(1)} %copy-done.15, bf16[512,768]{1,0:T(8,128)(2,1)S(1)} %copy-done.12), custom_call_target="tpu_custom_call" | custom-call | flops 6400000000 | bytes 24000000 | tf_op jit(solution)/shard_map/x_1/pallas_call | solution.py:325
  145.1 37.0 %all-to-all-done.2.in_ref = f32[32,8,8,256]{3,2,1,0:T(8,128)} async-done(((f32[32,8,8,256]{3,2,1,0:T(8,128)}), f32[32,8,8,256]{3,2,1,0:T(8,128)}, u32[]{:S(2)}, u32[]{:S(2)}) %all-to-all-start.2) | async-done | bytes 2097184 | tf_op jit(solution)/shard_map/all_to_all | solution.py:350
  182.2 4.7 %all-to-all-start.3 = ((f32[32,8,8,256]{3,2,1,0:T(8,128)}), f32[32,8,8,256]{3,2,1,0:T(8,128)}, u32[]{:S(2)}, u32[]{:S(2)}) async-start(f32[32,8,8,256]{3,2,1,0:T(8,128)} %bitcast.24), calls=%async_computation.3 | async-start | bytes 4194304 | tf_op jit(solution)/shard_map/all_to_all | solution.py:350
  186.9 5.5 %y_inverse_0.1 = (f32[8,32,256]{2,1,0:T(8,128)S(1)}, f32[8,32,256]{2,1,0:T(8,128)S(1)}, f32[8,32,256]{2,1,0:T(8,128)}, f32[8,32,256]{2,1,0:T(8,128)S(1)}, f32[8,...) custom-call(s32[1]{0:T(128)} %bitcast.idx_ref, ...), custom_call_target="tpu_custom_call" | custom-call | flops 3200000000 | bytes 12000000 | tf_op jit(solution)/shard_map/y_inverse_0/pallas_call | solution.py:338
  192.4 0.7 copy-done.7
  193.2 4.8 %collective-permute-start = (f32[8,32,256]{2,1,0:T(8,128)S(1)}, f32[8,32,256]{2,1,0:T(8,128)S(1)}, u32[]{:S(2)}, u32[]{:S(2)}) collective-permute-start(f32[8,32,256]{2,1,0:T(8,128)S(1)} %get-tuple-element.68), channel_id=1, source_target_pairs={{0,160},{32,128},{64,224},{96,192},{128,32},{160,0},{192,96},{224,... | collective-permute-start | bytes 786440 | tf_op jit(solution)/shard_map/ppermute | solution.py:357
  198.0 0.5 collective-permute-start.1
  198.5 1.2 collective-permute-start.2
  199.7 3.3 %collective-permute-start.3 = (f32[8,32,256]{2,1,0:T(8,128)S(1)}, f32[8,32,256]{2,1,0:T(8,128)S(1)}, u32[]{:S(2)}, u32[]{:S(2)}) collective-permute-start(f32[8,32,256]{2,1,0:T(8,128)S(1)} %get-tuple-element.71), channel_id=1, source_target_pairs={{0,96},{32,64},{64,160},{96,128},{128,224},{160,192},{192,32},{224... | collective-permute-start | bytes 786440 | tf_op jit(solution)/shard_map/ppermute | solution.py:357
  202.9 2.4 collective-permute-start.4
  205.3 5.1 %collective-permute-done.refs_0_ = f32[8,32,256]{2,1,0:T(8,128)S(1)} collective-permute-done((f32[8,32,256]{2,1,0:T(8,128)S(1)}, f32[8,32,256]{2,1,0:T(8,128)S(1)}, u32[]{:S(2)}, u32[]{:S(2)}) %collective-permute-start) | collective-permute-done | bytes 262176 | tf_op jit(solution)/shard_map/ppermute | solution.py:357
  210.4 3.2 %collective-permute-start.5 = (f32[8,32,256]{2,1,0:T(8,128)}, f32[8,32,256]{2,1,0:T(8,128)S(1)}, u32[]{:S(2)}, u32[]{:S(2)}) collective-permute-start(f32[8,32,256]{2,1,0:T(8,128)} %get-tuple-element.84), channel_id=1, source_target_pairs={{0,64},{32,96},{64,128},{96,160},{128,192},{160,224},{192,0},{224,... | collective-permute-start | bytes 786440 | tf_op jit(solution)/shard_map/ppermute | solution.py:357
  213.7 1.3 collective-permute-done.1.refs_0_
  215.0 0.8 collective-permute-start.6
  215.8 23.2 %collective-permute-done.2.in_ref = f32[8,32,256]{2,1,0:T(8,128)S(1)} collective-permute-done((f32[8,32,256]{2,1,0:T(8,128)S(1)}, f32[8,32,256]{2,1,0:T(8,128)S(1)}, u32[]{:S(2)}, u32[]{:S(2)}) %collective-permute-start.2) | collective-permute-done | bytes 262176 | tf_op jit(solution)/shard_map/ppermute | solution.py:357
  238.9 0.0 collective-permute-done.3.in_ref
  238.9 0.0 collective-permute-done.4.in_ref
  238.9 0.7 copy-done.9
  239.6 0.0 all-to-all-done.3.in_ref
  239.6 1.1 copy-done.13
  240.8 4.9 %y_inverse_1.1 = (f32[8,32,256]{2,1,0:T(8,128)S(1)}, f32[8,32,256]{2,1,0:T(8,128)S(1)}, f32[8,32,256]{2,1,0:T(8,128)S(1)}, f32[8,32,256]{2,1,0:T(8,128)S(1)}, f3...) custom-call(s32[1]{0:T(128)} %bitcast.idx_ref, ...), custom_call_target="tpu_custom_call" | custom-call | flops 3200000000 | bytes 12000000 | tf_op jit(solution)/shard_map/y_inverse_1/pallas_call | solution.py:338
  245.7 0.0 collective-permute-done.5.in_ref
  245.7 0.0 collective-permute-done.6.in_ref
  245.7 0.0 copy-start.3
  245.7 4.7 %collective-permute-start.7 = (f32[8,32,256]{2,1,0:T(8,128)S(1)}, f32[8,32,256]{2,1,0:T(8,128)S(1)}, u32[]{:S(2)}, u32[]{:S(2)}) collective-permute-start(f32[8,32,256]{2,1,0:T(8,128)S(1)} %get-tuple-element.88), channel_id=1, source_target_pairs={{0,160},{32,128},{64,224},{96,192},{128,32},{160,0},{192,96},{224,... | collective-permute-start | bytes 786440 | tf_op jit(solution)/shard_map/ppermute | solution.py:357
  250.4 2.0 collective-permute-start.9
  252.4 2.4 collective-permute-start.10
  254.8 1.4 collective-permute-start.11
  256.2 0.7 collective-permute-start.13
  257.0 1.5 gradient_0.1
  258.5 0.9 collective-permute-done.7.refs_1_
  259.4 2.1 collective-permute-start.12
  261.5 1.6 early_6.1
  263.1 1.2 early_7.1
  264.3 1.2 early_3.1
  265.6 1.2 early_1.1
  266.8 1.2 early_2.1
  268.0 7.6 %collective-permute-done.13.refs_1_ = f32[8,32,256]{2,1,0:T(8,128)S(1)} collective-permute-done((f32[8,32,256]{2,1,0:T(8,128)S(1)}, f32[8,32,256]{2,1,0:T(8,128)S(1)}, u32[]{:S(2)}, u32[]{:S(2)}) %collective-permute-start.13) | collective-permute-done | bytes 262176 | tf_op jit(solution)/shard_map/ppermute | solution.py:357
  275.6 1.6 collective-permute-start.8
  277.2 1.5 gradient_5.1
  278.7 0.0 copy-start.4
  278.8 1.5 gradient_4.1
  280.3 0.0 collective-permute-done.12.in_ref
  280.3 1.1 late_2.1
  281.4 0.0 collective-permute-done.11.in_ref
  281.4 1.1 late_1.1
  282.5 0.0 collective-permute-done.10.in_ref
  282.5 1.1 late_3.1
  283.6 0.0 collective-permute-done.9.in_ref
  283.6 1.1 late_7.1
  284.6 0.0 collective-permute-done.8.in_ref
  284.7 2.1 late_6.1
  (23 shorter events, 0.0 us)
Async XLA Ops:
  11.7 60.4 %all-to-all-start = ((f32[32,8,8,256]{3,2,1,0:T(8,128)}), f32[32,8,8,256]{3,2,1,0:T(8,128)}, u32[]{:S(2)}, u32[]{:S(2)}) async-start(f32[32,8,8,256]{3,2,1,0:T(8,128)} %head_0.1), calls=%async_computation | async-start | bytes 4194304 | tf_op jit(solution)/shard_map/all_to_all | solution.py:350
  32.9 44.0 %copy-start.11 = (f32[1,256,8,256]{3,2,1,0:T(8,128)S(1)}, f32[1,256,8,256]{3,2,1,0:T(8,128)}, u32[]{:S(2)}) copy-start(f32[1,256,8,256]{3,2,1,0:T(8,128)} %param.18) | copy-start | bytes 6291460
  32.9 44.0 %copy-start.12 = (bf16[512,768]{1,0:T(8,128)(2,1)S(1)}, bf16[512,768]{1,0:T(8,128)(2,1)}, u32[]{:S(2)}) copy-start(bf16[512,768]{1,0:T(8,128)(2,1)} %constant.19.clone.inverse_ref.table_ref) | copy-start | bytes 2359300
  72.1 55.0 %all-to-all-start.1 = ((f32[32,8,8,256]{3,2,1,0:T(8,128)}), f32[32,8,8,256]{3,2,1,0:T(8,128)}, u32[]{:S(2)}, u32[]{:S(2)}) async-start(f32[32,8,8,256]{3,2,1,0:T(8,128)} %head_1.1), calls=%async_computation.1 | async-start | bytes 4194304 | tf_op jit(solution)/shard_map/all_to_all | solution.py:350
  76.8 1.1 copy-start.14
  127.1 55.0 %all-to-all-start.2 = ((f32[32,8,8,256]{3,2,1,0:T(8,128)}), f32[32,8,8,256]{3,2,1,0:T(8,128)}, u32[]{:S(2)}, u32[]{:S(2)}) async-start(f32[32,8,8,256]{3,2,1,0:T(8,128)} %bitcast.25), calls=%async_computation.2 | async-start | bytes 4194304 | tf_op jit(solution)/shard_map/all_to_all | solution.py:350
  131.9 1.1 copy-start.15
  182.2 57.5 %all-to-all-start.3 = ((f32[32,8,8,256]{3,2,1,0:T(8,128)}), f32[32,8,8,256]{3,2,1,0:T(8,128)}, u32[]{:S(2)}, u32[]{:S(2)}) async-start(f32[32,8,8,256]{3,2,1,0:T(8,128)} %bitcast.24), calls=%async_computation.3 | async-start | bytes 4194304 | tf_op jit(solution)/shard_map/all_to_all | solution.py:350
  192.4 0.7 copy-start.7
  193.2 17.3 %collective-permute-start = (f32[8,32,256]{2,1,0:T(8,128)S(1)}, f32[8,32,256]{2,1,0:T(8,128)S(1)}, u32[]{:S(2)}, u32[]{:S(2)}) collective-permute-start(f32[8,32,256]{2,1,0:T(8,128)S(1)} %get-tuple-element.68), channel_id=1, source_target_pairs={{0,160},{32,128},{64,224},{96,192},{128,32},{160,0},{192,96},{224,... | collective-permute-start | bytes 786440 | tf_op jit(solution)/shard_map/ppermute | solution.py:357
  198.0 17.0 %collective-permute-start.1 = (f32[8,32,256]{2,1,0:T(8,128)S(1)}, f32[8,32,256]{2,1,0:T(8,128)S(1)}, u32[]{:S(2)}, u32[]{:S(2)}) collective-permute-start(f32[8,32,256]{2,1,0:T(8,128)S(1)} %get-tuple-element.69), channel_id=1, source_target_pairs={{0,128},{32,160},{64,192},{96,224},{128,0},{160,32},{192,64},{224,... | collective-permute-start | bytes 786440 | tf_op jit(solution)/shard_map/ppermute | solution.py:357
  198.5 40.5 %collective-permute-start.2 = (f32[8,32,256]{2,1,0:T(8,128)S(1)}, f32[8,32,256]{2,1,0:T(8,128)S(1)}, u32[]{:S(2)}, u32[]{:S(2)}) collective-permute-start(f32[8,32,256]{2,1,0:T(8,128)S(1)} %get-tuple-element.70), channel_id=1, source_target_pairs={{0,32},{32,0},{64,96},{96,64},{128,160},{160,128},{192,224},{224,1... | collective-permute-start | bytes 786440 | tf_op jit(solution)/shard_map/ppermute | solution.py:357
  199.7 39.3 %collective-permute-start.3 = (f32[8,32,256]{2,1,0:T(8,128)S(1)}, f32[8,32,256]{2,1,0:T(8,128)S(1)}, u32[]{:S(2)}, u32[]{:S(2)}) collective-permute-start(f32[8,32,256]{2,1,0:T(8,128)S(1)} %get-tuple-element.71), channel_id=1, source_target_pairs={{0,96},{32,64},{64,160},{96,128},{128,224},{160,192},{192,32},{224... | collective-permute-start | bytes 786440 | tf_op jit(solution)/shard_map/ppermute | solution.py:357
  202.9 36.0 %collective-permute-start.4 = (f32[8,32,256]{2,1,0:T(8,128)S(1)}, f32[8,32,256]{2,1,0:T(8,128)S(1)}, u32[]{:S(2)}, u32[]{:S(2)}) collective-permute-start(f32[8,32,256]{2,1,0:T(8,128)S(1)} %get-tuple-element.72), channel_id=1, source_target_pairs={{0,224},{32,192},{64,32},{96,0},{128,96},{160,64},{192,160},{224,1... | collective-permute-start | bytes 786440 | tf_op jit(solution)/shard_map/ppermute | solution.py:357
  210.4 46.5 %copy-start.1 = (s32[8,256,256]{2,1,0:T(8,128)S(1)}, s32[8,256,256]{2,1,0:T(8,128)}, u32[]{:S(2)}) copy-start(s32[8,256,256]{2,1,0:T(8,128)} %support_ref.19) | copy-start | bytes 6291460
  210.4 46.5 %copy-start.6 = (s32[8,3]{0,1:T(4,128)S(1)}, s32[8,3]{0,1:T(4,128)}, u32[]{:S(2)}) copy-start(s32[8,3]{0,1:T(4,128)} %param.17) | copy-start | bytes 292
  210.4 35.3 %collective-permute-start.5 = (f32[8,32,256]{2,1,0:T(8,128)}, f32[8,32,256]{2,1,0:T(8,128)S(1)}, u32[]{:S(2)}, u32[]{:S(2)}) collective-permute-start(f32[8,32,256]{2,1,0:T(8,128)} %get-tuple-element.84), channel_id=1, source_target_pairs={{0,64},{32,96},{64,128},{96,160},{128,192},{160,224},{192,0},{224,... | collective-permute-start | bytes 786440 | tf_op jit(solution)/shard_map/ppermute | solution.py:357
  215.0 30.7 %collective-permute-start.6 = (f32[8,32,256]{2,1,0:T(8,128)}, f32[8,32,256]{2,1,0:T(8,128)}, u32[]{:S(2)}, u32[]{:S(2)}) collective-permute-start(f32[8,32,256]{2,1,0:T(8,128)} %get-tuple-element.86), channel_id=1, source_target_pairs={{0,192},{32,224},{64,0},{96,32},{128,64},{160,96},{192,128},{224,1... | collective-permute-start | bytes 786440 | tf_op jit(solution)/shard_map/ppermute | solution.py:357
  238.9 0.7 copy-start.9
  239.6 1.1 copy-start.13
  240.8 16.2 %copy-start = (bf16[3,8,256,256]{3,2,1,0:T(8,128)(2,1)S(1)}, bf16[3,8,256,256]{3,2,1,0:T(8,128)(2,1)}, u32[]{:S(2)}) copy-start(bf16[3,8,256,256]{3,2,1,0:T(8,128)(2,1)} %shift_ref.19) | copy-start | bytes 9437188
  240.8 16.2 %copy-start.2 = (bf16[2,8,256,256]{3,2,1,0:T(8,128)(2,1)S(1)}, bf16[2,8,256,256]{3,2,1,0:T(8,128)(2,1)}, u32[]{:S(2)}) copy-start(bf16[2,8,256,256]{3,2,1,0:T(8,128)(2,1)} %rho_ref.19) | copy-start | bytes 6291460
  240.8 16.2 %copy-start.5 = (bf16[1536,512]{1,0:T(8,128)(2,1)S(1)}, bf16[1536,512]{1,0:T(8,128)(2,1)}, u32[]{:S(2)}) copy-start(bf16[1536,512]{1,0:T(8,128)(2,1)} %constant.20.clone.refs_2_) | copy-start | bytes 4718596
  240.8 16.2 %copy-start.8 = (f32[8,32,256]{2,1,0:T(8,128)S(1)}, f32[8,32,256]{2,1,0:T(8,128)}, u32[]{:S(2)}) copy-start(f32[8,32,256]{2,1,0:T(8,128)} %copy-done.7) | copy-start | bytes 786436
  245.7 15.8 %copy-start.3 = (bf16[768,512]{1,0:T(8,128)(2,1)S(1)}, bf16[768,512]{1,0:T(8,128)(2,1)}, u32[]{:S(2)}) copy-start(bf16[768,512]{1,0:T(8,128)(2,1)} %constant.21.clone.table_ref) | copy-start | bytes 2359300
  245.7 13.7 %collective-permute-start.7 = (f32[8,32,256]{2,1,0:T(8,128)S(1)}, f32[8,32,256]{2,1,0:T(8,128)S(1)}, u32[]{:S(2)}, u32[]{:S(2)}) collective-permute-start(f32[8,32,256]{2,1,0:T(8,128)S(1)} %get-tuple-element.88), channel_id=1, source_target_pairs={{0,160},{32,128},{64,224},{96,192},{128,32},{160,0},{192,96},{224,... | collective-permute-start | bytes 786440 | tf_op jit(solution)/shard_map/ppermute | solution.py:357
  250.4 33.2 %collective-permute-start.9 = (f32[8,32,256]{2,1,0:T(8,128)S(1)}, f32[8,32,256]{2,1,0:T(8,128)S(1)}, u32[]{:S(2)}, u32[]{:S(2)}) collective-permute-start(f32[8,32,256]{2,1,0:T(8,128)S(1)} %get-tuple-element.93), channel_id=1, source_target_pairs={{0,224},{32,192},{64,32},{96,0},{128,96},{160,64},{192,160},{224,1... | collective-permute-start | bytes 786440 | tf_op jit(solution)/shard_map/ppermute | solution.py:357
  252.4 30.1 %collective-permute-start.10 = (f32[8,32,256]{2,1,0:T(8,128)S(1)}, f32[8,32,256]{2,1,0:T(8,128)S(1)}, u32[]{:S(2)}, u32[]{:S(2)}) collective-permute-start(f32[8,32,256]{2,1,0:T(8,128)S(1)} %get-tuple-element.97), channel_id=1, source_target_pairs={{0,96},{32,64},{64,160},{96,128},{128,224},{160,192},{192,32},{224... | collective-permute-start | bytes 786440 | tf_op jit(solution)/shard_map/ppermute | solution.py:357
  254.8 26.6 %collective-permute-start.11 = (f32[8,32,256]{2,1,0:T(8,128)S(1)}, f32[8,32,256]{2,1,0:T(8,128)S(1)}, u32[]{:S(2)}, u32[]{:S(2)}) collective-permute-start(f32[8,32,256]{2,1,0:T(8,128)S(1)} %get-tuple-element.101), channel_id=1, source_target_pairs={{0,32},{32,0},{64,96},{96,64},{128,160},{160,128},{192,224},{224,1... | collective-permute-start | bytes 786440 | tf_op jit(solution)/shard_map/ppermute | solution.py:357
  256.2 19.4 %collective-permute-start.13 = (f32[8,32,256]{2,1,0:T(8,128)S(1)}, f32[8,32,256]{2,1,0:T(8,128)S(1)}, u32[]{:S(2)}, u32[]{:S(2)}) collective-permute-start(f32[8,32,256]{2,1,0:T(8,128)S(1)} %get-tuple-element.110), channel_id=1, source_target_pairs={{0,128},{32,160},{64,192},{96,224},{128,0},{160,32},{192,64},{224,... | collective-permute-start | bytes 786440 | tf_op jit(solution)/shard_map/ppermute | solution.py:357
  258.5 4.6 %copy-start.10 = (f32[8,32,256]{2,1,0:T(8,128)S(1)}, f32[8,32,256]{2,1,0:T(8,128)}, u32[]{:S(2)}) copy-start(f32[8,32,256]{2,1,0:T(8,128)} %copy-done.9) | copy-start | bytes 786436
  259.4 20.9 %collective-permute-start.12 = (f32[8,32,256]{2,1,0:T(8,128)S(1)}, f32[8,32,256]{2,1,0:T(8,128)S(1)}, u32[]{:S(2)}, u32[]{:S(2)}) collective-permute-start(f32[8,32,256]{2,1,0:T(8,128)S(1)} %get-tuple-element.106), channel_id=1, source_target_pairs={{0,64},{32,96},{64,128},{96,160},{128,192},{160,224},{192,0},{224,... | collective-permute-start | bytes 786440 | tf_op jit(solution)/shard_map/ppermute | solution.py:357
  275.6 9.0 %collective-permute-start.8 = (f32[8,32,256]{2,1,0:T(8,128)S(1)}, f32[8,32,256]{2,1,0:T(8,128)S(1)}, u32[]{:S(2)}, u32[]{:S(2)}) collective-permute-start(f32[8,32,256]{2,1,0:T(8,128)S(1)} %get-tuple-element.89), channel_id=1, source_target_pairs={{0,192},{32,224},{64,0},{96,32},{128,64},{160,96},{192,128},{224,1... | collective-permute-start | bytes 786440 | tf_op jit(solution)/shard_map/ppermute | solution.py:357
  278.7 1.6 copy-start.4
